TPU v7x, 32 devices: a whole 2x2x4 slice. The times are simulated.
32 devices in a mesh: groups: 2 (over y), lat: 4 (over z), lon: 4 (over x, core).
Axes of the slice: x: 2, y: 2, z: 4, core: 2. Of those that a mesh axis runs over, the one named last changes fastest.
Arguments:
- profiles: bfloat16 [4, 137, 32, 2048], P('groups', None, 'lat', 'lon'), parts along dimension 0, may hold values from -6 to 6
- obs_cell: int32 [8, 1536], P(('groups', 'lon'), 'lat'), parts along dimension 0, may hold values from 0 to 4095
- obs_weight: float32 [18, 4, 1536], P('groups', 'lon', 'lat'), parts along dimension 0, may hold values from 0 to 1
- batch_instr: int32 [8, 96], P(('groups', 'lon'), 'lat'), parts along dimension 0, may hold values from 0 to 15
- batch_dest: int32 [8, 96], P(('groups', 'lon'), 'lat'), parts along dimension 0, may hold values from -1 to 47, as said below
- absorption: bfloat16 [16, 128, 137], replicated, may hold values from 0.00049972534 to 0.19921875
- cotangent: float32 [8, 768, 128], P(('groups', 'lon'), 'lat'), parts along dimension 0, may hold values from -6 to 6
Outputs:
- brightness_signal: float32 [8, 768, 128], P(('groups', 'lon'), 'lat'), parts along dimension 0
- profile_grad: float32 [4, 137, 32, 2048], P('groups', None, 'lat', 'lon'), parts along dimension 0
There are 2 independent parts, one for each index of `groups`. A program takes and returns all parts, laid end to end along the dimension named above; an argument that names none is the same for every part. Nothing has to cross between parts.
Inputs may be any that keep to these rules, and one draw needn't show every extreme that they name: On each device the live batch slots (batch_dest >= 0) come first and are followed by empty ones (-1); the observation data of empty slots are drawn but unused. Within each longitude sector every processing slot 0 to 47 is named exactly once; slot g belongs to the lat device g // 12 of that sector. No device sends more than 6 of its batches to one lat device, and in every draw some device sends exactly 6 to one; in every sector some device owns 24 live batches.
All inputs are finite; a program needn't handle non-finite values.
Results may differ from a plain program's by a relative error of at most 0.014.
Values may be sent and summed in bfloat16 or wider, within the bound.
No kernel may reach another device: no remote copies, remote signals or barrier semaphores. Data moves between devices by JAX's collectives and lax.ppermute only.
A program may use at most 128 MiB of HBM per device.

v0:
```python
import functools

import jax
import jax.numpy as jnp
from jax import lax
from jax.experimental import pallas as pl
from jax.experimental.pallas import tpu as pltpu
from jax.sharding import PartitionSpec as P

F32 = jnp.float32
BF16 = jnp.bfloat16
LOG2E = 1.4426950408889634
LANES = 128
EDGE = 16
NEAR = ((0, -1), (0, 1), (-1, -1), (-1, 1), (1, -1), (1, 1))
VMEM = pl.BlockSpec(memory_space=pltpu.VMEM)
SMEM = pl.BlockSpec(memory_space=pltpu.SMEM)
NN = (((1,), (0,)), ((), ()))
NT = (((1,), (1,)), ((), ()))
TN = (((0,), (0,)), ((), ()))


def dot(a, b, dims=NN):
    return lax.dot_general(a, b, dims, preferred_element_type=F32)


def round_up(value, unit):
    return -(-value // unit) * unit


def params(mib=48):
    return pltpu.CompilerParams(vmem_limit_bytes=mib * 1024 * 1024)


def iota(shape, dim):
    return lax.broadcasted_iota(jnp.int32, shape, dim)


def split_cells(cells, width):
    if width & (width - 1) == 0:
        return lax.shift_right_logical(cells, width.bit_length() - 1), cells & (width - 1)
    row = lax.div(cells, width)
    return row, cells - row * width


def fill_columns(cells_ref, weight_ref, columns_ref):
    width, obs = columns_ref.shape[1:]
    _, col = split_cells(cells_ref[...], width)
    weights = [weight_ref[k] for k in range(9)]
    step = 32

    def chunk(i, carry):
        base = pl.multiple_of(i * step, step)
        for lane in range(0, obs, LANES):
            part = slice(lane, lane + LANES)
            away = iota((step, LANES), 0) + base - col[:, part]
            hit = [away == b - 1 for b in range(3)]
            for a in range(3):
                value = jnp.zeros((step, LANES), F32)
                for b in range(3):
                    value = jnp.where(hit[b], weights[3 * a + b][:, part], value)
                columns_ref[a, pl.ds(base, step), part] = value.astype(BF16)
        return carry

    lax.fori_loop(0, width // step, chunk, 0)


def row_stencil(columns_ref, row_of, r):
    total = None
    for a in range(3):
        keep = jnp.where(row_of == r - a + 1, 1.0, 0.0).astype(BF16)
        term = columns_ref[a] * keep
        total = term if total is None else total + term
    return total


def edge_weights(cells_ref, weight_ref, rows, width):
    lines = len(NEAR) * EDGE
    obs = cells_ref.shape[1]
    row, col = split_cells(cells_ref[...], width)
    line = iota((lines, obs), 0)
    near = lax.shift_right_logical(line, 4)
    k = line & (EDGE - 1)
    none = -99
    row_at = jnp.full((lines, obs), none, jnp.int32)
    col_at = jnp.where((near & 1) == 0, -1, width)
    row_at = jnp.where((near == 0) & (k >= rows), k - rows, row_at)
    row_at = jnp.where((near == 1) & (k < rows), k, row_at)
    row_at = jnp.where((near == 2) & (k == 2 * rows - 1), -1, row_at)
    row_at = jnp.where((near == 3) & (k == rows - 1), -1, row_at)
    row_at = jnp.where((near == 4) & (k == rows), rows, row_at)
    row_at = jnp.where((near == 5) & (k == 0), rows, row_at)
    total = jnp.zeros((lines, obs), F32)
    for a in range(3):
        for b in range(3):
            hit = (row_at == row + (a - 1)) & (col_at == col + (b - 1))
            total = total + jnp.where(hit, weight_ref[3 * a + b], 0.0)
    return total.astype(BF16)


def pack_kernel(dims, profiles_ref, cot_ref, mid_ref, top_ref, bottom_ref, edge_ref, cot_out_ref, wide_ref):
    levels, rows, width, pad = dims
    for lane in range(0, width, LANES):
        part = profiles_ref[:, :, lane : lane + LANES]
        wide_ref[lane // LANES] = part.astype(F32).reshape(2 * levels * rows, LANES)
    edges = jnp.zeros((EDGE, 2 * pad), F32)
    k = iota((EDGE, LANES), 0)
    at_lane = iota((EDGE, LANES), 1)
    for r in range(rows):
        out = top_ref if r == 0 else bottom_ref if r == rows - 1 else mid_ref.at[r - 1]
        for v in range(2):
            for lane in range(0, width, LANES):
                value = wide_ref[lane // LANES, pl.ds(v * levels * rows + r, levels, stride=rows), :]
                value = jnp.concatenate([value, jnp.zeros((pad - levels, LANES), F32)], axis=0)
                out[v * pad : (v + 1) * pad, lane : lane + LANES] = value.astype(BF16)
        west = jnp.where((k == r) & (at_lane == 0), 1.0, 0.0).astype(BF16)
        east = jnp.where((k == rows + r) & (at_lane == LANES - 1), 1.0, 0.0).astype(BF16)
        edges = edges + dot(west, out[:, :LANES], NT) + dot(east, out[:, width - LANES :], NT)
    edges = edges.astype(BF16)

    def spread(s, carry):
        edge_ref[s] = jnp.zeros(edge_ref.shape[1:], BF16)
        edge_ref[s, :, : 2 * pad] = edges
        return carry

    lax.fori_loop(0, edge_ref.shape[0], spread, 0)
    cot = cot_ref[0].astype(BF16)

    def share(s, carry):
        cot_out_ref[s] = cot
        return carry

    lax.fori_loop(0, cot_out_ref.shape[0], share, 0)


def neighbour(n, grid):
    n_lat, n_lon = grid
    i = lax.axis_index("lat") + NEAR[n][0]
    j = lax.axis_index("lon") + NEAR[n][1]
    valid = (i >= 0) & (i < n_lat) & (j >= 0) & (j < n_lon)
    return jnp.where(valid, i * n_lon + j, 0), valid


def transfer_kernel(
    dims,
    cells_ref,
    weight_ref,
    instr_ref,
    dest_ref,
    absorb_ref,
    mid_ref,
    top_ref,
    bottom_ref,
    above_ref,
    below_ref,
    edge_ref,
    cot_ref,
    grad_ref,
    grad_above_ref,
    grad_below_ref,
    grad_edge_ref,
    rad_ref,
    columns_ref,
    halo_ref,
    field_ref,
    rate_ref,
    step_ref,
    cot_rows_ref,
    cot_t_ref,
    absorb_t_ref,
    signal_ref,
    s_part_ref,
    r_part_ref,
    shift_ref,
):
    levels, rows, width, pad, batch, grid = dims
    obs = cells_ref.shape[1]
    slots = obs // batch
    channels = cot_ref.shape[1]
    instruments = absorb_ref.shape[1]
    fill_columns(cells_ref, weight_ref, columns_ref)
    row, _ = split_cells(cells_ref[...], width)

    field_ref[...] = dot(above_ref[...], row_stencil(columns_ref, row, -1))
    field_ref[...] += dot(below_ref[...], row_stencil(columns_ref, row, rows))
    for r in range(rows):
        source = top_ref if r == 0 else bottom_ref if r == rows - 1 else mid_ref.at[r - 1]
        field_ref[...] += dot(source[...], row_stencil(columns_ref, row, r))
    for n in range(len(NEAR)):
        at, valid = neighbour(n, grid)
        halo_ref[n * EDGE : (n + 1) * EDGE, :] = edge_ref[at].astype(F32) * jnp.where(valid, 1.0, 0.0)
    edge_w = edge_weights(cells_ref, weight_ref, rows, width)
    field_ref[...] += dot(halo_ref[:, : 2 * pad].astype(BF16), edge_w, TN)

    for q in range(slots):
        where = dest_ref[0, q]
        start = pl.multiple_of(jnp.maximum(where, 0) * batch, batch)
        value = cot_ref[pl.ds(start, batch), :].astype(F32)
        cot_rows_ref[q * batch : (q + 1) * batch, :] = jnp.where(where >= 0, value, 0.0)
    for lane in range(0, obs, LANES):
        cot_t_ref[:, lane : lane + LANES] = cot_rows_ref[lane : lane + LANES, :].T
    lane_slot = lax.shift_right_logical(iota((1, obs), 1), batch.bit_length() - 1)
    chosen = jnp.zeros((1, obs), jnp.int32)
    for q in range(slots):
        chosen = jnp.where(lane_slot == q, instr_ref[0, q], chosen)
    pick = jnp.where(iota((instruments, obs), 0) == chosen, 1.0, 0.0)
    pick_bf = pick.astype(BF16)

    def turn(l, carry):
        absorb_t_ref[l] = absorb_ref[l].astype(F32).T.astype(BF16)
        return carry

    lax.fori_loop(0, levels, turn, 0)

    temperature = field_ref[0:pad, :]
    step_ref[...] = field_ref[1 : pad + 1, :] - temperature
    bent = jnp.tanh(field_ref[pad : 2 * pad, :])
    rate_ref[...] = -LOG2E * (1.0 + 0.5 * bent)
    tail = jnp.zeros((obs // LANES, (pad - levels) * 8, LANES), F32)
    s_part_ref[:, levels * 8 :, :] = tail
    r_part_ref[:, levels * 8 :, :] = tail
    part = 64
    for lane in range(0, obs, LANES):
        lanes = slice(lane, lane + LANES)
        group = lane // LANES
        for c0 in range(0, channels, part):
            first = c0 == 0
            cs = slice(c0, c0 + part)

            def level(l, row_base, j, rates, steps, cum, signal):
                a = dot(absorb_t_ref[l, cs, :], pick_bf[:, lanes])
                cot = cot_t_ref[cs, lanes]
                cum = cum + a * rates[j : j + 1]
                transmit = jnp.exp2(cum)
                r_sum = jnp.sum((cot * signal * a).reshape(part // 8, 8, LANES), axis=0)
                s_sum = jnp.sum((cot * transmit).reshape(part // 8, 8, LANES), axis=0)
                signal = signal + transmit * steps[j : j + 1]
                at = pl.ds(pl.multiple_of(row_base + 8 * j, 8), 8)
                if first:
                    r_part_ref[group, at, :] = r_sum
                    s_part_ref[group, at, :] = s_sum
                else:
                    r_part_ref[group, at, :] += r_sum
                    s_part_ref[group, at, :] += s_sum
                return cum, signal

            def block(b, carry):
                cum, signal = carry
                base = pl.multiple_of(b * 8, 8)
                rates = rate_ref[pl.ds(base, 8), lanes]
                steps = step_ref[pl.ds(base, 8), lanes]
                for j in range(8):
                    cum, signal = level(base + j, b * 64, j, rates, steps, cum, signal)
                return cum, signal

            start = jnp.zeros((part, LANES), F32)
            full = levels // 8
            cum, signal = lax.fori_loop(0, full, block, (start, start))
            rates = rate_ref[full * 8 : full * 8 + 8, lanes]
            steps = step_ref[full * 8 : full * 8 + 8, lanes]
            for j in range(levels - full * 8):
                cum, signal = level(full * 8 + j, full * 64, j, rates, steps, cum, signal)
            signal_ref[cs, lanes] = signal

    rad_ref[...] = jnp.zeros(rad_ref.shape, BF16)
    for lane in range(0, obs, LANES):
        lanes = slice(lane, lane + LANES)
        value = (signal_ref[:, lanes] + field_ref[0:1, lanes]).T.astype(BF16)
        for q in range(LANES // batch):
            where = dest_ref[0, lane // batch + q]

            @pl.when(where >= 0)
            def _():
                start = pl.multiple_of(where * batch, batch)
                rad_ref[pl.ds(start, batch), :] = value[q * batch : (q + 1) * batch, :]

    held = cot_t_ref[...] * signal_ref[...]
    held_hi = held.astype(BF16)
    held_lo = (held - held_hi.astype(F32)).astype(BF16)

    def contract(l0, count):
        rows_in = absorb_ref[pl.ds(l0, count)].reshape(count * instruments, channels)
        value = dot(rows_in, held_hi) + dot(rows_in, held_lo)
        value = value.reshape(count, instruments, obs) * pick[None]
        value = jnp.sum(value.reshape(count, instruments // 8, 8, obs), axis=1)
        at = pl.ds(pl.multiple_of(l0 * 8, 8), count * 8)
        value = value.reshape(count * 8, obs)
        for lane in range(0, obs, LANES):
            r_part_ref[lane // LANES, at, :] -= value[:, lane : lane + LANES]

    def contract_block(b, carry):
        contract(b * 8, 8)
        return carry

    lax.fori_loop(0, levels // 8, contract_block, 0)
    if levels % 8:
        contract(levels // 8 * 8, levels % 8)

    for lane in range(0, obs, LANES):
        lanes = slice(lane, lane + LANES)
        group = lane // LANES
        s_sum = s_part_ref[group, pl.ds(0, pad, stride=8), :]
        r_sum = r_part_ref[group, pl.ds(0, pad, stride=8), :]
        for k in range(1, 8):
            s_sum = s_sum + s_part_ref[group, pl.ds(k, pad, stride=8), :]
            r_sum = r_sum + r_part_ref[group, pl.ds(k, pad, stride=8), :]
        shift_ref[7:8, lanes] = jnp.sum(cot_t_ref[:, lanes], axis=0, keepdims=True)
        shift_ref[8 : 8 + pad, lanes] = s_sum
        grad_ref[0:pad, lanes] = (shift_ref[7 : 7 + pad, lanes] - s_sum).astype(BF16)
        bent = jnp.tanh(field_ref[pad : 2 * pad, lanes])
        grad_ref[pad : 2 * pad, lanes] = (0.5 * (1.0 - bent * bent) * r_sum).astype(BF16)

    grad = grad_ref[...]
    grad_above_ref[...] = dot(grad, row_stencil(columns_ref, row, -1), NT).astype(BF16)
    grad_below_ref[...] = dot(grad, row_stencil(columns_ref, row, rows), NT).astype(BF16)
    out = dot(edge_w, grad, NT).astype(BF16)

    def clear(s, carry):
        grad_edge_ref[s] = jnp.zeros(grad_edge_ref.shape[1:], BF16)
        return carry

    lax.fori_loop(0, grad_edge_ref.shape[0], clear, 0)
    for n in range(len(NEAR)):
        at, valid = neighbour(n, grid)

        @pl.when(valid)
        def _():
            grad_edge_ref[at, :, : 2 * pad] = out[n * EDGE : (n + 1) * EDGE, :]


def scatter_kernel(
    dims,
    cells_ref,
    weight_ref,
    grad_ref,
    from_above_ref,
    from_below_ref,
    edge_ref,
    rad_ref,
    out_ref,
    rad_out_ref,
    columns_ref,
    halo_ref,
    wide_ref,
):
    levels, rows, width, pad, grid = dims
    rad_out_ref[...] = jnp.sum(rad_ref[...].astype(F32), axis=0)[None]
    fill_columns(cells_ref, weight_ref, columns_ref)
    row, _ = split_cells(cells_ref[...], width)
    total = jnp.zeros(edge_ref.shape[1:], F32)
    for n in range(len(NEAR)):
        at, valid = neighbour(n, grid)
        halo_ref[n * EDGE : (n + 1) * EDGE, :] = edge_ref[at].astype(F32) * jnp.where(valid, 1.0, 0.0)
    edges = halo_ref[:, : 2 * pad].T.astype(BF16)
    lines = edges.shape[1]
    k = iota((lines, LANES), 0) & (EDGE - 1)
    at_lane = iota((lines, LANES), 1)
    for r in range(rows):
        value = dot(grad_ref[...], row_stencil(columns_ref, row, r), NT)
        if r == 0:
            value = value + from_above_ref[...].astype(F32)
        if r == rows - 1:
            value = value + from_below_ref[...].astype(F32)
        west = jnp.where((k == r) & (at_lane == 0), 1.0, 0.0).astype(BF16)
        east = jnp.where((k == rows + r) & (at_lane == LANES - 1), 1.0, 0.0).astype(BF16)
        first = value[:, :LANES] + dot(edges, west)
        last = value[:, width - LANES :] + dot(edges, east)
        value = jnp.concatenate([first, value[:, LANES : width - LANES], last], axis=1)
        for v in range(2):
            at = pl.ds(v * levels * rows + r, levels, stride=rows)
            for lane in range(0, width, LANES):
                wide_ref[lane // LANES, at, :] = value[v * pad : v * pad + levels, lane : lane + LANES]
    for lane in range(0, width, LANES):
        out_ref[:, lane : lane + LANES] = wide_ref[lane // LANES]


def per_device(profiles, obs_cell, obs_weight, batch_instr, batch_dest, absorption, cotangent):
    n_lat, n_lon = lax.axis_size("lat"), lax.axis_size("lon")
    grid = (n_lat, n_lon)
    levels, rows, width = profiles.shape[1:]
    instruments, channels, _ = absorption.shape
    obs = obs_cell.shape[1]
    slots = batch_dest.shape[1]
    batch = obs // slots
    proc = cotangent.shape[1]
    pad = round_up(levels, 16)
    feat = round_up(2 * pad, LANES)
    up = [(i, i + 1) for i in range(n_lat - 1)]
    down = [(b, a) for a, b in up]
    shape = jax.ShapeDtypeStruct

    mid, top, bottom, edge, cot = pl.pallas_call(
        functools.partial(pack_kernel, (levels, rows, width, pad)),
        out_shape=(
            shape((rows - 2, 2 * pad, width), BF16),
            shape((2 * pad, width), BF16),
            shape((2 * pad, width), BF16),
            shape((n_lat * n_lon, EDGE, feat), BF16),
            shape((n_lat, proc, channels), BF16),
        ),
        in_specs=[VMEM, VMEM],
        out_specs=(VMEM,) * 5,
        scratch_shapes=[pltpu.VMEM((width // LANES, 2 * levels * rows, LANES), F32)],
        compiler_params=params(),
        name="pack",
    )(profiles.reshape(2 * levels, rows, width), cotangent)

    above = lax.ppermute(bottom, "lat", up)
    below = lax.ppermute(top, "lat", down)
    edge_in = lax.all_to_all(edge, ("lat", "lon"), 0, 0, tiled=True)
    cot_in = lax.all_to_all(cot, "lat", 0, 0, tiled=True).reshape(n_lat * proc, channels)

    lines = len(NEAR) * EDGE
    grad, grad_above, grad_below, grad_edge, rad = pl.pallas_call(
        functools.partial(transfer_kernel, (levels, rows, width, pad, batch, grid)),
        out_shape=(
            shape((2 * pad, obs), BF16),
            shape((2 * pad, width), BF16),
            shape((2 * pad, width), BF16),
            shape((n_lat * n_lon, EDGE, feat), BF16),
            shape((n_lat * proc, channels), BF16),
        ),
        in_specs=[VMEM, VMEM, SMEM, SMEM] + [VMEM] * 8,
        out_specs=(VMEM,) * 5,
        scratch_shapes=[
            pltpu.VMEM((3, width, obs), BF16),
            pltpu.VMEM((lines, feat), F32),
            pltpu.VMEM((2 * pad, obs), F32),
            pltpu.VMEM((pad, obs), F32),
            pltpu.VMEM((pad, obs), F32),
            pltpu.VMEM((obs, channels), F32),
            pltpu.VMEM((channels, obs), F32),
            pltpu.VMEM((levels, channels, instruments), BF16),
            pltpu.VMEM((channels, obs), F32),
            pltpu.VMEM((obs // LANES, pad * 8, LANES), F32),
            pltpu.VMEM((obs // LANES, pad * 8, LANES), F32),
            pltpu.VMEM((pad + 8, obs), F32),
        ],
        compiler_params=params(),
        name="transfer",
    )(
        obs_cell,
        obs_weight,
        batch_instr,
        batch_dest,
        jnp.transpose(absorption, (2, 0, 1)),
        mid,
        top,
        bottom,
        above,
        below,
        edge_in,
        cot_in,
    )

    from_below = lax.ppermute(grad_above, "lat", down)
    from_above = lax.ppermute(grad_below, "lat", up)
    grad_edge_in = lax.all_to_all(grad_edge, ("lat", "lon"), 0, 0, tiled=True)
    rad_in = lax.all_to_all(rad.reshape(n_lat, proc, channels), "lat", 0, 0, tiled=True)

    gradient, radiance = pl.pallas_call(
        functools.partial(scatter_kernel, (levels, rows, width, pad, grid)),
        out_shape=(
            shape((2 * levels * rows, width), F32),
            shape((1, proc, channels), F32),
        ),
        in_specs=[VMEM] * 7,
        out_specs=(VMEM,) * 2,
        scratch_shapes=[
            pltpu.VMEM((3, width, obs), BF16),
            pltpu.VMEM((lines, feat), F32),
            pltpu.VMEM((width // LANES, 2 * levels * rows, LANES), F32),
        ],
        compiler_params=params(),
        name="scatter",
    )(obs_cell, obs_weight, grad, from_above, from_below, grad_edge_in, rad_in)
    return radiance, gradient.reshape(2, levels, rows, width)


def solution(mesh):
    placed = (
        P("groups", None, "lat", "lon"),
        P(("groups", "lon"), "lat"),
        P("groups", "lon", "lat"),
        P(("groups", "lon"), "lat"),
        P(("groups", "lon"), "lat"),
        P(),
        P(("groups", "lon"), "lat", None),
    )
    return jax.shard_map(
        per_device,
        mesh=mesh,
        in_specs=placed,
        out_specs=(P(("groups", "lon"), "lat", None), P("groups", None, "lat", "lon")),
        check_vma=False,
    )
```

profile of v0, /device:TPU:0, one launch (start us, length us, event | category | flops | bytes accessed | tf_op | source)
XLA Modules:
  0.0 122.4 jit_solution(8025363978146678968)
XLA Ops:
  0.6 0.0 copy-start.9
  0.6 0.0 copy-start
  0.7 1.6 %copy-done = bf16[2,137,8,512]{3,2,1,0:T(8,128)(2,1)S(1)} copy-done((bf16[2,137,8,512]{3,2,1,0:T(8,128)(2,1)S(1)}, bf16[2,137,8,512]{3,2,1,0:T(8,128)(2,1)}, u32[]{:S(2)}) %copy-start) | copy-done | bytes 2244632
  2.3 0.0 copy-start.7
  2.3 0.9 copy-done.7
  3.2 0.0 copy-start.1
  3.2 0.0 copy-start.8
  3.2 2.4 %pack.1 = (bf16[6,288,512]{2,1,0:T(8,128)(2,1)S(1)}, bf16[288,512]{1,0:T(8,128)(2,1)S(1)}, bf16[288,512]{1,0:T(8,128)(2,1)S(1)}, bf16[16,16,384]{2,1,0:T(8,128)(2,1)}, bf16[4,192,128]{2,1,0:T(8,128)(2,1)S(1)}) custom-call(bf16[274,8,512]{2,1,0:T(8,128)(2,1)S(1)} %bitcast.5, f32[1,192,128]{2,1,0:T(8,128)S(1)} %copy-done.7), custom_call_target="tpu_custom_call" | custom-call | tf_op jit(solution)/shard_map/pack/pallas_call | solution.py:392
  5.6 13.6 %all_to_all.20 = bf16[4,192,128]{2,1,0:T(8,128)(2,1)S(1)} all-to-all(bf16[4,192,128]{2,1,0:T(8,128)(2,1)S(1)} %get-tuple-element.18), channel_id=1, replica_groups=mesh['groups'=2,'lat'=4,'lon'=4] {'lat'}, dimensions={0} | all-to-all | bytes 393216 | tf_op jit(solution)/shard_map/all_to_all | solution.py:411
  19.2 3.8 %all-to-all-start = ((bf16[16,16,384]{2,1,0:T(8,128)(2,1)}), bf16[16,16,384]{2,1,0:T(8,128)(2,1)S(1)}, u32[]{:S(2)}, u32[]{:S(2)}) async-start(bf16[16,16,384]{2,1,0:T(8,128)(2,1)} %get-tuple-element.17), calls=%async_computation | async-start | bytes 393216 | tf_op jit(solution)/shard_map/all_to_all | solution.py:410
  23.0 1.3 %collective-permute-start.1 = (bf16[288,512]{1,0:T(8,128)(2,1)S(1)}, bf16[288,512]{1,0:T(8,128)(2,1)S(1)}, u32[]{:S(2)}, u32[]{:S(2)}) collective-permute-start(bf16[288,512]{1,0:T(8,128)(2,1)S(1)} %get-tuple-element.15.top_ref), channel_id=1, source_target_pairs={{4,0},{8,4},{12,8},{5,1},{9,5},{13,9},{6,2},{10,6},{14,10},{7,3},{... | collective-permute-start | bytes 884744 | tf_op jit(solution)/shard_map/ppermute | solution.py:409
  24.3 4.6 %collective-permute-start = (bf16[288,512]{1,0:T(8,128)(2,1)S(1)}, bf16[288,512]{1,0:T(8,128)(2,1)S(1)}, u32[]{:S(2)}, u32[]{:S(2)}) collective-permute-start(bf16[288,512]{1,0:T(8,128)(2,1)S(1)} %get-tuple-element.16.bottom_ref), channel_id=1, source_target_pairs={{0,4},{4,8},{8,12},{1,5},{5,9},{9,13},{2,6},{6,10},{10,14},{3,7},{... | collective-permute-start | bytes 884744 | tf_op jit(solution)/shard_map/ppermute | solution.py:408
  28.8 6.8 %collective-permute-done.1.below_ref = bf16[288,512]{1,0:T(8,128)(2,1)S(1)} collective-permute-done((bf16[288,512]{1,0:T(8,128)(2,1)S(1)}, bf16[288,512]{1,0:T(8,128)(2,1)S(1)}, u32[]{:S(2)}, u32[]{:S(2)}) %collective-permute-start.1) | collective-permute-done | bytes 294944 | tf_op jit(solution)/shard_map/ppermute | solution.py:409
  35.7 0.0 copy-start.2
  35.7 0.7 copy-done.2
  36.4 0.0 collective-permute-done.above_ref
  36.4 0.0 copy-start.4
  36.4 0.7 copy-done.4
  37.1 0.0 all-to-all-done.edge_ref
  37.1 0.0 copy-done.9
  37.1 0.0 copy-done.1
  37.1 0.0 copy-done.8
  37.1 0.0 copy-start.3
  37.1 1.0 copy-done.3
  38.1 0.0 copy-start.5
  38.1 1.0 copy-done.5
  39.1 0.0 copy-start.10
  39.1 0.7 copy-done.10
  39.7 0.0 copy-start.11
  39.7 0.7 copy-done.11
  40.4 45.2 %transfer.1 = (bf16[288,384]{1,0:T(8,128)(2,1)S(1)}, bf16[288,512]{1,0:T(8,128)(2,1)S(1)}, bf16[288,512]{1,0:T(8,128)(2,1)S(1)}, bf16[16,16,384]{2,1,0:T(8,128)(2,1)S(1)}, bf16[768,128]{1,0:T(8,128)(2,1)S(1)}) custom-call(s32[1,384]{1,0:T(1,128)S(1)} %copy-done.9, f32[9,1,384]{2,1,0:T(1,128)S(1)} %copy-done.8, s32[1,24]{1,0:T(1,128)S(1)} %copy-done.10, ...), custom_call_target="tpu_custom_call" | custom-call | tf_op jit(solution)/shard_map/transfer/pallas_call | solution.py:414
  85.6 0.0 copy-start.12
  85.6 0.7 copy-done.12
  86.3 0.0 copy-start.13
  86.3 0.7 copy-done.13
  87.0 0.0 copy-start.6
  87.0 11.3 %all_to_all.21.rad_ref = bf16[4,192,128]{2,1,0:T(8,128)(2,1)S(1)} all-to-all(bf16[4,192,128]{2,1,0:T(8,128)(2,1)S(1)} %bitcast.8), channel_id=1, replica_groups=mesh['groups'=2,'lat'=4,'lon'=4] {'lat'}, dimensions={0} | all-to-all | bytes 393216 | tf_op jit(solution)/shard_map/all_to_all | solution.py:459
  98.3 0.0 copy-done.6
  98.3 3.6 %all-to-all-start.2 = ((bf16[16,16,384]{2,1,0:T(8,128)(2,1)}), bf16[16,16,384]{2,1,0:T(8,128)(2,1)S(1)}, u32[]{:S(2)}, u32[]{:S(2)}) async-start(bf16[16,16,384]{2,1,0:T(8,128)(2,1)} %copy-done.6), calls=%async_computation.2 | async-start | bytes 393216 | tf_op jit(solution)/shard_map/all_to_all | solution.py:458
  101.9 3.8 %collective-permute-start.2 = (bf16[288,512]{1,0:T(8,128)(2,1)}, bf16[288,512]{1,0:T(8,128)(2,1)S(1)}, u32[]{:S(2)}, u32[]{:S(2)}) collective-permute-start(bf16[288,512]{1,0:T(8,128)(2,1)} %copy-done.13), channel_id=1, source_target_pairs={{0,4},{4,8},{8,12},{1,5},{5,9},{9,13},{2,6},{6,10},{10,14},{3,7},{... | collective-permute-start | bytes 884744 | tf_op jit(solution)/shard_map/ppermute | solution.py:457
  105.7 1.3 %collective-permute-start.3 = (bf16[288,512]{1,0:T(8,128)(2,1)}, bf16[288,512]{1,0:T(8,128)(2,1)S(1)}, u32[]{:S(2)}, u32[]{:S(2)}) collective-permute-start(bf16[288,512]{1,0:T(8,128)(2,1)} %copy-done.12), channel_id=1, source_target_pairs={{4,0},{8,4},{12,8},{5,1},{9,5},{13,9},{6,2},{10,6},{14,10},{7,3},{... | collective-permute-start | bytes 884744 | tf_op jit(solution)/shard_map/ppermute | solution.py:456
  107.0 5.6 %collective-permute-done.2.from_above_ref = bf16[288,512]{1,0:T(8,128)(2,1)S(1)} collective-permute-done((bf16[288,512]{1,0:T(8,128)(2,1)}, bf16[288,512]{1,0:T(8,128)(2,1)S(1)}, u32[]{:S(2)}, u32[]{:S(2)}) %collective-permute-start.2) | collective-permute-done | bytes 294944 | tf_op jit(solution)/shard_map/ppermute | solution.py:457
  112.6 4.0 %collective-permute-done.3.from_below_ref = bf16[288,512]{1,0:T(8,128)(2,1)S(1)} collective-permute-done((bf16[288,512]{1,0:T(8,128)(2,1)}, bf16[288,512]{1,0:T(8,128)(2,1)S(1)}, u32[]{:S(2)}, u32[]{:S(2)}) %collective-permute-start.3) | collective-permute-done | bytes 294944 | tf_op jit(solution)/shard_map/ppermute | solution.py:456
  116.6 0.0 all-to-all-done.2.edge_ref
  116.6 5.8 %scatter.1 = (f32[2192,512]{1,0:T(8,128)}, f32[1,192,128]{2,1,0:T(8,128)}) custom-call(s32[1,384]{1,0:T(1,128)S(1)} %copy-done.9, f32[9,1,384]{2,1,0:T(1,128)S(1)} %copy-done.8, bf16[288,384]{1,0:T(8,128)(2,1)S(1)} %get-tuple-element.19.grad_ref, bf16[288,512]{1,0:T(8,128)(2,1)S(1)} %collective-permute-done.2.from_above_ref, ...), custom_call_target="tpu_custom_call" | custom-call | tf_op jit(solution)/shard_map/scatter/pallas_call | solution.py:461
Async XLA Ops:
  0.6 36.5 %copy-start.9 = (s32[1,384]{1,0:T(1,128)S(1)}, s32[1,384]{1,0:T(1,128)}, u32[]{:S(2)}) copy-start(s32[1,384]{1,0:T(1,128)} %cells_ref.3) | copy-start | bytes 4612
  0.6 1.6 %copy-start = (bf16[2,137,8,512]{3,2,1,0:T(8,128)(2,1)S(1)}, bf16[2,137,8,512]{3,2,1,0:T(8,128)(2,1)}, u32[]{:S(2)}) copy-start(bf16[2,137,8,512]{3,2,1,0:T(8,128)(2,1)} %param.7) | copy-start | bytes 6733828
  2.3 0.9 copy-start.7
  3.2 33.9 %copy-start.1 = (bf16[16,128,137]{1,0,2:T(8,128)(2,1)S(1)}, bf16[16,128,137]{1,0,2:T(8,128)(2,1)}, u32[]{:S(2)}) copy-start(bf16[16,128,137]{1,0,2:T(8,128)(2,1)} %param.12) | copy-start | bytes 1683460
  3.2 33.9 %copy-start.8 = (f32[9,1,384]{2,1,0:T(1,128)S(1)}, f32[9,1,384]{2,1,0:T(1,128)}, u32[]{:S(2)}) copy-start(f32[9,1,384]{2,1,0:T(1,128)} %weight_ref.3) | copy-start | bytes 41476
  19.2 17.9 %all-to-all-start = ((bf16[16,16,384]{2,1,0:T(8,128)(2,1)}), bf16[16,16,384]{2,1,0:T(8,128)(2,1)S(1)}, u32[]{:S(2)}, u32[]{:S(2)}) async-start(bf16[16,16,384]{2,1,0:T(8,128)(2,1)} %get-tuple-element.17), calls=%async_computation | async-start | bytes 393216 | tf_op jit(solution)/shard_map/all_to_all | solution.py:410
  23.0 12.7 %collective-permute-start.1 = (bf16[288,512]{1,0:T(8,128)(2,1)S(1)}, bf16[288,512]{1,0:T(8,128)(2,1)S(1)}, u32[]{:S(2)}, u32[]{:S(2)}) collective-permute-start(bf16[288,512]{1,0:T(8,128)(2,1)S(1)} %get-tuple-element.15.top_ref), channel_id=1, source_target_pairs={{4,0},{8,4},{12,8},{5,1},{9,5},{13,9},{6,2},{10,6},{14,10},{7,3},{... | collective-permute-start | bytes 884744 | tf_op jit(solution)/shard_map/ppermute | solution.py:409
  24.3 12.1 %collective-permute-start = (bf16[288,512]{1,0:T(8,128)(2,1)S(1)}, bf16[288,512]{1,0:T(8,128)(2,1)S(1)}, u32[]{:S(2)}, u32[]{:S(2)}) collective-permute-start(bf16[288,512]{1,0:T(8,128)(2,1)S(1)} %get-tuple-element.16.bottom_ref), channel_id=1, source_target_pairs={{0,4},{4,8},{8,12},{1,5},{5,9},{9,13},{2,6},{6,10},{10,14},{3,7},{... | collective-permute-start | bytes 884744 | tf_op jit(solution)/shard_map/ppermute | solution.py:408
  35.7 0.7 copy-start.2
  36.4 0.7 copy-start.4
  37.1 1.0 copy-start.3
  38.1 1.0 copy-start.5
  39.1 0.7 copy-start.10
  39.7 0.7 copy-start.11
  85.6 0.7 copy-start.12
  86.3 0.7 copy-start.13
  87.0 11.3 %copy-start.6 = (bf16[16,16,384]{2,1,0:T(8,128)(2,1)}, bf16[16,16,384]{2,1,0:T(8,128)(2,1)S(1)}, u32[]{:S(2)}) copy-start(bf16[16,16,384]{2,1,0:T(8,128)(2,1)S(1)} %get-tuple-element.22) | copy-start | bytes 589828
  98.3 18.3 %all-to-all-start.2 = ((bf16[16,16,384]{2,1,0:T(8,128)(2,1)}), bf16[16,16,384]{2,1,0:T(8,128)(2,1)S(1)}, u32[]{:S(2)}, u32[]{:S(2)}) async-start(bf16[16,16,384]{2,1,0:T(8,128)(2,1)} %copy-done.6), calls=%async_computation.2 | async-start | bytes 393216 | tf_op jit(solution)/shard_map/all_to_all | solution.py:458
  101.9 10.7 %collective-permute-start.2 = (bf16[288,512]{1,0:T(8,128)(2,1)}, bf16[288,512]{1,0:T(8,128)(2,1)S(1)}, u32[]{:S(2)}, u32[]{:S(2)}) collective-permute-start(bf16[288,512]{1,0:T(8,128)(2,1)} %copy-done.13), channel_id=1, source_target_pairs={{0,4},{4,8},{8,12},{1,5},{5,9},{9,13},{2,6},{6,10},{10,14},{3,7},{... | collective-permute-start | bytes 884744 | tf_op jit(solution)/shard_map/ppermute | solution.py:457
  105.7 10.9 %collective-permute-start.3 = (bf16[288,512]{1,0:T(8,128)(2,1)}, bf16[288,512]{1,0:T(8,128)(2,1)S(1)}, u32[]{:S(2)}, u32[]{:S(2)}) collective-permute-start(bf16[288,512]{1,0:T(8,128)(2,1)} %copy-done.12), channel_id=1, source_target_pairs={{4,0},{8,4},{12,8},{5,1},{9,5},{13,9},{6,2},{10,6},{14,10},{7,3},{... | collective-permute-start | bytes 884744 | tf_op jit(solution)/shard_map/ppermute | solution.py:456
where the time goes:
time: 123 us; the launch traced here: 122 us
  Pallas kernels  53.4 us (43%)
  blocking collectives  24.9 us (20%)
  starting transfers between devices  18.4 us (15%)
  waiting for transfers between devices  16.4 us (13%)
  local copies, waits for them, and re-layouts  8.61 us (7%)
    pallas_call x1, Pallas kernels, per_device(): pl.pallas_call(functools.partial(transfer_kernel, (levels, rows, width, p...  45.2 us
    all_to_all x1, blocking collectives, per_device(): lax.all_to_all(cot, 'lat', 0, 0, tiled=True).reshape(n_lat * proc, channels)  13.6 us
    all_to_all x1, blocking collectives, per_device(): lax.all_to_all(rad.reshape(n_lat, proc, channels), 'lat', 0, 0, tiled=True)  11.3 us
    unnamed x28, local copies, waits for them, and re-layouts  8.61 us
    ppermute x1, waiting for transfers between devices, per_device(): below = lax.ppermute(top, 'lat', down)  6.85 us
    pallas_call x1, Pallas kernels, per_device(): pl.pallas_call(functools.partial(scatter_kernel, (levels, rows, width, pa...  5.78 us
    ppermute x1, waiting for transfers between devices, per_device(): from_above = lax.ppermute(grad_below, 'lat', up)  5.56 us
    ppermute x1, starting transfers between devices, per_device(): above = lax.ppermute(bottom, 'lat', up)  4.56 us
  transfers between devices with their start and end apart: 6, of which 3 were waited for; matrix products, arithmetic and copies ran while one was open for 0% of the time, Pallas kernels for 0%

commit v1 on v0

v1 whole, which is shorter than its diff:
```python
import functools

import jax
import jax.numpy as jnp
from jax import lax
from jax.experimental import pallas as pl
from jax.experimental.pallas import tpu as pltpu
from jax.sharding import PartitionSpec as P

F32 = jnp.float32
BF16 = jnp.bfloat16
LOG2E = 1.4426950408889634
LANES = 128
EDGE = 16
BLOCKS = 3
VMEM = pl.BlockSpec(memory_space=pltpu.VMEM)
SMEM = pl.BlockSpec(memory_space=pltpu.SMEM)
NN = (((1,), (0,)), ((), ()))
NT = (((1,), (1,)), ((), ()))
TN = (((0,), (0,)), ((), ()))


def dot(a, b, dims=NN):
    return lax.dot_general(a, b, dims, preferred_element_type=F32)


def round_up(value, unit):
    return -(-value // unit) * unit


def params(mib=48):
    return pltpu.CompilerParams(vmem_limit_bytes=mib * 1024 * 1024)


def iota(shape, dim):
    return lax.broadcasted_iota(jnp.int32, shape, dim)


def split_cells(cells, width):
    if width & (width - 1) == 0:
        return lax.shift_right_logical(cells, width.bit_length() - 1), cells & (width - 1)
    row = lax.div(cells, width)
    return row, cells - row * width


def fill_columns(cells_ref, weight_ref, columns_ref):
    width, obs = columns_ref.shape[1:]
    _, col = split_cells(cells_ref[...], width)
    weights = [weight_ref[k] for k in range(9)]
    step = 32

    def chunk(i, carry):
        base = pl.multiple_of(i * step, step)
        for lane in range(0, obs, LANES):
            part = slice(lane, lane + LANES)
            away = iota((step, LANES), 0) + base - col[:, part]
            hit = [away == b - 1 for b in range(3)]
            for a in range(3):
                value = jnp.zeros((step, LANES), F32)
                for b in range(3):
                    value = jnp.where(hit[b], weights[3 * a + b][:, part], value)
                columns_ref[a, pl.ds(base, step), part] = value.astype(BF16)
        return carry

    lax.fori_loop(0, width // step, chunk, 0)


def row_stencil(columns_ref, row_of, r):
    total = None
    for a in range(3):
        keep = jnp.where(row_of == r - a + 1, 1.0, 0.0).astype(BF16)
        term = columns_ref[a] * keep
        total = term if total is None else total + term
    return total


def edge_weights(cells_ref, weight_ref, rows, width):
    lines = BLOCKS * EDGE
    obs = cells_ref.shape[1]
    row, col = split_cells(cells_ref[...], width)
    line = iota((lines, obs), 0)
    block = lax.shift_right_logical(line, 4)
    k = line & (EDGE - 1)
    none = -99
    west = k >= rows
    col_at = jnp.where(west, -1, width)
    row_at = jnp.where(west, k - rows, k)
    row_at = jnp.where(block == 1, jnp.where(row_at == rows - 1, -1, none), row_at)
    row_at = jnp.where(block == 2, jnp.where(row_at == 0, rows, none), row_at)
    total = jnp.zeros((lines, obs), F32)
    for a in range(3):
        for b in range(3):
            hit = (row_at == row + (a - 1)) & (col_at == col + (b - 1))
            total = total + jnp.where(hit, weight_ref[3 * a + b], 0.0)
    return total.astype(BF16)


def pack_kernel(dims, profiles_ref, mid_ref, top_ref, bottom_ref, edge_ref, wide_ref):
    levels, rows, width, pad = dims
    for lane in range(0, width, LANES):
        part = profiles_ref[:, :, lane : lane + LANES]
        wide_ref[lane // LANES] = part.astype(F32).reshape(2 * levels * rows, LANES)
    edges = jnp.zeros((EDGE, 2 * pad), F32)
    k = iota((EDGE, LANES), 0)
    at_lane = iota((EDGE, LANES), 1)
    for r in range(rows):
        out = top_ref if r == 0 else bottom_ref if r == rows - 1 else mid_ref.at[r - 1]
        for v in range(2):
            for lane in range(0, width, LANES):
                value = wide_ref[lane // LANES, pl.ds(v * levels * rows + r, levels, stride=rows), :]
                value = jnp.concatenate([value, jnp.zeros((pad - levels, LANES), F32)], axis=0)
                out[v * pad : (v + 1) * pad, lane : lane + LANES] = value.astype(BF16)
        west = jnp.where((k == r) & (at_lane == 0), 1.0, 0.0).astype(BF16)
        east = jnp.where((k == rows + r) & (at_lane == LANES - 1), 1.0, 0.0).astype(BF16)
        edges = edges + dot(west, out[:, :LANES], NT) + dot(east, out[:, width - LANES :], NT)
    edge_ref[...] = jnp.zeros(edge_ref.shape, BF16)
    edge_ref[:, : 2 * pad] = edges.astype(BF16)


def blend_kernel(rows, cot_ref, from_west_ref, from_east_ref, send_ref, edge_ref):
    proc = cot_ref.shape[1]
    west = iota(edge_ref.shape, 0) >= rows
    edge = jnp.where(west, from_west_ref[...].astype(F32), from_east_ref[...].astype(F32)).astype(BF16)
    edge_ref[...] = edge
    cot = cot_ref[0].astype(BF16)

    def share(s, carry):
        send_ref[s, 0:proc, :] = cot
        for t in range(edge.shape[1] // LANES):
            send_ref[s, proc + EDGE * t : proc + EDGE * (t + 1), :] = edge[:, t * LANES : (t + 1) * LANES]
        return carry

    lax.fori_loop(0, send_ref.shape[0], share, 0)


def lat_block(ref, proc, side):
    at = lax.axis_index("lat") + side
    valid = (at >= 0) & (at < ref.shape[0])
    at = jnp.where(valid, at, 0)
    keep = jnp.where(valid, 1.0, 0.0)
    parts = [ref[at, proc + EDGE * t : proc + EDGE * (t + 1), :] for t in range((ref.shape[1] - proc) // EDGE)]
    return [part.astype(F32) * keep for part in parts]


def gather_rows(rows, row, columns_ref, mid_ref, top_ref, bottom_ref, field_ref):
    for r in range(rows):
        source = top_ref if r == 0 else bottom_ref if r == rows - 1 else mid_ref.at[r - 1]
        value = dot(source[...], row_stencil(columns_ref, row, r))
        if r == 0:
            field_ref[...] = value
        else:
            field_ref[...] += value


def gather_halo(rows, row, columns_ref, above_ref, below_ref, field_ref):
    field_ref[...] += dot(above_ref[...], row_stencil(columns_ref, row, -1))
    field_ref[...] += dot(below_ref[...], row_stencil(columns_ref, row, rows))


def gather_edges(pad, proc, edge_ref, lat_ref, halo_ref, edge_w, field_ref):
    halo_ref[0:EDGE, :] = edge_ref[...].astype(F32)
    for n, side in enumerate((-1, 1)):
        for t, part in enumerate(lat_block(lat_ref, proc, side)):
            halo_ref[(n + 1) * EDGE : (n + 2) * EDGE, t * LANES : (t + 1) * LANES] = part
    field_ref[...] += dot(halo_ref[:, : 2 * pad].astype(BF16), edge_w, TN)


def departures(batch, proc, dest_ref, lat_ref, cot_rows_ref, cot_t_ref):
    obs = cot_rows_ref.shape[0]
    owned = proc // batch
    for q in range(obs // batch):
        where = dest_ref[0, q]
        slot = jnp.maximum(where, 0)
        lat = lax.div(slot, owned)
        start = pl.multiple_of((slot - lat * owned) * batch, batch)
        value = lat_ref[lat, pl.ds(start, batch), :].astype(F32)
        cot_rows_ref[q * batch : (q + 1) * batch, :] = jnp.where(where >= 0, value, 0.0)
    for lane in range(0, obs, LANES):
        cot_t_ref[:, lane : lane + LANES] = cot_rows_ref[lane : lane + LANES, :].T


def chosen_instruments(batch, obs, instr_ref):
    lane_slot = lax.shift_right_logical(iota((1, obs), 1), batch.bit_length() - 1)
    chosen = jnp.zeros((1, obs), jnp.int32)
    for q in range(obs // batch):
        chosen = jnp.where(lane_slot == q, instr_ref[0, q], chosen)
    return chosen


def turn_absorption(absorb_ref, turned_ref):
    levels, instruments, channels = absorb_ref.shape
    per = LANES // instruments
    for b in range(turned_ref.shape[0]):
        count = min(per, levels - b * per)
        block = absorb_ref[b * per : b * per + count].astype(F32).reshape(count * instruments, channels)
        if count < per:
            block = jnp.concatenate([block, jnp.zeros(((per - count) * instruments, channels), F32)], axis=0)
        turned_ref[b] = block.T


def prepare_levels(pad, field_ref, step_ref, rate_ref):
    step_ref[...] = field_ref[1 : pad + 1, :] - field_ref[0:pad, :]
    rate_ref[...] = -LOG2E * (1.0 + 0.5 * jnp.tanh(field_ref[pad : 2 * pad, :]))


def walk_levels(levels, instruments, chosen, turned_ref, cot_t_ref, rate_ref, step_ref, signal_ref, s_part_ref, r_part_ref):
    channels, obs = cot_t_ref.shape
    groups, padded, _ = s_part_ref.shape
    per = LANES // instruments
    tail = jnp.zeros((groups, padded - levels * 8, LANES), F32)
    s_part_ref[:, levels * 8 :, :] = tail
    r_part_ref[:, levels * 8 :, :] = tail
    for lane in range(0, obs, LANES):
        lanes = slice(lane, lane + LANES)
        group = lane // LANES

        def level(b, row_base, j, rates, steps, cum, signal):
            index = jnp.broadcast_to(chosen[:, lanes] + instruments * j, (8, LANES))
            a = jnp.concatenate(
                [
                    jnp.take_along_axis(turned_ref[b, c : c + 8, :], index, axis=1, mode="promise_in_bounds")
                    for c in range(0, channels, 8)
                ],
                axis=0,
            )
            cot = cot_t_ref[:, lanes]
            cum = cum + a * rates[j : j + 1]
            transmit = jnp.exp2(cum)
            at = pl.ds(pl.multiple_of(row_base + 8 * j, 8), 8)
            r_part_ref[group, at, :] = jnp.sum((cot * signal * a).reshape(channels // 8, 8, LANES), axis=0)
            s_part_ref[group, at, :] = jnp.sum((cot * transmit).reshape(channels // 8, 8, LANES), axis=0)
            signal = signal + transmit * steps[j : j + 1]
            return cum, signal

        def block(b, carry):
            cum, signal = carry
            base = pl.multiple_of(b * per, per)
            rates = rate_ref[pl.ds(base, per), lanes]
            steps = step_ref[pl.ds(base, per), lanes]
            for j in range(per):
                cum, signal = level(b, b * (8 * per), j, rates, steps, cum, signal)
            return cum, signal

        start = jnp.zeros((channels, LANES), F32)
        full = levels // per
        cum, signal = lax.fori_loop(0, full, block, (start, start))
        if levels % per:
            rates = rate_ref[full * per : (full + 1) * per, lanes]
            steps = step_ref[full * per : (full + 1) * per, lanes]
            for j in range(levels % per):
                cum, signal = level(full, full * (8 * per), j, rates, steps, cum, signal)
        signal_ref[:, lanes] = signal


def radiances(batch, proc, dest_ref, signal_ref, field_ref, send_ref):
    obs = signal_ref.shape[1]
    owned = proc // batch
    send_ref[...] = jnp.zeros(send_ref.shape, BF16)
    for lane in range(0, obs, LANES):
        lanes = slice(lane, lane + LANES)
        value = (signal_ref[:, lanes] + field_ref[0:1, lanes]).T.astype(BF16)
        for q in range(LANES // batch):
            where = dest_ref[0, lane // batch + q]

            @pl.when(where >= 0)
            def _():
                lat = lax.div(where, owned)
                start = pl.multiple_of((where - lat * owned) * batch, batch)
                send_ref[lat, pl.ds(start, batch), :] = value[q * batch : (q + 1) * batch, :]


def held_part(levels, pick, absorb_ref, cot_t_ref, signal_ref, r_part_ref):
    channels, obs = cot_t_ref.shape
    instruments = absorb_ref.shape[1]
    held = cot_t_ref[...] * signal_ref[...]
    held_hi = held.astype(BF16)
    held_lo = (held - held_hi.astype(F32)).astype(BF16)

    def contract(l0, count):
        rows_in = absorb_ref[pl.ds(l0, count)].reshape(count * instruments, channels)
        value = dot(rows_in, held_hi) + dot(rows_in, held_lo)
        value = value.reshape(count, instruments, obs) * pick[None]
        value = jnp.sum(value.reshape(count, instruments // 8, 8, obs), axis=1)
        at = pl.ds(pl.multiple_of(l0 * 8, 8), count * 8)
        value = value.reshape(count * 8, obs)
        for lane in range(0, obs, LANES):
            r_part_ref[lane // LANES, at, :] -= value[:, lane : lane + LANES]

    def contract_block(b, carry):
        contract(b * 8, 8)
        return carry

    lax.fori_loop(0, levels // 8, contract_block, 0)
    if levels % 8:
        contract(levels // 8 * 8, levels % 8)


def gradients(pad, s_part_ref, r_part_ref, cot_t_ref, field_ref, shift_ref, grad_ref):
    obs = cot_t_ref.shape[1]
    for lane in range(0, obs, LANES):
        lanes = slice(lane, lane + LANES)
        group = lane // LANES
        s_sum = s_part_ref[group, pl.ds(0, pad, stride=8), :]
        r_sum = r_part_ref[group, pl.ds(0, pad, stride=8), :]
        for k in range(1, 8):
            s_sum = s_sum + s_part_ref[group, pl.ds(k, pad, stride=8), :]
            r_sum = r_sum + r_part_ref[group, pl.ds(k, pad, stride=8), :]
        shift_ref[7:8, lanes] = jnp.sum(cot_t_ref[:, lanes], axis=0, keepdims=True)
        shift_ref[8 : 8 + pad, lanes] = s_sum
        grad_ref[0:pad, lanes] = (shift_ref[7 : 7 + pad, lanes] - s_sum).astype(BF16)
        bent = jnp.tanh(field_ref[pad : 2 * pad, lanes])
        grad_ref[pad : 2 * pad, lanes] = (0.5 * (1.0 - bent * bent) * r_sum).astype(BF16)


def scatter_outside(rows, pad, proc, row, columns_ref, edge_w, grad_ref, above_ref, below_ref, edge_ref, send_ref):
    grad = grad_ref[...]
    above_ref[...] = dot(grad, row_stencil(columns_ref, row, -1), NT).astype(BF16)
    below_ref[...] = dot(grad, row_stencil(columns_ref, row, rows), NT).astype(BF16)
    out = dot(edge_w, grad, NT)
    edge_ref[...] = jnp.zeros(edge_ref.shape, F32)
    edge_ref[:, : 2 * pad] = out
    for n, side in enumerate((-1, 1)):
        at = lax.axis_index("lat") + side

        @pl.when((at >= 0) & (at < send_ref.shape[0]))
        def _():
            for t in range(edge_ref.shape[1] // LANES):
                part = edge_ref[(n + 1) * EDGE : (n + 2) * EDGE, t * LANES : (t + 1) * LANES]
                send_ref[at, proc + EDGE * t : proc + EDGE * (t + 1), :] = part.astype(BF16)


def gather_kernel(
    dims, cells_ref, weight_ref, absorb_ref, mid_ref, top_ref, bottom_ref, field_ref, turned_ref, columns_ref
):
    rows, width = dims
    fill_columns(cells_ref, weight_ref, columns_ref)
    row, _ = split_cells(cells_ref[...], width)
    gather_rows(rows, row, columns_ref, mid_ref, top_ref, bottom_ref, field_ref)
    turn_absorption(absorb_ref, turned_ref)


def transfer_kernel(
    dims,
    cells_ref,
    weight_ref,
    instr_ref,
    dest_ref,
    absorb_ref,
    field_in_ref,
    turned_ref,
    columns_ref,
    above_ref,
    below_ref,
    edge_ref,
    lat_ref,
    grad_ref,
    grad_above_ref,
    grad_below_ref,
    grad_edge_ref,
    send_ref,
    halo_ref,
    field_ref,
    rate_ref,
    step_ref,
    cot_rows_ref,
    cot_t_ref,
    signal_ref,
    s_part_ref,
    r_part_ref,
    shift_ref,
):
    levels, rows, width, pad, batch, proc = dims
    obs = cells_ref.shape[1]
    instruments = absorb_ref.shape[1]
    row, _ = split_cells(cells_ref[...], width)
    edge_w = edge_weights(cells_ref, weight_ref, rows, width)
    field_ref[...] = field_in_ref[...]
    gather_halo(rows, row, columns_ref, above_ref, below_ref, field_ref)
    gather_edges(pad, proc, edge_ref, lat_ref, halo_ref, edge_w, field_ref)
    departures(batch, proc, dest_ref, lat_ref, cot_rows_ref, cot_t_ref)
    chosen = chosen_instruments(batch, obs, instr_ref)
    prepare_levels(pad, field_ref, step_ref, rate_ref)
    walk_levels(
        levels, instruments, chosen, turned_ref, cot_t_ref, rate_ref, step_ref, signal_ref, s_part_ref, r_part_ref
    )
    radiances(batch, proc, dest_ref, signal_ref, field_ref, send_ref)
    pick = jnp.where(iota((instruments, obs), 0) == chosen, 1.0, 0.0)
    held_part(levels, pick, absorb_ref, cot_t_ref, signal_ref, r_part_ref)
    gradients(pad, s_part_ref, r_part_ref, cot_t_ref, field_ref, shift_ref, grad_ref)
    scatter_outside(
        rows, pad, proc, row, columns_ref, edge_w, grad_ref, grad_above_ref, grad_below_ref, halo_ref, send_ref
    )
    grad_edge_ref[...] = halo_ref[0:EDGE, :].astype(BF16)


def corner_kernel(proc, edge_ref, lat_ref, out_ref):
    ups, downs = lat_block(lat_ref, proc, -1), lat_block(lat_ref, proc, 1)
    for t in range(edge_ref.shape[1] // LANES):
        lanes = slice(t * LANES, (t + 1) * LANES)
        out_ref[:, lanes] = (edge_ref[:, lanes].astype(F32) + ups[t] + downs[t]).astype(BF16)


def scatter_kernel(
    dims,
    cells_ref,
    columns_ref,
    grad_ref,
    from_above_ref,
    from_below_ref,
    from_west_ref,
    from_east_ref,
    lat_ref,
    out_ref,
    rad_out_ref,
    halo_ref,
    wide_ref,
):
    levels, rows, width, pad, proc = dims
    rad_out_ref[...] = jnp.sum(lat_ref[:, 0:proc, :].astype(F32), axis=0)[None]
    row, _ = split_cells(cells_ref[...], width)
    west = iota(halo_ref.shape, 0) < rows
    halo_ref[...] = jnp.where(west, from_west_ref[...].astype(F32), from_east_ref[...].astype(F32))
    edges = halo_ref[:, : 2 * pad].T.astype(BF16)
    k = iota((EDGE, LANES), 0)
    at_lane = iota((EDGE, LANES), 1)
    for r in range(rows):
        value = dot(grad_ref[...], row_stencil(columns_ref, row, r), NT)
        if r == 0:
            value = value + from_above_ref[...].astype(F32)
        if r == rows - 1:
            value = value + from_below_ref[...].astype(F32)
        first_at = jnp.where((k == r) & (at_lane == 0), 1.0, 0.0).astype(BF16)
        last_at = jnp.where((k == rows + r) & (at_lane == LANES - 1), 1.0, 0.0).astype(BF16)
        first = value[:, :LANES] + dot(edges, first_at)
        last = value[:, width - LANES :] + dot(edges, last_at)
        value = jnp.concatenate([first, value[:, LANES : width - LANES], last], axis=1)
        for v in range(2):
            at = pl.ds(v * levels * rows + r, levels, stride=rows)
            for lane in range(0, width, LANES):
                wide_ref[lane // LANES, at, :] = value[v * pad : v * pad + levels, lane : lane + LANES]
    for lane in range(0, width, LANES):
        out_ref[:, lane : lane + LANES] = wide_ref[lane // LANES]


def per_device(profiles, obs_cell, obs_weight, batch_instr, batch_dest, absorption, cotangent):
    n_lat, n_lon = lax.axis_size("lat"), lax.axis_size("lon")
    levels, rows, width = profiles.shape[1:]
    instruments, channels, _ = absorption.shape
    obs = obs_cell.shape[1]
    slots = batch_dest.shape[1]
    batch = obs // slots
    proc = cotangent.shape[1]
    pad = round_up(levels, 16)
    feat = round_up(2 * pad, LANES)
    lat_rows = proc + EDGE * (feat // LANES)
    blocks = -(-levels * instruments // LANES)
    up = [(i, i + 1) for i in range(n_lat - 1)]
    down = [(b, a) for a, b in up]
    east = [(j, j + 1) for j in range(n_lon - 1)]
    west = [(b, a) for a, b in east]
    shape = jax.ShapeDtypeStruct
    row_shape = shape((2 * pad, width), BF16)
    edge_shape = shape((EDGE, feat), BF16)
    lat_shape = shape((n_lat, lat_rows, channels), BF16)
    absorb = jnp.transpose(absorption, (2, 0, 1))

    mid, top, bottom, edge = pl.pallas_call(
        functools.partial(pack_kernel, (levels, rows, width, pad)),
        out_shape=(shape((rows - 2, 2 * pad, width), BF16), row_shape, row_shape, edge_shape),
        in_specs=[VMEM],
        out_specs=(VMEM,) * 4,
        scratch_shapes=[pltpu.VMEM((width // LANES, 2 * levels * rows, LANES), F32)],
        compiler_params=params(),
        name="pack",
    )(profiles.reshape(2 * levels, rows, width))

    from_west = lax.ppermute(edge, "lon", east)
    from_east = lax.ppermute(edge, "lon", west)
    above = lax.ppermute(bottom, "lat", up)
    below = lax.ppermute(top, "lat", down)

    lat_send, side = pl.pallas_call(
        functools.partial(blend_kernel, rows),
        out_shape=(lat_shape, edge_shape),
        in_specs=[VMEM] * 3,
        out_specs=(VMEM,) * 2,
        compiler_params=params(),
        name="blend",
    )(cotangent, from_west, from_east)
    lat_in = lax.all_to_all(lat_send, "lat", 0, 0, tiled=True)

    field, turned, columns = pl.pallas_call(
        functools.partial(gather_kernel, (rows, width)),
        out_shape=(
            shape((2 * pad, obs), F32),
            shape((blocks, channels, LANES), F32),
            shape((3, width, obs), BF16),
        ),
        in_specs=[VMEM] * 6,
        out_specs=(VMEM,) * 3,
        compiler_params=params(),
        name="gather",
    )(obs_cell, obs_weight, absorb, mid, top, bottom)

    grad, grad_above, grad_below, grad_edge, lat_back = pl.pallas_call(
        functools.partial(transfer_kernel, (levels, rows, width, pad, batch, proc)),
        out_shape=(shape((2 * pad, obs), BF16), row_shape, row_shape, edge_shape, lat_shape),
        in_specs=[VMEM, VMEM, SMEM, SMEM] + [VMEM] * 8,
        out_specs=(VMEM,) * 5,
        scratch_shapes=[
            pltpu.VMEM((BLOCKS * EDGE, feat), F32),
            pltpu.VMEM((2 * pad, obs), F32),
            pltpu.VMEM((pad, obs), F32),
            pltpu.VMEM((pad, obs), F32),
            pltpu.VMEM((obs, channels), F32),
            pltpu.VMEM((channels, obs), F32),
            pltpu.VMEM((channels, obs), F32),
            pltpu.VMEM((obs // LANES, pad * 8, LANES), F32),
            pltpu.VMEM((obs // LANES, pad * 8, LANES), F32),
            pltpu.VMEM((pad + 8, obs), F32),
        ],
        compiler_params=params(),
        name="transfer",
    )(
        obs_cell,
        obs_weight,
        batch_instr,
        batch_dest,
        absorb,
        field,
        turned,
        columns,
        above,
        below,
        side,
        lat_in,
    )

    from_below = lax.ppermute(grad_above, "lat", down)
    from_above = lax.ppermute(grad_below, "lat", up)
    lat_got = lax.all_to_all(lat_back, "lat", 0, 0, tiled=True)
    grad_side = pl.pallas_call(
        functools.partial(corner_kernel, proc),
        out_shape=edge_shape,
        in_specs=[VMEM] * 2,
        out_specs=VMEM,
        compiler_params=params(),
        name="corner",
    )(grad_edge, lat_got)
    grad_from_west = lax.ppermute(grad_side, "lon", east)
    grad_from_east = lax.ppermute(grad_side, "lon", west)

    gradient, radiance = pl.pallas_call(
        functools.partial(scatter_kernel, (levels, rows, width, pad, proc)),
        out_shape=(
            shape((2 * levels * rows, width), F32),
            shape((1, proc, channels), F32),
        ),
        in_specs=[VMEM] * 8,
        out_specs=(VMEM,) * 2,
        scratch_shapes=[
            pltpu.VMEM((EDGE, feat), F32),
            pltpu.VMEM((width // LANES, 2 * levels * rows, LANES), F32),
        ],
        compiler_params=params(),
        name="scatter",
    )(obs_cell, columns, grad, from_above, from_below, grad_from_west, grad_from_east, lat_got)
    return radiance, gradient.reshape(2, levels, rows, width)


def solution(mesh):
    placed = (
        P("groups", None, "lat", "lon"),
        P(("groups", "lon"), "lat"),
        P("groups", "lon", "lat"),
        P(("groups", "lon"), "lat"),
        P(("groups", "lon"), "lat"),
        P(),
        P(("groups", "lon"), "lat", None),
    )
    return jax.shard_map(
        per_device,
        mesh=mesh,
        in_specs=placed,
        out_specs=(P(("groups", "lon"), "lat", None), P("groups", None, "lat", "lon")),
        check_vma=False,
    )
```

time: 123 us -> 82.4 us (0.67)
  blocking collectives: 24.9 us -> 0 us
  Pallas kernels: 53.4 us -> 32.5 us
  starting transfers between devices: 18.4 us -> 29.8 us
  waiting for transfers between devices: 16.4 us -> 9.58 us
    all_to_all x2 -> x0, blocking collectives: 24.9 us -> none  [the longest x1 13.6 us: per_device(): lax.all_to_all(cot, 'lat', 0, 0, tiled=True).reshape(n_lat * proc, channels)]
    pallas_call x1, Pallas kernels: 45.2 us -> 21.2 us  [per_device(): pl.pallas_call(functools.partial(transfer_kernel, (levels, rows, width, p...]
    ppermute x0 -> x4, starting transfers between devices: none -> 8.77 us  [the longest x1 3.03 us: per_device(): grad_from_west = lax.ppermute(grad_side, 'lon', east)]
    ppermute x1, waiting for transfers between devices: 5.56 us -> 0.01 us  [per_device(): from_above = lax.ppermute(grad_below, 'lat', up)]
    pallas_call x0 -> x3, Pallas kernels: none -> 3.87 us  [the longest x1 3.12 us: per_device(): pl.pallas_call(functools.partial(gather_kernel, (rows, width)), out_shape...]
    all_to_all x2, waiting for transfers between devices: 0.01 us -> 3.73 us  [the longest x1 3.73 us: per_device(): lat_got = lax.all_to_all(lat_back, 'lat', 0, 0, tiled=True)]
    ppermute x1, waiting for transfers between devices: 6.85 us -> 3.66 us  [per_device(): below = lax.ppermute(top, 'lat', down)]
    ppermute x1, waiting for transfers between devices: 4.02 us -> 1.37 us  [per_device(): from_below = lax.ppermute(grad_above, 'lat', down)]
  transfers between devices with their start and end apart: 6 -> 10, of which waited for: 3 -> 4; matrix products, arithmetic and copies ran while one was open for 0% -> 0% of each run, Pallas kernels for 0% -> 4%
where the time goes in v1:
time: 82.4 us; the launch traced here: 81.8 us
  Pallas kernels  32.5 us (39%)
  starting transfers between devices  29.8 us (36%)
  waiting for transfers between devices  9.58 us (12%)
  local copies, waits for them, and re-layouts  9.07 us (11%)
    pallas_call x1, Pallas kernels, per_device(): pl.pallas_call(functools.partial(transfer_kernel, (levels, rows, width, p...  21.2 us
    unnamed x30, local copies, waits for them, and re-layouts  9.07 us
    all_to_all x1, starting transfers between devices, per_device(): lat_in = lax.all_to_all(lat_send, 'lat', 0, 0, tiled=True)  6.32 us
    pallas_call x1, Pallas kernels, per_device(): pl.pallas_call(functools.partial(scatter_kernel, (levels, rows, width, pa...  5.19 us
    ppermute x1, starting transfers between devices, per_device(): above = lax.ppermute(bottom, 'lat', up)  4.57 us
    ppermute x1, starting transfers between devices, per_device(): from_above = lax.ppermute(grad_below, 'lat', up)  3.93 us
    all_to_all x1, waiting for transfers between devices, per_device(): lat_got = lax.all_to_all(lat_back, 'lat', 0, 0, tiled=True)  3.73 us
    ppermute x1, waiting for transfers between devices, per_device(): below = lax.ppermute(top, 'lat', down)  3.66 us
  transfers between devices with their start and end apart: 10, of which 4 were waited for; matrix products, arithmetic and copies ran while one was open for 0% of the time, Pallas kernels for 4%

profile of v1, /device:TPU:0, one launch (start us, length us, event | category | flops | bytes accessed | tf_op | source)
XLA Modules:
  0.0 81.8 jit_solution(15917015568637127344)
XLA Ops:
  0.6 0.0 copy-start.12
  0.6 0.0 copy-start
  0.7 1.6 %copy-done = bf16[2,137,8,512]{3,2,1,0:T(8,128)(2,1)S(1)} copy-done((bf16[2,137,8,512]{3,2,1,0:T(8,128)(2,1)S(1)}, bf16[2,137,8,512]{3,2,1,0:T(8,128)(2,1)}, u32[]{:S(2)}) %copy-start) | copy-done | bytes 2244632
  2.3 0.0 copy-start.10
  2.3 0.0 copy-start.1
  2.3 0.0 copy-start.11
  2.3 2.2 %pack.1 = (bf16[6,288,512]{2,1,0:T(8,128)(2,1)S(1)}, bf16[288,512]{1,0:T(8,128)(2,1)}, bf16[288,512]{1,0:T(8,128)(2,1)}, bf16[16,384]{1,0:T(8,128)(2,1)S(1)}) custom-call(bf16[274,8,512]{2,1,0:T(8,128)(2,1)S(1)} %bitcast.3), custom_call_target="tpu_custom_call" | custom-call | tf_op jit(solution)/shard_map/pack/pallas_call | solution.py:467
  4.5 0.0 copy-start.13
  4.5 0.0 copy-start.14
  4.5 1.4 %collective-permute-start.3 = (bf16[16,384]{1,0:T(8,128)(2,1)S(1)}, bf16[16,384]{1,0:T(8,128)(2,1)S(1)}, u32[]{:S(2)}, u32[]{:S(2)}) collective-permute-start(bf16[16,384]{1,0:T(8,128)(2,1)S(1)} %get-tuple-element.24), channel_id=1, source_target_pairs={{1,0},{2,1},{3,2},{5,4},{6,5},{7,6},{9,8},{10,9},{11,10},{13,12},{... | collective-permute-start | bytes 36872 | tf_op jit(solution)/shard_map/ppermute | solution.py:478
  6.0 3.0 %collective-permute-start.2 = (bf16[16,384]{1,0:T(8,128)(2,1)S(1)}, bf16[16,384]{1,0:T(8,128)(2,1)S(1)}, u32[]{:S(2)}, u32[]{:S(2)}) collective-permute-start(bf16[16,384]{1,0:T(8,128)(2,1)S(1)} %get-tuple-element.24), channel_id=1, source_target_pairs={{0,1},{1,2},{2,3},{4,5},{5,6},{6,7},{8,9},{9,10},{10,11},{12,13},{... | collective-permute-start | bytes 36872 | tf_op jit(solution)/shard_map/ppermute | solution.py:477
  9.0 0.0 collective-permute-done.3.from_east_ref
  9.0 0.8 collective-permute-done.2.from_west_ref
  9.8 0.0 copy-done.10
  9.8 0.7 blend.1
  10.6 6.3 %all-to-all-start = ((bf16[4,240,128]{2,1,0:T(8,128)(2,1)}), bf16[4,240,128]{2,1,0:T(8,128)(2,1)}, u32[]{:S(2)}, u32[]{:S(2)}) async-start(bf16[4,240,128]{2,1,0:T(8,128)(2,1)} %get-tuple-element.26), calls=%async_computation | async-start | bytes 491520 | tf_op jit(solution)/shard_map/all_to_all | solution.py:490
  16.9 1.3 %collective-permute-start.1 = (bf16[288,512]{1,0:T(8,128)(2,1)}, bf16[288,512]{1,0:T(8,128)(2,1)S(1)}, u32[]{:S(2)}, u32[]{:S(2)}) collective-permute-start(bf16[288,512]{1,0:T(8,128)(2,1)} %get-tuple-element.19.top_ref), channel_id=1, source_target_pairs={{4,0},{8,4},{12,8},{5,1},{9,5},{13,9},{6,2},{10,6},{14,10},{7,3},{... | collective-permute-start | bytes 884744 | tf_op jit(solution)/shard_map/ppermute | solution.py:480
  18.2 4.6 %collective-permute-start = (bf16[288,512]{1,0:T(8,128)(2,1)}, bf16[288,512]{1,0:T(8,128)(2,1)S(1)}, u32[]{:S(2)}, u32[]{:S(2)}) collective-permute-start(bf16[288,512]{1,0:T(8,128)(2,1)} %get-tuple-element.20.bottom_ref), channel_id=1, source_target_pairs={{0,4},{4,8},{8,12},{1,5},{5,9},{9,13},{2,6},{6,10},{10,14},{3,7},{... | collective-permute-start | bytes 884744 | tf_op jit(solution)/shard_map/ppermute | solution.py:479
  22.7 0.0 copy-done.12
  22.8 0.0 copy-done.1
  22.8 0.0 copy-done.11
  22.8 3.1 %gather.1 = (f32[288,384]{1,0:T(8,128)S(1)}, f32[18,128,128]{2,1,0:T(8,128)S(1)}, bf16[3,512,384]{2,1,0:T(8,128)(2,1)S(1)}) custom-call(s32[1,384]{1,0:T(1,128)S(1)} %copy-done.12, f32[9,1,384]{2,1,0:T(1,128)S(1)} %copy-done.11, bf16[137,16,128]{2,1,0:T(8,128)(2,1)S(1)} %bitcast.4, bf16[6,288,512]{2,1,0:T(8,128)(2,1)S(1)} %get-tuple-element.18.mid_ref, ...), custom_call_target="tpu_custom_call" | custom-call | tf_op jit(solution)/shard_map/gather/pallas_call | solution.py:492
  25.9 0.0 copy-start.2
  25.9 1.0 %copy-done.2 = f32[18,128,128]{2,1,0:T(8,128)} copy-done((f32[18,128,128]{2,1,0:T(8,128)}, f32[18,128,128]{2,1,0:T(8,128)S(1)}, u32[]{:S(2)}) %copy-start.2) | copy-done | bytes 1179672
  26.9 0.0 copy-start.4
  26.9 0.8 copy-done.4
  27.7 3.7 %collective-permute-done.1.below_ref = bf16[288,512]{1,0:T(8,128)(2,1)S(1)} collective-permute-done((bf16[288,512]{1,0:T(8,128)(2,1)}, bf16[288,512]{1,0:T(8,128)(2,1)S(1)}, u32[]{:S(2)}, u32[]{:S(2)}) %collective-permute-start.1) | collective-permute-done | bytes 294944 | tf_op jit(solution)/shard_map/ppermute | solution.py:480
  31.3 0.0 copy-start.6
  31.3 0.7 copy-done.6
  32.1 0.0 collective-permute-done.above_ref
  32.1 0.0 copy-start.8
  32.1 0.7 copy-done.8
  32.8 0.0 all-to-all-done.lat_ref
  32.8 0.0 copy-done.13
  32.8 0.0 copy-done.14
  32.8 0.0 copy-start.3
  32.8 1.3 %copy-done.3 = f32[18,128,128]{2,1,0:T(8,128)S(1)} copy-done((f32[18,128,128]{2,1,0:T(8,128)S(1)}, f32[18,128,128]{2,1,0:T(8,128)}, u32[]{:S(2)}) %copy-start.3) | copy-done | bytes 1179672
  34.1 0.0 copy-start.5
  34.1 1.0 %copy-done.5 = f32[288,384]{1,0:T(8,128)S(1)} copy-done((f32[288,384]{1,0:T(8,128)S(1)}, f32[288,384]{1,0:T(8,128)}, u32[]{:S(2)}) %copy-start.5) | copy-done | bytes 442392
  35.1 0.0 copy-start.7
  35.1 1.0 %copy-done.7 = bf16[288,512]{1,0:T(8,128)(2,1)S(1)} copy-done((bf16[288,512]{1,0:T(8,128)(2,1)S(1)}, bf16[288,512]{1,0:T(8,128)(2,1)}, u32[]{:S(2)}) %copy-start.7) | copy-done | bytes 294936
  36.1 0.0 copy-start.9
  36.1 1.0 %copy-done.9 = bf16[288,512]{1,0:T(8,128)(2,1)S(1)} copy-done((bf16[288,512]{1,0:T(8,128)(2,1)S(1)}, bf16[288,512]{1,0:T(8,128)(2,1)}, u32[]{:S(2)}) %copy-start.9) | copy-done | bytes 294936
  37.0 21.2 %transfer.1 = (bf16[288,384]{1,0:T(8,128)(2,1)S(1)}, bf16[288,512]{1,0:T(8,128)(2,1)S(1)}, bf16[288,512]{1,0:T(8,128)(2,1)S(1)}, bf16[16,384]{1,0:T(8,128)(2,1)S(1)}, bf16[4,240,128]{2,1,0:T(8,128)(2,1)}) custom-call(s32[1,384]{1,0:T(1,128)S(1)} %copy-done.12, f32[9,1,384]{2,1,0:T(1,128)S(1)} %copy-done.11, s32[1,24]{1,0:T(1,128)S(1)} %copy-done.13, ...), custom_call_target="tpu_custom_call" | custom-call | tf_op jit(solution)/shard_map/transfer/pallas_call | solution.py:505
  58.2 3.7 %all-to-all-start.1 = ((bf16[4,240,128]{2,1,0:T(8,128)(2,1)}), bf16[4,240,128]{2,1,0:T(8,128)(2,1)S(1)}, u32[]{:S(2)}, u32[]{:S(2)}) async-start(bf16[4,240,128]{2,1,0:T(8,128)(2,1)} %get-tuple-element.31), calls=%async_computation.1 | async-start | bytes 491520 | tf_op jit(solution)/shard_map/all_to_all | solution.py:541
  61.9 3.9 %collective-permute-start.4 = (bf16[288,512]{1,0:T(8,128)(2,1)S(1)}, bf16[288,512]{1,0:T(8,128)(2,1)S(1)}, u32[]{:S(2)}, u32[]{:S(2)}) collective-permute-start(bf16[288,512]{1,0:T(8,128)(2,1)S(1)} %get-tuple-element.28), channel_id=1, source_target_pairs={{0,4},{4,8},{8,12},{1,5},{5,9},{9,13},{2,6},{6,10},{10,14},{3,7},{... | collective-permute-start | bytes 884744 | tf_op jit(solution)/shard_map/ppermute | solution.py:540
  65.8 1.3 %collective-permute-start.5 = (bf16[288,512]{1,0:T(8,128)(2,1)S(1)}, bf16[288,512]{1,0:T(8,128)(2,1)S(1)}, u32[]{:S(2)}, u32[]{:S(2)}) collective-permute-start(bf16[288,512]{1,0:T(8,128)(2,1)S(1)} %get-tuple-element.29), channel_id=1, source_target_pairs={{4,0},{8,4},{12,8},{5,1},{9,5},{13,9},{6,2},{10,6},{14,10},{7,3},{... | collective-permute-start | bytes 884744 | tf_op jit(solution)/shard_map/ppermute | solution.py:539
  67.1 3.7 %all-to-all-done.1.lat_ref = bf16[4,240,128]{2,1,0:T(8,128)(2,1)S(1)} async-done(((bf16[4,240,128]{2,1,0:T(8,128)(2,1)}), bf16[4,240,128]{2,1,0:T(8,128)(2,1)S(1)}, u32[]{:S(2)}, u32[]{:S(2)}) %all-to-all-start.1) | async-done | bytes 245792 | tf_op jit(solution)/shard_map/all_to_all | solution.py:541
  70.9 1.3 %collective-permute-start.7 = (bf16[16,384]{1,0:T(8,128)(2,1)S(1)}, bf16[16,384]{1,0:T(8,128)(2,1)S(1)}, u32[]{:S(2)}, u32[]{:S(2)}) collective-permute-start(bf16[16,384]{1,0:T(8,128)(2,1)S(1)} %corner.1), channel_id=1, source_target_pairs={{1,0},{2,1},{3,2},{5,4},{6,5},{7,6},{9,8},{10,9},{11,10},{13,12},{... | collective-permute-start | bytes 36872 | tf_op jit(solution)/shard_map/ppermute | solution.py:551
  72.2 3.0 %collective-permute-start.6 = (bf16[16,384]{1,0:T(8,128)(2,1)S(1)}, bf16[16,384]{1,0:T(8,128)(2,1)S(1)}, u32[]{:S(2)}, u32[]{:S(2)}) collective-permute-start(bf16[16,384]{1,0:T(8,128)(2,1)S(1)} %corner.1), channel_id=1, source_target_pairs={{0,1},{1,2},{2,3},{4,5},{5,6},{6,7},{8,9},{9,10},{10,11},{12,13},{... | collective-permute-start | bytes 36872 | tf_op jit(solution)/shard_map/ppermute | solution.py:550
  75.2 0.0 collective-permute-done.4.from_above_ref
  75.2 1.4 %collective-permute-done.5.from_below_ref = bf16[288,512]{1,0:T(8,128)(2,1)S(1)} collective-permute-done((bf16[288,512]{1,0:T(8,128)(2,1)S(1)}, bf16[288,512]{1,0:T(8,128)(2,1)S(1)}, u32[]{:S(2)}, u32[]{:S(2)}) %collective-permute-start.5) | collective-permute-done | bytes 294944 | tf_op jit(solution)/shard_map/ppermute | solution.py:539
  76.6 0.0 collective-permute-done.7.from_east_ref
  76.6 0.0 collective-permute-done.6.from_west_ref
  76.6 5.2 %scatter.1 = (f32[2192,512]{1,0:T(8,128)}, f32[1,192,128]{2,1,0:T(8,128)}) custom-call(s32[1,384]{1,0:T(1,128)S(1)} %copy-done.12, bf16[3,512,384]{2,1,0:T(8,128)(2,1)S(1)} %get-tuple-element.21.columns_ref, bf16[288,384]{1,0:T(8,128)(2,1)S(1)} %get-tuple-element.27.grad_ref, bf16[288,512]{1,0:T(8,128)(2,1)S(1)} %collective-permute-done.4.from_above_ref, ...), custom_call_target="tpu_custom_call" | custom-call | tf_op jit(solution)/shard_map/scatter/pallas_call | solution.py:553
  (1 shorter events, 0.0 us)
Async XLA Ops:
  0.6 22.1 %copy-start.12 = (s32[1,384]{1,0:T(1,128)S(1)}, s32[1,384]{1,0:T(1,128)}, u32[]{:S(2)}) copy-start(s32[1,384]{1,0:T(1,128)} %cells_ref.5) | copy-start | bytes 4612
  0.6 1.6 %copy-start = (bf16[2,137,8,512]{3,2,1,0:T(8,128)(2,1)S(1)}, bf16[2,137,8,512]{3,2,1,0:T(8,128)(2,1)}, u32[]{:S(2)}) copy-start(bf16[2,137,8,512]{3,2,1,0:T(8,128)(2,1)} %param.7) | copy-start | bytes 6733828
  2.3 7.5 %copy-start.10 = (f32[1,192,128]{2,1,0:T(8,128)S(1)}, f32[1,192,128]{2,1,0:T(8,128)}, u32[]{:S(2)}) copy-start(f32[1,192,128]{2,1,0:T(8,128)} %cot_ref.1) | copy-start | bytes 294916
  2.3 20.5 %copy-start.1 = (bf16[16,128,137]{1,0,2:T(8,128)(2,1)S(1)}, bf16[16,128,137]{1,0,2:T(8,128)(2,1)}, u32[]{:S(2)}) copy-start(bf16[16,128,137]{1,0,2:T(8,128)(2,1)} %param.12) | copy-start | bytes 1683460
  2.3 20.5 %copy-start.11 = (f32[9,1,384]{2,1,0:T(1,128)S(1)}, f32[9,1,384]{2,1,0:T(1,128)}, u32[]{:S(2)}) copy-start(f32[9,1,384]{2,1,0:T(1,128)} %weight_ref.3) | copy-start | bytes 41476
  4.5 28.3 %copy-start.13 = (s32[1,24]{1,0:T(1,128)S(1)}, s32[1,24]{1,0:T(1,128)}, u32[]{:S(2)}) copy-start(s32[1,24]{1,0:T(1,128)} %instr_ref.1) | copy-start | bytes 292
  4.5 28.3 %copy-start.14 = (s32[1,24]{1,0:T(1,128)S(1)}, s32[1,24]{1,0:T(1,128)}, u32[]{:S(2)}) copy-start(s32[1,24]{1,0:T(1,128)} %dest_ref.1) | copy-start | bytes 292
  4.5 4.5 %collective-permute-start.3 = (bf16[16,384]{1,0:T(8,128)(2,1)S(1)}, bf16[16,384]{1,0:T(8,128)(2,1)S(1)}, u32[]{:S(2)}, u32[]{:S(2)}) collective-permute-start(bf16[16,384]{1,0:T(8,128)(2,1)S(1)} %get-tuple-element.24), channel_id=1, source_target_pairs={{1,0},{2,1},{3,2},{5,4},{6,5},{7,6},{9,8},{10,9},{11,10},{13,12},{... | collective-permute-start | bytes 36872 | tf_op jit(solution)/shard_map/ppermute | solution.py:478
  6.0 3.9 %collective-permute-start.2 = (bf16[16,384]{1,0:T(8,128)(2,1)S(1)}, bf16[16,384]{1,0:T(8,128)(2,1)S(1)}, u32[]{:S(2)}, u32[]{:S(2)}) collective-permute-start(bf16[16,384]{1,0:T(8,128)(2,1)S(1)} %get-tuple-element.24), channel_id=1, source_target_pairs={{0,1},{1,2},{2,3},{4,5},{5,6},{6,7},{8,9},{9,10},{10,11},{12,13},{... | collective-permute-start | bytes 36872 | tf_op jit(solution)/shard_map/ppermute | solution.py:477
  10.6 22.2 %all-to-all-start = ((bf16[4,240,128]{2,1,0:T(8,128)(2,1)}), bf16[4,240,128]{2,1,0:T(8,128)(2,1)}, u32[]{:S(2)}, u32[]{:S(2)}) async-start(bf16[4,240,128]{2,1,0:T(8,128)(2,1)} %get-tuple-element.26), calls=%async_computation | async-start | bytes 491520 | tf_op jit(solution)/shard_map/all_to_all | solution.py:490
  16.9 14.5 %collective-permute-start.1 = (bf16[288,512]{1,0:T(8,128)(2,1)}, bf16[288,512]{1,0:T(8,128)(2,1)S(1)}, u32[]{:S(2)}, u32[]{:S(2)}) collective-permute-start(bf16[288,512]{1,0:T(8,128)(2,1)} %get-tuple-element.19.top_ref), channel_id=1, source_target_pairs={{4,0},{8,4},{12,8},{5,1},{9,5},{13,9},{6,2},{10,6},{14,10},{7,3},{... | collective-permute-start | bytes 884744 | tf_op jit(solution)/shard_map/ppermute | solution.py:480
  18.2 13.9 %collective-permute-start = (bf16[288,512]{1,0:T(8,128)(2,1)}, bf16[288,512]{1,0:T(8,128)(2,1)S(1)}, u32[]{:S(2)}, u32[]{:S(2)}) collective-permute-start(bf16[288,512]{1,0:T(8,128)(2,1)} %get-tuple-element.20.bottom_ref), channel_id=1, source_target_pairs={{0,4},{4,8},{8,12},{1,5},{5,9},{9,13},{2,6},{6,10},{10,14},{3,7},{... | collective-permute-start | bytes 884744 | tf_op jit(solution)/shard_map/ppermute | solution.py:479
  25.9 1.0 %copy-start.2 = (f32[18,128,128]{2,1,0:T(8,128)}, f32[18,128,128]{2,1,0:T(8,128)S(1)}, u32[]{:S(2)}) copy-start(f32[18,128,128]{2,1,0:T(8,128)S(1)} %get-tuple-element.23.turned_ref) | copy-start | bytes 3538948
  26.9 0.8 copy-start.4
  31.3 0.7 copy-start.6
  32.1 0.7 copy-start.8
  32.8 1.3 %copy-start.3 = (f32[18,128,128]{2,1,0:T(8,128)S(1)}, f32[18,128,128]{2,1,0:T(8,128)}, u32[]{:S(2)}) copy-start(f32[18,128,128]{2,1,0:T(8,128)} %copy-done.2) | copy-start | bytes 3538948
  34.1 1.0 %copy-start.5 = (f32[288,384]{1,0:T(8,128)S(1)}, f32[288,384]{1,0:T(8,128)}, u32[]{:S(2)}) copy-start(f32[288,384]{1,0:T(8,128)} %copy-done.4) | copy-start | bytes 1327108
  35.1 1.0 %copy-start.7 = (bf16[288,512]{1,0:T(8,128)(2,1)S(1)}, bf16[288,512]{1,0:T(8,128)(2,1)}, u32[]{:S(2)}) copy-start(bf16[288,512]{1,0:T(8,128)(2,1)} %copy-done.6) | copy-start | bytes 884740
  36.1 1.0 %copy-start.9 = (bf16[288,512]{1,0:T(8,128)(2,1)S(1)}, bf16[288,512]{1,0:T(8,128)(2,1)}, u32[]{:S(2)}) copy-start(bf16[288,512]{1,0:T(8,128)(2,1)} %copy-done.8) | copy-start | bytes 884740
  58.2 12.6 %all-to-all-start.1 = ((bf16[4,240,128]{2,1,0:T(8,128)(2,1)}), bf16[4,240,128]{2,1,0:T(8,128)(2,1)S(1)}, u32[]{:S(2)}, u32[]{:S(2)}) async-start(bf16[4,240,128]{2,1,0:T(8,128)(2,1)} %get-tuple-element.31), calls=%async_computation.1 | async-start | bytes 491520 | tf_op jit(solution)/shard_map/all_to_all | solution.py:541
  61.9 13.3 %collective-permute-start.4 = (bf16[288,512]{1,0:T(8,128)(2,1)S(1)}, bf16[288,512]{1,0:T(8,128)(2,1)S(1)}, u32[]{:S(2)}, u32[]{:S(2)}) collective-permute-start(bf16[288,512]{1,0:T(8,128)(2,1)S(1)} %get-tuple-element.28), channel_id=1, source_target_pairs={{0,4},{4,8},{8,12},{1,5},{5,9},{9,13},{2,6},{6,10},{10,14},{3,7},{... | collective-permute-start | bytes 884744 | tf_op jit(solution)/shard_map/ppermute | solution.py:540
  65.8 10.8 %collective-permute-start.5 = (bf16[288,512]{1,0:T(8,128)(2,1)S(1)}, bf16[288,512]{1,0:T(8,128)(2,1)S(1)}, u32[]{:S(2)}, u32[]{:S(2)}) collective-permute-start(bf16[288,512]{1,0:T(8,128)(2,1)S(1)} %get-tuple-element.29), channel_id=1, source_target_pairs={{4,0},{8,4},{12,8},{5,1},{9,5},{13,9},{6,2},{10,6},{14,10},{7,3},{... | collective-permute-start | bytes 884744 | tf_op jit(solution)/shard_map/ppermute | solution.py:539
  70.9 5.7 %collective-permute-start.7 = (bf16[16,384]{1,0:T(8,128)(2,1)S(1)}, bf16[16,384]{1,0:T(8,128)(2,1)S(1)}, u32[]{:S(2)}, u32[]{:S(2)}) collective-permute-start(bf16[16,384]{1,0:T(8,128)(2,1)S(1)} %corner.1), channel_id=1, source_target_pairs={{1,0},{2,1},{3,2},{5,4},{6,5},{7,6},{9,8},{10,9},{11,10},{13,12},{... | collective-permute-start | bytes 36872 | tf_op jit(solution)/shard_map/ppermute | solution.py:551
  72.2 4.4 %collective-permute-start.6 = (bf16[16,384]{1,0:T(8,128)(2,1)S(1)}, bf16[16,384]{1,0:T(8,128)(2,1)S(1)}, u32[]{:S(2)}, u32[]{:S(2)}) collective-permute-start(bf16[16,384]{1,0:T(8,128)(2,1)S(1)} %corner.1), channel_id=1, source_target_pairs={{0,1},{1,2},{2,3},{4,5},{5,6},{6,7},{8,9},{9,10},{10,11},{12,13},{... | collective-permute-start | bytes 36872 | tf_op jit(solution)/shard_map/ppermute | solution.py:550

commit v2 on v1

--- a/solution.py
+++ b/solution.py
@@ -12,9 +12,11 @@
 LOG2E = 1.4426950408889634
 LANES = 128
 EDGE = 16
-BLOCKS = 3
+BLOCKS = 2
 VMEM = pl.BlockSpec(memory_space=pltpu.VMEM)
 SMEM = pl.BlockSpec(memory_space=pltpu.SMEM)
+HBM = pl.BlockSpec(memory_space=pl.ANY)
+SMALL = pl.CostEstimate(flops=1000, bytes_accessed=1000, transcendentals=0)
 NN = (((1,), (0,)), ((), ()))
 NT = (((1,), (1,)), ((), ()))
 TN = (((0,), (0,)), ((), ()))
@@ -28,7 +30,7 @@
     return -(-value // unit) * unit
 
 
-def params(mib=48):
+def params(mib):
     return pltpu.CompilerParams(vmem_limit_bytes=mib * 1024 * 1024)
 
 
@@ -65,11 +67,11 @@
     lax.fori_loop(0, width // step, chunk, 0)
 
 
-def row_stencil(columns_ref, row_of, r):
+def row_stencil(columns_ref, row_of, r, part=slice(None)):
     total = None
     for a in range(3):
         keep = jnp.where(row_of == r - a + 1, 1.0, 0.0).astype(BF16)
-        term = columns_ref[a] * keep
+        term = columns_ref[a, part, :] * keep
         total = term if total is None else total + term
     return total
 
@@ -85,8 +87,8 @@
     west = k >= rows
     col_at = jnp.where(west, -1, width)
     row_at = jnp.where(west, k - rows, k)
-    row_at = jnp.where(block == 1, jnp.where(row_at == rows - 1, -1, none), row_at)
-    row_at = jnp.where(block == 2, jnp.where(row_at == 0, rows, none), row_at)
+    corner = jnp.where(row_at == rows - 1, -1, jnp.where(row_at == 0, rows, none))
+    row_at = jnp.where(block == 1, corner, row_at)
     total = jnp.zeros((lines, obs), F32)
     for a in range(3):
         for b in range(3):
@@ -95,7 +97,37 @@
     return total.astype(BF16)
 
 
-def pack_kernel(dims, profiles_ref, mid_ref, top_ref, bottom_ref, edge_ref, wide_ref):
+def pairs(count, offset, ring):
+    swap = [(i, i + 1) for i in range(offset, count - 1, 2)]
+    if ring and offset and count % 2 == 0 and count > 2:
+        swap.append((0, count - 1))
+    return sorted(swap + [(b, a) for a, b in swap])
+
+
+def pair_place(axis):
+    at = lax.axis_index(axis)
+    return (at & 1) == 0, at
+
+
+def pair_rows(rows, count):
+    even, at = pair_place("lat")
+    below = jnp.where(at < count - 1, rows, -99)
+    above = jnp.where(at > 0, -1, -99)
+    return jnp.where(even, below, above), jnp.where(even, above, below)
+
+
+def choose(pred, a, b):
+    return jnp.where(pred, a.astype(F32), b.astype(F32))
+
+
+def from_sides(first, second, count):
+    even, at = pair_place("lon")
+    west = choose(even, second, first) * jnp.where(at > 0, 1.0, 0.0)
+    east = choose(even, first, second) * jnp.where(at < count - 1, 1.0, 0.0)
+    return west, east
+
+
+def pack_kernel(dims, profiles_ref, cot_ref, rows_ref, first_ref, second_ref, edge_ref, send_ref, wide_ref):
     levels, rows, width, pad = dims
     for lane in range(0, width, LANES):
         part = profiles_ref[:, :, lane : lane + LANES]
@@ -104,7 +136,7 @@
     k = iota((EDGE, LANES), 0)
     at_lane = iota((EDGE, LANES), 1)
     for r in range(rows):
-        out = top_ref if r == 0 else bottom_ref if r == rows - 1 else mid_ref.at[r - 1]
+        out = rows_ref.at[r]
         for v in range(2):
             for lane in range(0, width, LANES):
                 value = wide_ref[lane // LANES, pl.ds(v * levels * rows + r, levels, stride=rows), :]
@@ -115,19 +147,16 @@
         edges = edges + dot(west, out[:, :LANES], NT) + dot(east, out[:, width - LANES :], NT)
     edge_ref[...] = jnp.zeros(edge_ref.shape, BF16)
     edge_ref[:, : 2 * pad] = edges.astype(BF16)
-
-
-def blend_kernel(rows, cot_ref, from_west_ref, from_east_ref, send_ref, edge_ref):
+    even, _ = pair_place("lat")
+    first_ref[...] = rows_ref[jnp.where(even, rows - 1, 0)]
+    second_ref[...] = rows_ref[jnp.where(even, 0, rows - 1)]
     proc = cot_ref.shape[1]
-    west = iota(edge_ref.shape, 0) >= rows
-    edge = jnp.where(west, from_west_ref[...].astype(F32), from_east_ref[...].astype(F32)).astype(BF16)
-    edge_ref[...] = edge
     cot = cot_ref[0].astype(BF16)
 
     def share(s, carry):
         send_ref[s, 0:proc, :] = cot
-        for t in range(edge.shape[1] // LANES):
-            send_ref[s, proc + EDGE * t : proc + EDGE * (t + 1), :] = edge[:, t * LANES : (t + 1) * LANES]
+        for t in range(edge_ref.shape[1] // LANES):
+            send_ref[s, proc + EDGE * t : proc + EDGE * (t + 1), :] = edge_ref[:, t * LANES : (t + 1) * LANES]
         return carry
 
     lax.fori_loop(0, send_ref.shape[0], share, 0)
@@ -142,26 +171,35 @@
     return [part.astype(F32) * keep for part in parts]
 
 
-def gather_rows(rows, row, columns_ref, mid_ref, top_ref, bottom_ref, field_ref):
+def blend_kernel(rows, proc, edge_ref, lat_ref, out_ref):
+    k = iota((EDGE, LANES), 0)
+    last = (k == rows - 1) | (k == 2 * rows - 1)
+    first = (k == 0) | (k == rows)
+    ups, downs = lat_block(lat_ref, proc, -1), lat_block(lat_ref, proc, 1)
+    out_ref[0:EDGE, :] = edge_ref[...]
+    for t in range(edge_ref.shape[1] // LANES):
+        corner = jnp.where(last, ups[t], jnp.where(first, downs[t], 0.0))
+        out_ref[EDGE : 2 * EDGE, t * LANES : (t + 1) * LANES] = corner.astype(BF16)
+
+
+def gather_rows(rows, row, columns_ref, rows_ref, field_ref):
     for r in range(rows):
-        source = top_ref if r == 0 else bottom_ref if r == rows - 1 else mid_ref.at[r - 1]
-        value = dot(source[...], row_stencil(columns_ref, row, r))
+        value = dot(rows_ref[r], row_stencil(columns_ref, row, r))
         if r == 0:
             field_ref[...] = value
         else:
             field_ref[...] += value
 
 
-def gather_halo(rows, row, columns_ref, above_ref, below_ref, field_ref):
-    field_ref[...] += dot(above_ref[...], row_stencil(columns_ref, row, -1))
-    field_ref[...] += dot(below_ref[...], row_stencil(columns_ref, row, rows))
-
-
-def gather_edges(pad, proc, edge_ref, lat_ref, halo_ref, edge_w, field_ref):
-    halo_ref[0:EDGE, :] = edge_ref[...].astype(F32)
-    for n, side in enumerate((-1, 1)):
-        for t, part in enumerate(lat_block(lat_ref, proc, side)):
-            halo_ref[(n + 1) * EDGE : (n + 2) * EDGE, t * LANES : (t + 1) * LANES] = part
+def gather_halo(halo_rows, row, columns_ref, first_ref, second_ref, field_ref):
+    field_ref[...] += dot(first_ref[...], row_stencil(columns_ref, row, halo_rows[0]))
+    field_ref[...] += dot(second_ref[...], row_stencil(columns_ref, row, halo_rows[1]))
+
+
+def gather_edges(rows, pad, n_lon, first_ref, second_ref, halo_ref, edge_w, field_ref):
+    west = (iota(halo_ref.shape, 0) & (EDGE - 1)) >= rows
+    from_west, from_east = from_sides(first_ref[...], second_ref[...], n_lon)
+    halo_ref[...] = jnp.where(west, from_west, from_east)
     field_ref[...] += dot(halo_ref[:, : 2 * pad].astype(BF16), edge_w, TN)
 
 
@@ -275,10 +313,11 @@
     held = cot_t_ref[...] * signal_ref[...]
     held_hi = held.astype(BF16)
     held_lo = (held - held_hi.astype(F32)).astype(BF16)
+    halves = jnp.concatenate([held_hi, held_lo], axis=0)
 
     def contract(l0, count):
         rows_in = absorb_ref[pl.ds(l0, count)].reshape(count * instruments, channels)
-        value = dot(rows_in, held_hi) + dot(rows_in, held_lo)
+        value = dot(jnp.concatenate([rows_in, rows_in], axis=1), halves)
         value = value.reshape(count, instruments, obs) * pick[None]
         value = jnp.sum(value.reshape(count, instruments // 8, 8, obs), axis=1)
         at = pl.ds(pl.multiple_of(l0 * 8, 8), count * 8)
@@ -286,13 +325,15 @@
         for lane in range(0, obs, LANES):
             r_part_ref[lane // LANES, at, :] -= value[:, lane : lane + LANES]
 
+    step = 16
+
     def contract_block(b, carry):
-        contract(b * 8, 8)
+        contract(b * step, step)
         return carry
 
-    lax.fori_loop(0, levels // 8, contract_block, 0)
-    if levels % 8:
-        contract(levels // 8 * 8, levels % 8)
+    lax.fori_loop(0, levels // step, contract_block, 0)
+    if levels % step:
+        contract(levels // step * step, levels % step)
 
 
 def gradients(pad, s_part_ref, r_part_ref, cot_t_ref, field_ref, shift_ref, grad_ref):
@@ -312,31 +353,27 @@
         grad_ref[pad : 2 * pad, lanes] = (0.5 * (1.0 - bent * bent) * r_sum).astype(BF16)
 
 
-def scatter_outside(rows, pad, proc, row, columns_ref, edge_w, grad_ref, above_ref, below_ref, edge_ref, send_ref):
+def scatter_outside(
+    rows, pad, proc, halo_rows, row, columns_ref, edge_w, grad_ref, first_ref, second_ref, edge_ref, send_ref
+):
     grad = grad_ref[...]
-    above_ref[...] = dot(grad, row_stencil(columns_ref, row, -1), NT).astype(BF16)
-    below_ref[...] = dot(grad, row_stencil(columns_ref, row, rows), NT).astype(BF16)
+    first_ref[...] = dot(grad, row_stencil(columns_ref, row, halo_rows[0]), NT).astype(BF16)
+    second_ref[...] = dot(grad, row_stencil(columns_ref, row, halo_rows[1]), NT).astype(BF16)
     out = dot(edge_w, grad, NT)
     edge_ref[...] = jnp.zeros(edge_ref.shape, F32)
     edge_ref[:, : 2 * pad] = out
-    for n, side in enumerate((-1, 1)):
+    k = iota((EDGE, LANES), 0)
+    last = (k == rows - 1) | (k == 2 * rows - 1)
+    first = (k == 0) | (k == rows)
+    for side, mine in ((-1, last), (1, first)):
         at = lax.axis_index("lat") + side
 
         @pl.when((at >= 0) & (at < send_ref.shape[0]))
         def _():
             for t in range(edge_ref.shape[1] // LANES):
-                part = edge_ref[(n + 1) * EDGE : (n + 2) * EDGE, t * LANES : (t + 1) * LANES]
-                send_ref[at, proc + EDGE * t : proc + EDGE * (t + 1), :] = part.astype(BF16)
-
-
-def gather_kernel(
-    dims, cells_ref, weight_ref, absorb_ref, mid_ref, top_ref, bottom_ref, field_ref, turned_ref, columns_ref
-):
-    rows, width = dims
-    fill_columns(cells_ref, weight_ref, columns_ref)
-    row, _ = split_cells(cells_ref[...], width)
-    gather_rows(rows, row, columns_ref, mid_ref, top_ref, bottom_ref, field_ref)
-    turn_absorption(absorb_ref, turned_ref)
+                part = edge_ref[EDGE : 2 * EDGE, t * LANES : (t + 1) * LANES]
+                part = jnp.where(mine, part, 0.0).astype(BF16)
+                send_ref[at, proc + EDGE * t : proc + EDGE * (t + 1), :] = part
 
 
 def transfer_kernel(
@@ -346,18 +383,19 @@
     instr_ref,
     dest_ref,
     absorb_ref,
-    field_in_ref,
-    turned_ref,
-    columns_ref,
-    above_ref,
-    below_ref,
-    edge_ref,
-    lat_ref,
+    side_first_ref,
+    side_second_ref,
+    rows_hbm,
+    row_first_hbm,
+    row_second_hbm,
+    lat_hbm,
     grad_ref,
-    grad_above_ref,
-    grad_below_ref,
+    grad_first_ref,
+    grad_second_ref,
     grad_edge_ref,
     send_ref,
+    columns_ref,
+    turned_ref,
     halo_ref,
     field_ref,
     rate_ref,
@@ -368,15 +406,39 @@
     s_part_ref,
     r_part_ref,
     shift_ref,
+    rows_ref,
+    row_first_ref,
+    row_second_ref,
+    lat_ref,
+    sems,
 ):
-    levels, rows, width, pad, batch, proc = dims
+    levels, rows, width, pad, batch, proc, n_lat, n_lon = dims
+    moves = [
+        pltpu.make_async_copy(source, target, sems.at[k])
+        for k, (source, target) in enumerate(
+            (
+                (rows_hbm, rows_ref),
+                (row_first_hbm, row_first_ref),
+                (row_second_hbm, row_second_ref),
+                (lat_hbm, lat_ref),
+            )
+        )
+    ]
+    for move in moves:
+        move.start()
     obs = cells_ref.shape[1]
     instruments = absorb_ref.shape[1]
+    fill_columns(cells_ref, weight_ref, columns_ref)
     row, _ = split_cells(cells_ref[...], width)
+    halo_rows = pair_rows(rows, n_lat)
     edge_w = edge_weights(cells_ref, weight_ref, rows, width)
-    field_ref[...] = field_in_ref[...]
-    gather_halo(rows, row, columns_ref, above_ref, below_ref, field_ref)
-    gather_edges(pad, proc, edge_ref, lat_ref, halo_ref, edge_w, field_ref)
+    turn_absorption(absorb_ref, turned_ref)
+    moves[0].wait()
+    gather_rows(rows, row, columns_ref, rows_ref, field_ref)
+    for move in moves[1:]:
+        move.wait()
+    gather_halo(halo_rows, row, columns_ref, row_first_ref, row_second_ref, field_ref)
+    gather_edges(rows, pad, n_lon, side_first_ref, side_second_ref, halo_ref, edge_w, field_ref)
     departures(batch, proc, dest_ref, lat_ref, cot_rows_ref, cot_t_ref)
     chosen = chosen_instruments(batch, obs, instr_ref)
     prepare_levels(pad, field_ref, step_ref, rate_ref)
@@ -388,7 +450,18 @@
     held_part(levels, pick, absorb_ref, cot_t_ref, signal_ref, r_part_ref)
     gradients(pad, s_part_ref, r_part_ref, cot_t_ref, field_ref, shift_ref, grad_ref)
     scatter_outside(
-        rows, pad, proc, row, columns_ref, edge_w, grad_ref, grad_above_ref, grad_below_ref, halo_ref, send_ref
+        rows,
+        pad,
+        proc,
+        halo_rows,
+        row,
+        columns_ref,
+        edge_w,
+        grad_ref,
+        grad_first_ref,
+        grad_second_ref,
+        halo_ref,
+        send_ref,
     )
     grad_edge_ref[...] = halo_ref[0:EDGE, :].astype(BF16)
 
@@ -403,43 +476,59 @@
 def scatter_kernel(
     dims,
     cells_ref,
-    columns_ref,
+    weight_ref,
     grad_ref,
-    from_above_ref,
-    from_below_ref,
-    from_west_ref,
-    from_east_ref,
+    row_first_ref,
+    row_second_ref,
+    side_first_ref,
+    side_second_ref,
     lat_ref,
     out_ref,
     rad_out_ref,
+    columns_ref,
     halo_ref,
     wide_ref,
+    sems,
 ):
-    levels, rows, width, pad, proc = dims
+    levels, rows, width, pad, proc, n_lat, n_lon = dims
+    fill_columns(cells_ref, weight_ref, columns_ref)
+    even, at_lat = pair_place("lat")
+    inside = jnp.where(at_lat > 0, 1.0, 0.0), jnp.where(at_lat < n_lat - 1, 1.0, 0.0)
     rad_out_ref[...] = jnp.sum(lat_ref[:, 0:proc, :].astype(F32), axis=0)[None]
     row, _ = split_cells(cells_ref[...], width)
     west = iota(halo_ref.shape, 0) < rows
-    halo_ref[...] = jnp.where(west, from_west_ref[...].astype(F32), from_east_ref[...].astype(F32))
+    from_west, from_east = from_sides(side_first_ref[...], side_second_ref[...], n_lon)
+    halo_ref[...] = jnp.where(west, from_west, from_east)
     edges = halo_ref[:, : 2 * pad].T.astype(BF16)
     k = iota((EDGE, LANES), 0)
     at_lane = iota((EDGE, LANES), 1)
-    for r in range(rows):
-        value = dot(grad_ref[...], row_stencil(columns_ref, row, r), NT)
-        if r == 0:
-            value = value + from_above_ref[...].astype(F32)
-        if r == rows - 1:
-            value = value + from_below_ref[...].astype(F32)
-        first_at = jnp.where((k == r) & (at_lane == 0), 1.0, 0.0).astype(BF16)
-        last_at = jnp.where((k == rows + r) & (at_lane == LANES - 1), 1.0, 0.0).astype(BF16)
-        first = value[:, :LANES] + dot(edges, first_at)
-        last = value[:, width - LANES :] + dot(edges, last_at)
-        value = jnp.concatenate([first, value[:, LANES : width - LANES], last], axis=1)
-        for v in range(2):
-            at = pl.ds(v * levels * rows + r, levels, stride=rows)
-            for lane in range(0, width, LANES):
-                wide_ref[lane // LANES, at, :] = value[v * pad : v * pad + levels, lane : lane + LANES]
-    for lane in range(0, width, LANES):
-        out_ref[:, lane : lane + LANES] = wide_ref[lane // LANES]
+    moves = []
+    half = 2 * LANES if width % (2 * LANES) == 0 else LANES
+    for start in range(0, width, half):
+        part = slice(start, start + half)
+        for r in range(rows):
+            value = dot(grad_ref[...], row_stencil(columns_ref, row, r, part), NT)
+            if r == 0:
+                value = value + choose(even, row_second_ref[:, part], row_first_ref[:, part]) * inside[0]
+            if r == rows - 1:
+                value = value + choose(even, row_first_ref[:, part], row_second_ref[:, part]) * inside[1]
+            for lane in range(start, start + half, LANES):
+                piece = value[:, lane - start : lane - start + LANES]
+                if lane == 0:
+                    piece = piece + dot(edges, jnp.where((k == r) & (at_lane == 0), 1.0, 0.0).astype(BF16))
+                if lane + LANES == width:
+                    last_at = jnp.where((k == rows + r) & (at_lane == LANES - 1), 1.0, 0.0).astype(BF16)
+                    piece = piece + dot(edges, last_at)
+                for v in range(2):
+                    at = pl.ds(v * levels * rows + r, levels, stride=rows)
+                    wide_ref[lane // LANES, at, :] = piece[v * pad : v * pad + levels, :]
+        for lane in range(start, start + half, LANES):
+            t = lane // LANES
+            move = pltpu.make_async_copy(wide_ref.at[t], out_ref.at[:, lane : lane + LANES], sems.at[t])
+            move.start()
+            moves.append(move)
+    for move in moves:
+        move.wait()
 
 
 def per_device(profiles, obs_cell, obs_weight, batch_instr, batch_dest, absorption, cotangent):
@@ -454,60 +543,48 @@
     feat = round_up(2 * pad, LANES)
     lat_rows = proc + EDGE * (feat // LANES)
     blocks = -(-levels * instruments // LANES)
-    up = [(i, i + 1) for i in range(n_lat - 1)]
-    down = [(b, a) for a, b in up]
-    east = [(j, j + 1) for j in range(n_lon - 1)]
-    west = [(b, a) for a, b in east]
+    lat_pairs = [pairs(n_lat, offset, False) for offset in (0, 1)]
+    lon_pairs = [pairs(n_lon, offset, True) for offset in (0, 1)]
     shape = jax.ShapeDtypeStruct
     row_shape = shape((2 * pad, width), BF16)
     edge_shape = shape((EDGE, feat), BF16)
     lat_shape = shape((n_lat, lat_rows, channels), BF16)
     absorb = jnp.transpose(absorption, (2, 0, 1))
 
-    mid, top, bottom, edge = pl.pallas_call(
+    row_data, row_first, row_second, edge, lat_send = pl.pallas_call(
         functools.partial(pack_kernel, (levels, rows, width, pad)),
-        out_shape=(shape((rows - 2, 2 * pad, width), BF16), row_shape, row_shape, edge_shape),
-        in_specs=[VMEM],
-        out_specs=(VMEM,) * 4,
+        out_shape=(shape((rows, 2 * pad, width), BF16), row_shape, row_shape, edge_shape, lat_shape),
+        in_specs=[VMEM] * 2,
+        out_specs=(VMEM,) * 5,
         scratch_shapes=[pltpu.VMEM((width // LANES, 2 * levels * rows, LANES), F32)],
-        compiler_params=params(),
+        compiler_params=params(12),
         name="pack",
-    )(profiles.reshape(2 * levels, rows, width))
-
-    from_west = lax.ppermute(edge, "lon", east)
-    from_east = lax.ppermute(edge, "lon", west)
-    above = lax.ppermute(bottom, "lat", up)
-    below = lax.ppermute(top, "lat", down)
-
-    lat_send, side = pl.pallas_call(
-        functools.partial(blend_kernel, rows),
-        out_shape=(lat_shape, edge_shape),
-        in_specs=[VMEM] * 3,
-        out_specs=(VMEM,) * 2,
-        compiler_params=params(),
+    )(profiles.reshape(2 * levels, rows, width), cotangent)
+
+    lat_in = lax.all_to_all(lat_send, "lat", 0, 0, tiled=True)
+    row_first = lax.ppermute(row_first, "lat", lat_pairs[0])
+    row_second = lax.ppermute(row_second, "lat", lat_pairs[1])
+
+    side = pl.pallas_call(
+        functools.partial(blend_kernel, rows, proc),
+        out_shape=shape((BLOCKS * EDGE, feat), BF16),
+        in_specs=[VMEM] * 2,
+        out_specs=VMEM,
+        compiler_params=params(4),
+        cost_estimate=SMALL,
         name="blend",
-    )(cotangent, from_west, from_east)
-    lat_in = lax.all_to_all(lat_send, "lat", 0, 0, tiled=True)
-
-    field, turned, columns = pl.pallas_call(
-        functools.partial(gather_kernel, (rows, width)),
-        out_shape=(
-            shape((2 * pad, obs), F32),
-            shape((blocks, channels, LANES), F32),
-            shape((3, width, obs), BF16),
-        ),
-        in_specs=[VMEM] * 6,
-        out_specs=(VMEM,) * 3,
-        compiler_params=params(),
-        name="gather",
-    )(obs_cell, obs_weight, absorb, mid, top, bottom)
-
-    grad, grad_above, grad_below, grad_edge, lat_back = pl.pallas_call(
-        functools.partial(transfer_kernel, (levels, rows, width, pad, batch, proc)),
+    )(edge, lat_in)
+    side_first = lax.ppermute(side, "lon", lon_pairs[0])
+    side_second = lax.ppermute(side, "lon", lon_pairs[1])
+
+    grad, grad_first, grad_second, grad_edge, lat_back = pl.pallas_call(
+        functools.partial(transfer_kernel, (levels, rows, width, pad, batch, proc, n_lat, n_lon)),
         out_shape=(shape((2 * pad, obs), BF16), row_shape, row_shape, edge_shape, lat_shape),
-        in_specs=[VMEM, VMEM, SMEM, SMEM] + [VMEM] * 8,
+        in_specs=[VMEM, VMEM, SMEM, SMEM] + [VMEM] * 3 + [HBM] * 4,
         out_specs=(VMEM,) * 5,
         scratch_shapes=[
+            pltpu.VMEM((3, width, obs), BF16),
+            pltpu.VMEM((blocks, channels, LANES), F32),
             pltpu.VMEM((BLOCKS * EDGE, feat), F32),
             pltpu.VMEM((2 * pad, obs), F32),
             pltpu.VMEM((pad, obs), F32),
@@ -518,8 +595,13 @@
             pltpu.VMEM((obs // LANES, pad * 8, LANES), F32),
             pltpu.VMEM((obs // LANES, pad * 8, LANES), F32),
             pltpu.VMEM((pad + 8, obs), F32),
+            pltpu.VMEM((rows, 2 * pad, width), BF16),
+            pltpu.VMEM(row_shape.shape, BF16),
+            pltpu.VMEM(row_shape.shape, BF16),
+            pltpu.VMEM(lat_shape.shape, BF16),
+            pltpu.SemaphoreType.DMA((4,)),
         ],
-        compiler_params=params(),
+        compiler_params=params(56),
         name="transfer",
     )(
         obs_cell,
@@ -527,44 +609,46 @@
         batch_instr,
         batch_dest,
         absorb,
-        field,
-        turned,
-        columns,
-        above,
-        below,
-        side,
+        side_first,
+        side_second,
+        row_data,
+        row_first,
+        row_second,
         lat_in,
     )
 
-    from_below = lax.ppermute(grad_above, "lat", down)
-    from_above = lax.ppermute(grad_below, "lat", up)
+    grad_first = lax.ppermute(grad_first, "lat", lat_pairs[0])
+    grad_second = lax.ppermute(grad_second, "lat", lat_pairs[1])
     lat_got = lax.all_to_all(lat_back, "lat", 0, 0, tiled=True)
     grad_side = pl.pallas_call(
         functools.partial(corner_kernel, proc),
         out_shape=edge_shape,
         in_specs=[VMEM] * 2,
         out_specs=VMEM,
-        compiler_params=params(),
+        compiler_params=params(4),
+        cost_estimate=SMALL,
         name="corner",
     )(grad_edge, lat_got)
-    grad_from_west = lax.ppermute(grad_side, "lon", east)
-    grad_from_east = lax.ppermute(grad_side, "lon", west)
+    grad_side_first = lax.ppermute(grad_side, "lon", lon_pairs[0])
+    grad_side_second = lax.ppermute(grad_side, "lon", lon_pairs[1])
 
     gradient, radiance = pl.pallas_call(
-        functools.partial(scatter_kernel, (levels, rows, width, pad, proc)),
+        functools.partial(scatter_kernel, (levels, rows, width, pad, proc, n_lat, n_lon)),
         out_shape=(
             shape((2 * levels * rows, width), F32),
             shape((1, proc, channels), F32),
         ),
         in_specs=[VMEM] * 8,
-        out_specs=(VMEM,) * 2,
+        out_specs=(HBM, VMEM),
         scratch_shapes=[
+            pltpu.VMEM((3, width, obs), BF16),
             pltpu.VMEM((EDGE, feat), F32),
             pltpu.VMEM((width // LANES, 2 * levels * rows, LANES), F32),
+            pltpu.SemaphoreType.DMA((width // LANES,)),
         ],
-        compiler_params=params(),
+        compiler_params=params(20),
         name="scatter",
-    )(obs_cell, columns, grad, from_above, from_below, grad_from_west, grad_from_east, lat_got)
+    )(obs_cell, obs_weight, grad, grad_first, grad_second, grad_side_first, grad_side_second, lat_got)
     return radiance, gradient.reshape(2, levels, rows, width)
 
 

time: 82.4 us -> 73.9 us (0.90)
  starting transfers between devices: 29.8 us -> 17.5 us
  waiting for transfers between devices: 9.58 us -> 18.6 us
  local copies, waits for them, and re-layouts: 9.07 us -> 6.18 us
  Pallas kernels: 32.5 us -> 30.5 us
    ppermute x8, starting transfers between devices: 19.8 us -> 7.45 us  [the longest x1 2.19 us: per_device(): grad_first = lax.ppermute(grad_first, 'lat', lat_pairs[0])]
    all_to_all x1, waiting for transfers between devices: 0.01 us -> 6.85 us  [per_device(): lat_in = lax.all_to_all(lat_send, 'lat', 0, 0, tiled=True)]
    pallas_call x2 -> x1, Pallas kernels: 3.86 us -> 0.01 us  [per_device(): pl.pallas_call(functools.partial(blend_kernel, rows, proc), out_shape=sha...]
    all_to_all x1, waiting for transfers between devices: 3.73 us -> 6.93 us  [per_device(): lat_got = lax.all_to_all(lat_back, 'lat', 0, 0, tiled=True)]
    unnamed x30 -> x24, local copies, waits for them, and re-layouts: 9.07 us -> 6.18 us
    pallas_call x1, Pallas kernels: 21.2 us -> 23.1 us  [per_device(): pl.pallas_call(functools.partial(transfer_kernel, (levels, rows, width, p...]
    ppermute x8, waiting for transfers between devices: 5.84 us -> 4.79 us  [the longest x1 2.05 us: per_device(): grad_first = lax.ppermute(grad_first, 'lat', lat_pairs[0])]
  transfers between devices with their start and end apart: 10 -> 10, of which waited for: 4 -> 6; matrix products, arithmetic and copies ran while one was open for 0% -> 0% of each run, Pallas kernels for 4% -> 0%
where the time goes in v2:
time: 73.9 us; the launch traced here: 73.5 us
  Pallas kernels  30.5 us (41%)
  waiting for transfers between devices  18.6 us (25%)
  starting transfers between devices  17.5 us (24%)
  local copies, waits for them, and re-layouts  6.18 us (8%)
    pallas_call x1, Pallas kernels, per_device(): pl.pallas_call(functools.partial(transfer_kernel, (levels, rows, width, p...  23.1 us
    all_to_all x1, waiting for transfers between devices, per_device(): lat_got = lax.all_to_all(lat_back, 'lat', 0, 0, tiled=True)  6.93 us
    all_to_all x1, waiting for transfers between devices, per_device(): lat_in = lax.all_to_all(lat_send, 'lat', 0, 0, tiled=True)  6.85 us
    all_to_all x1, starting transfers between devices, per_device(): lat_in = lax.all_to_all(lat_send, 'lat', 0, 0, tiled=True)  6.32 us
    unnamed x24, local copies, waits for them, and re-layouts  6.18 us
    pallas_call x1, Pallas kernels, per_device(): pl.pallas_call(functools.partial(scatter_kernel, (levels, rows, width, pa...  5.12 us
    all_to_all x1, starting transfers between devices, per_device(): lat_got = lax.all_to_all(lat_back, 'lat', 0, 0, tiled=True)  3.68 us
    pallas_call x1, Pallas kernels, per_device(): pl.pallas_call(functools.partial(pack_kernel, (levels, rows, width, pad))...  2.29 us
  transfers between devices with their start and end apart: 10, of which 6 were waited for; matrix products, arithmetic and copies ran while one was open for 0% of the time, Pallas kernels for 0%

profile of v2, /device:TPU:0, one launch (start us, length us, event | category | flops | bytes accessed | tf_op | source)
XLA Modules:
  0.0 73.5 jit_solution(7035733915839334863)
XLA Ops:
  0.6 0.0 copy-start.1
  0.6 1.6 %copy-done.1 = bf16[2,137,8,512]{3,2,1,0:T(8,128)(2,1)S(1)} copy-done((bf16[2,137,8,512]{3,2,1,0:T(8,128)(2,1)S(1)}, bf16[2,137,8,512]{3,2,1,0:T(8,128)(2,1)}, u32[]{:S(2)}) %copy-start.1) | copy-done | bytes 2244632
  2.3 0.0 copy-start.4
  2.3 0.9 %copy-done.4 = f32[1,192,128]{2,1,0:T(8,128)S(1)} copy-done((f32[1,192,128]{2,1,0:T(8,128)S(1)}, f32[1,192,128]{2,1,0:T(8,128)}, u32[]{:S(2)}) %copy-start.4) | copy-done | bytes 98328
  3.2 2.3 %pack.1 = (bf16[8,288,512]{2,1,0:T(8,128)(2,1)S(1)}, bf16[288,512]{1,0:T(8,128)(2,1)S(1)}, bf16[288,512]{1,0:T(8,128)(2,1)S(1)}, bf16[16,384]{1,0:T(8,128)(2,1)S(1)}, bf16[4,240,128]{2,1,0:T(8,128)(2,1)}) custom-call(bf16[274,8,512]{2,1,0:T(8,128)(2,1)S(1)} %bitcast.3, f32[1,192,128]{2,1,0:T(8,128)S(1)} %copy-done.4), custom_call_target="tpu_custom_call" | custom-call | tf_op jit(solution)/shard_map/pack/pallas_call | solution.py:554
  5.4 0.0 copy-start
  5.5 1.4 %copy-done = bf16[8,288,512]{2,1,0:T(8,128)(2,1)} copy-done((bf16[8,288,512]{2,1,0:T(8,128)(2,1)}, bf16[8,288,512]{2,1,0:T(8,128)(2,1)S(1)}, u32[]{:S(2)}) %copy-start) | copy-done | bytes 2359320
  6.9 6.3 %all-to-all-start = ((bf16[4,240,128]{2,1,0:T(8,128)(2,1)}), bf16[4,240,128]{2,1,0:T(8,128)(2,1)S(1)}, u32[]{:S(2)}, u32[]{:S(2)}) async-start(bf16[4,240,128]{2,1,0:T(8,128)(2,1)} %get-tuple-element.15), calls=%async_computation | async-start | bytes 491520 | tf_op jit(solution)/shard_map/all_to_all | solution.py:564
  13.2 2.0 %collective-permute-start.2 = (bf16[288,512]{1,0:T(8,128)(2,1)S(1)}, bf16[288,512]{1,0:T(8,128)(2,1)S(1)}, u32[]{:S(2)}, u32[]{:S(2)}) collective-permute-start(bf16[288,512]{1,0:T(8,128)(2,1)S(1)} %get-tuple-element.17), channel_id=1, source_target_pairs={{0,4},{4,0},{8,12},{12,8},{1,5},{5,1},{9,13},{13,9},{2,6},{6,2},{1... | collective-permute-start | bytes 884744 | tf_op jit(solution)/shard_map/ppermute | solution.py:565
  15.2 0.7 collective-permute-start.3
  15.9 6.9 %all-to-all-done.lat_ref.lat_hbm = bf16[4,240,128]{2,1,0:T(8,128)(2,1)S(1)} async-done(((bf16[4,240,128]{2,1,0:T(8,128)(2,1)}), bf16[4,240,128]{2,1,0:T(8,128)(2,1)S(1)}, u32[]{:S(2)}, u32[]{:S(2)}) %all-to-all-start) | async-done | bytes 245792 | tf_op jit(solution)/shard_map/all_to_all | solution.py:564
  22.7 0.0 copy-start.2
  22.7 0.0 copy-start.5
  22.8 0.0 copy-start.7
  22.8 0.1 collective-permute-start.1
  22.8 1.6 %collective-permute-start = (bf16[32,384]{1,0:T(8,128)(2,1)S(1)}, bf16[32,384]{1,0:T(8,128)(2,1)S(1)}, u32[]{:S(2)}, u32[]{:S(2)}) collective-permute-start(bf16[32,384]{1,0:T(8,128)(2,1)S(1)} %blend.1), channel_id=1, source_target_pairs={{0,1},{1,0},{2,3},{3,2},{4,5},{5,4},{6,7},{7,6},{8,9},{9,8},{10,11... | collective-permute-start | bytes 73736 | tf_op jit(solution)/shard_map/ppermute | solution.py:577
  24.4 1.4 %collective-permute-done.2.row_first_hbm = bf16[288,512]{1,0:T(8,128)(2,1)S(1)} collective-permute-done((bf16[288,512]{1,0:T(8,128)(2,1)S(1)}, bf16[288,512]{1,0:T(8,128)(2,1)S(1)}, u32[]{:S(2)}, u32[]{:S(2)}) %collective-permute-start.2) | collective-permute-done | bytes 294944 | tf_op jit(solution)/shard_map/ppermute | solution.py:565
  25.8 0.0 copy-start.8
  25.8 0.0 collective-permute-done.3.row_second_hbm
  25.8 0.0 copy-start.9
  25.8 0.5 collective-permute-done.1.side_second_ref
  26.3 0.0 copy-start.10
  26.3 0.0 collective-permute-done.side_first_ref
  26.3 0.0 copy-start.11
  26.3 0.0 copy-done.2
  26.3 0.2 copy-done.8
  26.5 0.1 copy-done.9
  26.7 0.3 copy-done.10
  26.9 0.0 copy-done.11
  26.9 23.1 %transfer.1 = (bf16[288,384]{1,0:T(8,128)(2,1)}, bf16[288,512]{1,0:T(8,128)(2,1)}, bf16[288,512]{1,0:T(8,128)(2,1)}, bf16[16,384]{1,0:T(8,128)(2,1)}, bf16[4,240,128]{2,1,0:T(8,128)(2,1)}) custom-call(s32[1,384]{1,0:T(1,128)} %cells_ref.3, f32[9,1,384]{2,1,0:T(1,128)} %weight_ref.3, s32[1,24]{1,0:T(1,128)} %instr_ref.1, s32[1,24]{1,0:T(1,128)} %dest_ref.1, ...), custom_call_target="tpu_custom_call" | custom-call | tf_op jit(solution)/shard_map/transfer/pallas_call | solution.py:580
  50.0 3.7 %all-to-all-start.1 = ((bf16[4,240,128]{2,1,0:T(8,128)(2,1)}), bf16[4,240,128]{2,1,0:T(8,128)(2,1)S(1)}, u32[]{:S(2)}, u32[]{:S(2)}) async-start(bf16[4,240,128]{2,1,0:T(8,128)(2,1)} %get-tuple-element.23), calls=%async_computation.1 | async-start | bytes 491520 | tf_op jit(solution)/shard_map/all_to_all | solution.py:622
  53.7 2.2 %collective-permute-start.4 = (bf16[288,512]{1,0:T(8,128)(2,1)}, bf16[288,512]{1,0:T(8,128)(2,1)S(1)}, u32[]{:S(2)}, u32[]{:S(2)}) collective-permute-start(bf16[288,512]{1,0:T(8,128)(2,1)} %get-tuple-element.20), channel_id=1, source_target_pairs={{0,4},{4,0},{8,12},{12,8},{1,5},{5,1},{9,13},{13,9},{2,6},{6,2},{1... | collective-permute-start | bytes 884744 | tf_op jit(solution)/shard_map/ppermute | solution.py:620
  55.9 0.7 collective-permute-start.5
  56.5 6.9 %all-to-all-done.1.lat_ref = bf16[4,240,128]{2,1,0:T(8,128)(2,1)S(1)} async-done(((bf16[4,240,128]{2,1,0:T(8,128)(2,1)}), bf16[4,240,128]{2,1,0:T(8,128)(2,1)S(1)}, u32[]{:S(2)}, u32[]{:S(2)}) %all-to-all-start.1) | async-done | bytes 245792 | tf_op jit(solution)/shard_map/all_to_all | solution.py:622
  63.5 0.0 copy-start.6
  63.5 0.7 copy-done.6
  64.2 0.1 collective-permute-start.7
  64.3 0.2 collective-permute-start.6
  64.5 2.1 %collective-permute-done.4.row_first_ref = bf16[288,512]{1,0:T(8,128)(2,1)S(1)} collective-permute-done((bf16[288,512]{1,0:T(8,128)(2,1)}, bf16[288,512]{1,0:T(8,128)(2,1)S(1)}, u32[]{:S(2)}, u32[]{:S(2)}) %collective-permute-start.4) | collective-permute-done | bytes 294944 | tf_op jit(solution)/shard_map/ppermute | solution.py:620
  66.5 0.0 collective-permute-done.5.row_second_ref
  66.5 0.9 %collective-permute-done.7.side_second_ref = bf16[16,384]{1,0:T(8,128)(2,1)S(1)} collective-permute-done((bf16[16,384]{1,0:T(8,128)(2,1)S(1)}, bf16[16,384]{1,0:T(8,128)(2,1)S(1)}, u32[]{:S(2)}, u32[]{:S(2)}) %collective-permute-start.7) | collective-permute-done | bytes 12320 | tf_op jit(solution)/shard_map/ppermute | solution.py:633
  67.4 0.0 collective-permute-done.6.side_first_ref
  67.4 0.0 copy-done.5
  67.4 0.0 copy-done.7
  67.4 0.0 copy-start.3
  67.4 0.9 %copy-done.3 = bf16[288,384]{1,0:T(8,128)(2,1)S(1)} copy-done((bf16[288,384]{1,0:T(8,128)(2,1)S(1)}, bf16[288,384]{1,0:T(8,128)(2,1)}, u32[]{:S(2)}) %copy-start.3) | copy-done | bytes 221208
  68.3 5.1 %scatter.1 = (f32[2192,512]{1,0:T(8,128)}, f32[1,192,128]{2,1,0:T(8,128)}) custom-call(s32[1,384]{1,0:T(1,128)S(1)} %copy-done.7, f32[9,1,384]{2,1,0:T(1,128)S(1)} %copy-done.5, bf16[288,384]{1,0:T(8,128)(2,1)S(1)} %copy-done.3, bf16[288,512]{1,0:T(8,128)(2,1)S(1)} %collective-permute-done.4.row_first_ref, ...), custom_call_target="tpu_custom_call" | custom-call | tf_op jit(solution)/shard_map/scatter/pallas_call | solution.py:635
  (2 shorter events, 0.0 us)
Async XLA Ops:
  0.6 1.6 %copy-start.1 = (bf16[2,137,8,512]{3,2,1,0:T(8,128)(2,1)S(1)}, bf16[2,137,8,512]{3,2,1,0:T(8,128)(2,1)}, u32[]{:S(2)}) copy-start(bf16[2,137,8,512]{3,2,1,0:T(8,128)(2,1)} %param.7) | copy-start | bytes 6733828
  2.3 0.9 %copy-start.4 = (f32[1,192,128]{2,1,0:T(8,128)S(1)}, f32[1,192,128]{2,1,0:T(8,128)}, u32[]{:S(2)}) copy-start(f32[1,192,128]{2,1,0:T(8,128)} %cot_ref.1) | copy-start | bytes 294916
  5.4 1.4 %copy-start = (bf16[8,288,512]{2,1,0:T(8,128)(2,1)}, bf16[8,288,512]{2,1,0:T(8,128)(2,1)S(1)}, u32[]{:S(2)}) copy-start(bf16[8,288,512]{2,1,0:T(8,128)(2,1)S(1)} %get-tuple-element.16.rows_hbm) | copy-start | bytes 7077892
  6.9 15.9 %all-to-all-start = ((bf16[4,240,128]{2,1,0:T(8,128)(2,1)}), bf16[4,240,128]{2,1,0:T(8,128)(2,1)S(1)}, u32[]{:S(2)}, u32[]{:S(2)}) async-start(bf16[4,240,128]{2,1,0:T(8,128)(2,1)} %get-tuple-element.15), calls=%async_computation | async-start | bytes 491520 | tf_op jit(solution)/shard_map/all_to_all | solution.py:564
  13.2 12.6 %collective-permute-start.2 = (bf16[288,512]{1,0:T(8,128)(2,1)S(1)}, bf16[288,512]{1,0:T(8,128)(2,1)S(1)}, u32[]{:S(2)}, u32[]{:S(2)}) collective-permute-start(bf16[288,512]{1,0:T(8,128)(2,1)S(1)} %get-tuple-element.17), channel_id=1, source_target_pairs={{0,4},{4,0},{8,12},{12,8},{1,5},{5,1},{9,13},{13,9},{2,6},{6,2},{1... | collective-permute-start | bytes 884744 | tf_op jit(solution)/shard_map/ppermute | solution.py:565
  15.2 10.6 %collective-permute-start.3 = (bf16[288,512]{1,0:T(8,128)(2,1)S(1)}, bf16[288,512]{1,0:T(8,128)(2,1)S(1)}, u32[]{:S(2)}, u32[]{:S(2)}) collective-permute-start(bf16[288,512]{1,0:T(8,128)(2,1)S(1)} %get-tuple-element.18), channel_id=1, source_target_pairs={{4,8},{8,4},{5,9},{9,5},{6,10},{10,6},{7,11},{11,7},{20,24},{24,20... | collective-permute-start | bytes 884744 | tf_op jit(solution)/shard_map/ppermute | solution.py:566
  22.7 3.6 %copy-start.2 = (bf16[4,240,128]{2,1,0:T(8,128)(2,1)}, bf16[4,240,128]{2,1,0:T(8,128)(2,1)S(1)}, u32[]{:S(2)}) copy-start(bf16[4,240,128]{2,1,0:T(8,128)(2,1)S(1)} %all-to-all-done.lat_ref.lat_hbm) | copy-start | bytes 737284
  22.7 44.6 %copy-start.5 = (f32[9,1,384]{2,1,0:T(1,128)S(1)}, f32[9,1,384]{2,1,0:T(1,128)}, u32[]{:S(2)}) copy-start(f32[9,1,384]{2,1,0:T(1,128)} %weight_ref.3) | copy-start | bytes 41476
  22.8 44.6 %copy-start.7 = (s32[1,384]{1,0:T(1,128)S(1)}, s32[1,384]{1,0:T(1,128)}, u32[]{:S(2)}) copy-start(s32[1,384]{1,0:T(1,128)} %cells_ref.3) | copy-start | bytes 4612
  22.8 3.5 %collective-permute-start.1 = (bf16[32,384]{1,0:T(8,128)(2,1)S(1)}, bf16[32,384]{1,0:T(8,128)(2,1)S(1)}, u32[]{:S(2)}, u32[]{:S(2)}) collective-permute-start(bf16[32,384]{1,0:T(8,128)(2,1)S(1)} %blend.1), channel_id=1, source_target_pairs={{0,3},{1,2},{2,1},{3,0},{4,7},{5,6},{6,5},{7,4},{8,11},{9,10},{10,... | collective-permute-start | bytes 73736 | tf_op jit(solution)/shard_map/ppermute | solution.py:578
  22.8 3.5 %collective-permute-start = (bf16[32,384]{1,0:T(8,128)(2,1)S(1)}, bf16[32,384]{1,0:T(8,128)(2,1)S(1)}, u32[]{:S(2)}, u32[]{:S(2)}) collective-permute-start(bf16[32,384]{1,0:T(8,128)(2,1)S(1)} %blend.1), channel_id=1, source_target_pairs={{0,1},{1,0},{2,3},{3,2},{4,5},{5,4},{6,7},{7,6},{8,9},{9,8},{10,11... | collective-permute-start | bytes 73736 | tf_op jit(solution)/shard_map/ppermute | solution.py:577
  25.8 0.7 copy-start.8
  25.8 0.8 %copy-start.9 = (bf16[288,512]{1,0:T(8,128)(2,1)}, bf16[288,512]{1,0:T(8,128)(2,1)S(1)}, u32[]{:S(2)}) copy-start(bf16[288,512]{1,0:T(8,128)(2,1)S(1)} %collective-permute-done.3.row_second_hbm) | copy-start | bytes 884740
  26.3 0.6 copy-start.10
  26.3 0.6 copy-start.11
  50.0 13.5 %all-to-all-start.1 = ((bf16[4,240,128]{2,1,0:T(8,128)(2,1)}), bf16[4,240,128]{2,1,0:T(8,128)(2,1)S(1)}, u32[]{:S(2)}, u32[]{:S(2)}) async-start(bf16[4,240,128]{2,1,0:T(8,128)(2,1)} %get-tuple-element.23), calls=%async_computation.1 | async-start | bytes 491520 | tf_op jit(solution)/shard_map/all_to_all | solution.py:622
  53.7 12.8 %collective-permute-start.4 = (bf16[288,512]{1,0:T(8,128)(2,1)}, bf16[288,512]{1,0:T(8,128)(2,1)S(1)}, u32[]{:S(2)}, u32[]{:S(2)}) collective-permute-start(bf16[288,512]{1,0:T(8,128)(2,1)} %get-tuple-element.20), channel_id=1, source_target_pairs={{0,4},{4,0},{8,12},{12,8},{1,5},{5,1},{9,13},{13,9},{2,6},{6,2},{1... | collective-permute-start | bytes 884744 | tf_op jit(solution)/shard_map/ppermute | solution.py:620
  55.9 10.6 %collective-permute-start.5 = (bf16[288,512]{1,0:T(8,128)(2,1)}, bf16[288,512]{1,0:T(8,128)(2,1)S(1)}, u32[]{:S(2)}, u32[]{:S(2)}) collective-permute-start(bf16[288,512]{1,0:T(8,128)(2,1)} %get-tuple-element.21), channel_id=1, source_target_pairs={{4,8},{8,4},{5,9},{9,5},{6,10},{10,6},{7,11},{11,7},{20,24},{24,20... | collective-permute-start | bytes 884744 | tf_op jit(solution)/shard_map/ppermute | solution.py:621
  63.5 0.7 copy-start.6
  64.2 3.2 %collective-permute-start.7 = (bf16[16,384]{1,0:T(8,128)(2,1)S(1)}, bf16[16,384]{1,0:T(8,128)(2,1)S(1)}, u32[]{:S(2)}, u32[]{:S(2)}) collective-permute-start(bf16[16,384]{1,0:T(8,128)(2,1)S(1)} %corner.1), channel_id=1, source_target_pairs={{0,3},{1,2},{2,1},{3,0},{4,7},{5,6},{6,5},{7,4},{8,11},{9,10},{10,... | collective-permute-start | bytes 36872 | tf_op jit(solution)/shard_map/ppermute | solution.py:633
  64.3 3.1 %collective-permute-start.6 = (bf16[16,384]{1,0:T(8,128)(2,1)S(1)}, bf16[16,384]{1,0:T(8,128)(2,1)S(1)}, u32[]{:S(2)}, u32[]{:S(2)}) collective-permute-start(bf16[16,384]{1,0:T(8,128)(2,1)S(1)} %corner.1), channel_id=1, source_target_pairs={{0,1},{1,0},{2,3},{3,2},{4,5},{5,4},{6,7},{7,6},{8,9},{9,8},{10,11... | collective-permute-start | bytes 36872 | tf_op jit(solution)/shard_map/ppermute | solution.py:632
  67.4 0.9 %copy-start.3 = (bf16[288,384]{1,0:T(8,128)(2,1)S(1)}, bf16[288,384]{1,0:T(8,128)(2,1)}, u32[]{:S(2)}) copy-start(bf16[288,384]{1,0:T(8,128)(2,1)} %get-tuple-element.19.grad_ref) | copy-start | bytes 663556

commit v3 on v2

--- a/solution.py
+++ b/solution.py
@@ -15,7 +15,7 @@
 BLOCKS = 2
 VMEM = pl.BlockSpec(memory_space=pltpu.VMEM)
 SMEM = pl.BlockSpec(memory_space=pltpu.SMEM)
-HBM = pl.BlockSpec(memory_space=pl.ANY)
+HBM = pl.BlockSpec(memory_space=pltpu.HBM)
 SMALL = pl.CostEstimate(flops=1000, bytes_accessed=1000, transcendentals=0)
 NN = (((1,), (0,)), ((), ()))
 NT = (((1,), (1,)), ((), ()))
@@ -127,30 +127,76 @@
     return west, east
 
 
-def pack_kernel(dims, profiles_ref, cot_ref, rows_ref, first_ref, second_ref, edge_ref, send_ref, wide_ref):
+def copies(pairs_of, sems):
+    moves = [pltpu.make_async_copy(source, target, sems.at[k]) for k, (source, target) in enumerate(pairs_of)]
+    for move in moves:
+        move.start()
+    return moves
+
+
+def load_profiles(profiles_hbm, part_ref, sems):
+    tiles = part_ref.shape[0]
+    return copies(
+        [(profiles_hbm.at[:, :, t * LANES : (t + 1) * LANES], part_ref.at[t]) for t in range(tiles)], sems
+    )
+
+
+def widen(t, part_ref, wide_ref):
+    wide_ref[t] = part_ref[t].astype(F32).reshape(wide_ref.shape[1:])
+
+
+def grid_row(levels, rows, pad, wide_ref, t, r):
+    blank = jnp.zeros((pad - levels, LANES), F32)
+    halves = []
+    for v in range(2):
+        halves += [wide_ref[t, pl.ds(v * levels * rows + r, levels, stride=rows), :], blank]
+    return jnp.concatenate(halves, axis=0).astype(BF16)
+
+
+def pack_kernel(
+    dims,
+    profiles_hbm,
+    cot_hbm,
+    first_ref,
+    second_ref,
+    edge_ref,
+    send_ref,
+    part_ref,
+    wide_ref,
+    ends_ref,
+    cot_ref,
+    sems,
+    cot_sem,
+):
     levels, rows, width, pad = dims
-    for lane in range(0, width, LANES):
-        part = profiles_ref[:, :, lane : lane + LANES]
-        wide_ref[lane // LANES] = part.astype(F32).reshape(2 * levels * rows, LANES)
+    tiles = width // LANES
+    loads = load_profiles(profiles_hbm, part_ref, sems)
+    cot_load = copies([(cot_hbm, cot_ref)], cot_sem)[0]
     edges = jnp.zeros((EDGE, 2 * pad), F32)
     k = iota((EDGE, LANES), 0)
     at_lane = iota((EDGE, LANES), 1)
-    for r in range(rows):
-        out = rows_ref.at[r]
-        for v in range(2):
-            for lane in range(0, width, LANES):
-                value = wide_ref[lane // LANES, pl.ds(v * levels * rows + r, levels, stride=rows), :]
-                value = jnp.concatenate([value, jnp.zeros((pad - levels, LANES), F32)], axis=0)
-                out[v * pad : (v + 1) * pad, lane : lane + LANES] = value.astype(BF16)
-        west = jnp.where((k == r) & (at_lane == 0), 1.0, 0.0).astype(BF16)
-        east = jnp.where((k == rows + r) & (at_lane == LANES - 1), 1.0, 0.0).astype(BF16)
-        edges = edges + dot(west, out[:, :LANES], NT) + dot(east, out[:, width - LANES :], NT)
+    for t in range(tiles):
+        loads[t].wait()
+        widen(t, part_ref, wide_ref)
+        for r in range(rows):
+            if 0 < r < rows - 1 and 0 < t < tiles - 1:
+                continue
+            value = grid_row(levels, rows, pad, wide_ref, t, r)
+            if r in (0, rows - 1):
+                ends_ref[min(r, 1), :, t * LANES : (t + 1) * LANES] = value
+            if t == 0:
+                at = jnp.where((k == r) & (at_lane == 0), 1.0, 0.0).astype(BF16)
+                edges = edges + dot(at, value, NT)
+            if t == tiles - 1:
+                at = jnp.where((k == rows + r) & (at_lane == LANES - 1), 1.0, 0.0).astype(BF16)
+                edges = edges + dot(at, value, NT)
     edge_ref[...] = jnp.zeros(edge_ref.shape, BF16)
     edge_ref[:, : 2 * pad] = edges.astype(BF16)
     even, _ = pair_place("lat")
-    first_ref[...] = rows_ref[jnp.where(even, rows - 1, 0)]
-    second_ref[...] = rows_ref[jnp.where(even, 0, rows - 1)]
+    first_ref[...] = ends_ref[jnp.where(even, 1, 0)]
+    second_ref[...] = ends_ref[jnp.where(even, 0, 1)]
     proc = cot_ref.shape[1]
+    cot_load.wait()
     cot = cot_ref[0].astype(BF16)
 
     def share(s, carry):
@@ -376,6 +422,40 @@
                 send_ref[at, proc + EDGE * t : proc + EDGE * (t + 1), :] = part
 
 
+def gather_kernel(
+    dims,
+    cells_ref,
+    weight_ref,
+    absorb_ref,
+    profiles_hbm,
+    field_hbm,
+    turned_hbm,
+    part_ref,
+    wide_ref,
+    rows_ref,
+    columns_ref,
+    field_ref,
+    turned_ref,
+    sems,
+    out_sems,
+):
+    levels, rows, width, pad = dims
+    loads = load_profiles(profiles_hbm, part_ref, sems)
+    fill_columns(cells_ref, weight_ref, columns_ref)
+    row, _ = split_cells(cells_ref[...], width)
+    turn_absorption(absorb_ref, turned_ref)
+    outs = copies([(turned_ref, turned_hbm)], out_sems.at[pl.ds(0, 1)])
+    for t in range(width // LANES):
+        loads[t].wait()
+        widen(t, part_ref, wide_ref)
+        for r in range(rows):
+            rows_ref[r, :, t * LANES : (t + 1) * LANES] = grid_row(levels, rows, pad, wide_ref, t, r)
+    gather_rows(rows, row, columns_ref, rows_ref, field_ref)
+    outs += copies([(field_ref, field_hbm)], out_sems.at[pl.ds(1, 1)])
+    for move in outs:
+        move.wait()
+
+
 def transfer_kernel(
     dims,
     cells_ref,
@@ -385,7 +465,8 @@
     absorb_ref,
     side_first_ref,
     side_second_ref,
-    rows_hbm,
+    field_hbm,
+    turned_hbm,
     row_first_hbm,
     row_second_hbm,
     lat_hbm,
@@ -406,7 +487,6 @@
     s_part_ref,
     r_part_ref,
     shift_ref,
-    rows_ref,
     row_first_ref,
     row_second_ref,
     lat_ref,
@@ -417,7 +497,8 @@
         pltpu.make_async_copy(source, target, sems.at[k])
         for k, (source, target) in enumerate(
             (
-                (rows_hbm, rows_ref),
+                (field_hbm, field_ref),
+                (turned_hbm, turned_ref),
                 (row_first_hbm, row_first_ref),
                 (row_second_hbm, row_second_ref),
                 (lat_hbm, lat_ref),
@@ -432,10 +513,7 @@
     row, _ = split_cells(cells_ref[...], width)
     halo_rows = pair_rows(rows, n_lat)
     edge_w = edge_weights(cells_ref, weight_ref, rows, width)
-    turn_absorption(absorb_ref, turned_ref)
-    moves[0].wait()
-    gather_rows(rows, row, columns_ref, rows_ref, field_ref)
-    for move in moves[1:]:
+    for move in moves:
         move.wait()
     gather_halo(halo_rows, row, columns_ref, row_first_ref, row_second_ref, field_ref)
     gather_edges(rows, pad, n_lon, side_first_ref, side_second_ref, halo_ref, edge_w, field_ref)
@@ -551,18 +629,49 @@
     lat_shape = shape((n_lat, lat_rows, channels), BF16)
     absorb = jnp.transpose(absorption, (2, 0, 1))
 
-    row_data, row_first, row_second, edge, lat_send = pl.pallas_call(
+    profiles = profiles.reshape(2 * levels, rows, width)
+    tiles = width // LANES
+    unpacked = [
+        pltpu.VMEM((tiles, 2 * levels, rows, LANES), BF16),
+        pltpu.VMEM((tiles, 2 * levels * rows, LANES), F32),
+    ]
+    row_first, row_second, edge, lat_send = pl.pallas_call(
         functools.partial(pack_kernel, (levels, rows, width, pad)),
-        out_shape=(shape((rows, 2 * pad, width), BF16), row_shape, row_shape, edge_shape, lat_shape),
-        in_specs=[VMEM] * 2,
-        out_specs=(VMEM,) * 5,
-        scratch_shapes=[pltpu.VMEM((width // LANES, 2 * levels * rows, LANES), F32)],
-        compiler_params=params(12),
+        out_shape=(row_shape, row_shape, edge_shape, lat_shape),
+        in_specs=[HBM] * 2,
+        out_specs=(VMEM,) * 4,
+        scratch_shapes=unpacked
+        + [
+            pltpu.VMEM((2, 2 * pad, width), BF16),
+            pltpu.VMEM((1, proc, channels), F32),
+            pltpu.SemaphoreType.DMA((tiles,)),
+            pltpu.SemaphoreType.DMA((1,)),
+        ],
+        compiler_params=params(56),
         name="pack",
-    )(profiles.reshape(2 * levels, rows, width), cotangent)
+    )(profiles, cotangent)
 
     lat_in = lax.all_to_all(lat_send, "lat", 0, 0, tiled=True)
     row_first = lax.ppermute(row_first, "lat", lat_pairs[0])
+
+    field, turned = pl.pallas_call(
+        functools.partial(gather_kernel, (levels, rows, width, pad)),
+        out_shape=(shape((2 * pad, obs), F32), shape((blocks, channels, LANES), F32)),
+        in_specs=[VMEM] * 3 + [HBM],
+        out_specs=(HBM,) * 2,
+        scratch_shapes=unpacked
+        + [
+            pltpu.VMEM((rows, 2 * pad, width), BF16),
+            pltpu.VMEM((3, width, obs), BF16),
+            pltpu.VMEM((2 * pad, obs), F32),
+            pltpu.VMEM((blocks, channels, LANES), F32),
+            pltpu.SemaphoreType.DMA((tiles,)),
+            pltpu.SemaphoreType.DMA((2,)),
+        ],
+        compiler_params=params(56),
+        name="gather",
+    )(obs_cell, obs_weight, absorb, profiles)
+    row_second, field = lax.optimization_barrier((row_second, field))
     row_second = lax.ppermute(row_second, "lat", lat_pairs[1])
 
     side = pl.pallas_call(
@@ -580,7 +689,7 @@
     grad, grad_first, grad_second, grad_edge, lat_back = pl.pallas_call(
         functools.partial(transfer_kernel, (levels, rows, width, pad, batch, proc, n_lat, n_lon)),
         out_shape=(shape((2 * pad, obs), BF16), row_shape, row_shape, edge_shape, lat_shape),
-        in_specs=[VMEM, VMEM, SMEM, SMEM] + [VMEM] * 3 + [HBM] * 4,
+        in_specs=[VMEM, VMEM, SMEM, SMEM] + [VMEM] * 3 + [HBM] * 5,
         out_specs=(VMEM,) * 5,
         scratch_shapes=[
             pltpu.VMEM((3, width, obs), BF16),
@@ -595,11 +704,10 @@
             pltpu.VMEM((obs // LANES, pad * 8, LANES), F32),
             pltpu.VMEM((obs // LANES, pad * 8, LANES), F32),
             pltpu.VMEM((pad + 8, obs), F32),
-            pltpu.VMEM((rows, 2 * pad, width), BF16),
             pltpu.VMEM(row_shape.shape, BF16),
             pltpu.VMEM(row_shape.shape, BF16),
             pltpu.VMEM(lat_shape.shape, BF16),
-            pltpu.SemaphoreType.DMA((4,)),
+            pltpu.SemaphoreType.DMA((5,)),
         ],
         compiler_params=params(56),
         name="transfer",
@@ -611,7 +719,8 @@
         absorb,
         side_first,
         side_second,
-        row_data,
+        field,
+        turned,
         row_first,
         row_second,
         lat_in,

time: 73.9 us -> 72.4 us (0.980)
  waiting for transfers between devices: 18.6 us -> 9.72 us
  starting transfers between devices: 17.5 us -> 23.2 us
  Pallas kernels: 30.5 us -> 35.6 us
  local copies, waits for them, and re-layouts: 6.18 us -> 2.46 us
    all_to_all x1, waiting for transfers between devices: 6.85 us -> 0.01 us  [per_device(): lat_in = lax.all_to_all(lat_send, 'lat', 0, 0, tiled=True)]
    pallas_call x0 -> x1, Pallas kernels: none -> 5.38 us  [per_device(): pl.pallas_call(functools.partial(gather_kernel, (levels, rows, width, pad...]
    all_to_all x1, starting transfers between devices: 3.68 us -> 8.09 us  [per_device(): lat_got = lax.all_to_all(lat_back, 'lat', 0, 0, tiled=True)]
    unnamed x24 -> x22, local copies, waits for them, and re-layouts: 6.18 us -> 2.46 us
    all_to_all x1, waiting for transfers between devices: 6.93 us -> 5.26 us  [per_device(): lat_got = lax.all_to_all(lat_back, 'lat', 0, 0, tiled=True)]
    ppermute x1, waiting for transfers between devices: 2.05 us -> 0.48 us  [per_device(): grad_first = lax.ppermute(grad_first, 'lat', lat_pairs[0])]
    ppermute x1, waiting for transfers between devices: 1.36 us -> 2.75 us  [per_device(): row_first = lax.ppermute(row_first, 'lat', lat_pairs[0])]
    ppermute x1, starting transfers between devices: 0.17 us -> 1.54 us  [per_device(): grad_side_first = lax.ppermute(grad_side, 'lon', lon_pairs[0])]
  transfers between devices with their start and end apart: 10 -> 10, of which waited for: 6 -> 4; matrix products, arithmetic and copies ran while one was open for 0% -> 0% of each run, Pallas kernels for 0% -> 8%
where the time goes in v3:
time: 72.4 us; the launch traced here: 71.8 us
  Pallas kernels  35.6 us (49%)
  starting transfers between devices  23.2 us (32%)
  waiting for transfers between devices  9.72 us (13%)
  local copies, waits for them, and re-layouts  2.46 us (3%)
  between operations  0.81 us (1%)
    pallas_call x1, Pallas kernels, per_device(): pl.pallas_call(functools.partial(transfer_kernel, (levels, rows, width, p...  21.8 us
    all_to_all x1, starting transfers between devices, per_device(): lat_got = lax.all_to_all(lat_back, 'lat', 0, 0, tiled=True)  8.09 us
    all_to_all x1, starting transfers between devices, per_device(): lat_in = lax.all_to_all(lat_send, 'lat', 0, 0, tiled=True)  6.46 us
    pallas_call x1, Pallas kernels, per_device(): pl.pallas_call(functools.partial(gather_kernel, (levels, rows, width, pad...  5.38 us
    all_to_all x1, waiting for transfers between devices, per_device(): lat_got = lax.all_to_all(lat_back, 'lat', 0, 0, tiled=True)  5.26 us
    pallas_call x1, Pallas kernels, per_device(): pl.pallas_call(functools.partial(scatter_kernel, (levels, rows, width, pa...  5.12 us
    pallas_call x1, Pallas kernels, per_device(): pl.pallas_call(functools.partial(pack_kernel, (levels, rows, width, pad))...  3.26 us
    ppermute x1, waiting for transfers between devices, per_device(): row_first = lax.ppermute(row_first, 'lat', lat_pairs[0])  2.75 us
  transfers between devices with their start and end apart: 10, of which 4 were waited for; matrix products, arithmetic and copies ran while one was open for 0% of the time, Pallas kernels for 8%

profile of v3, /device:TPU:0, one launch (start us, length us, event | category | flops | bytes accessed | tf_op | source)
XLA Modules:
  0.0 71.8 jit_solution(12891723495326334047)
XLA Ops:
  0.6 3.3 %pack.1 = (bf16[288,512]{1,0:T(8,128)(2,1)}, bf16[288,512]{1,0:T(8,128)(2,1)}, bf16[16,384]{1,0:T(8,128)(2,1)}, bf16[4,240,128]{2,1,0:T(8,128)(2,1)}) custom-call(bf16[274,8,512]{2,1,0:T(8,128)(2,1)} %bitcast.3, f32[1,192,128]{2,1,0:T(8,128)} %cot_hbm.1), custom_call_target="tpu_custom_call" | custom-call | tf_op jit(solution)/shard_map/pack/pallas_call | solution.py:638
  3.9 0.0 copy-start.10
  3.9 0.0 copy-start.5
  3.9 6.5 %all-to-all-start = ((bf16[4,240,128]{2,1,0:T(8,128)(2,1)}), bf16[4,240,128]{2,1,0:T(8,128)(2,1)S(1)}, u32[]{:S(2)}, u32[]{:S(2)}) async-start(bf16[4,240,128]{2,1,0:T(8,128)(2,1)} %get-tuple-element.18), calls=%async_computation | async-start | bytes 491520 | tf_op jit(solution)/shard_map/all_to_all | solution.py:654
  10.4 2.0 %collective-permute-start.2 = (bf16[288,512]{1,0:T(8,128)(2,1)}, bf16[288,512]{1,0:T(8,128)(2,1)S(1)}, u32[]{:S(2)}, u32[]{:S(2)}) collective-permute-start(bf16[288,512]{1,0:T(8,128)(2,1)} %get-tuple-element.23), channel_id=1, source_target_pairs={{0,4},{4,0},{8,12},{12,8},{1,5},{5,1},{9,13},{13,9},{2,6},{6,2},{1... | collective-permute-start | bytes 884744 | tf_op jit(solution)/shard_map/ppermute | solution.py:655
  12.4 5.4 %gather.1 = (f32[288,384]{1,0:T(8,128)}, f32[18,128,128]{2,1,0:T(8,128)}) custom-call(s32[1,384]{1,0:T(1,128)} %cells_ref.5, f32[9,1,384]{2,1,0:T(1,128)} %weight_ref.5, bf16[137,16,128]{2,1,0:T(8,128)(2,1)} %bitcast.5, bf16[274,8,512]{2,1,0:T(8,128)(2,1)} %bitcast.4), custom_call_target="tpu_custom_call" | custom-call | tf_op jit(solution)/shard_map/gather/pallas_call | solution.py:657
  17.8 0.0 copy-start.2
  17.8 0.0 copy-start.3
  17.8 0.0 copy-done.10
  17.8 0.7 collective-permute-start.3
  18.5 0.0 all-to-all-done.lat_ref.lat_hbm
  18.5 0.0 copy-start
  18.5 0.0 copy-done.5
  18.6 0.2 collective-permute-start.1
  18.7 1.5 %collective-permute-start = (bf16[32,384]{1,0:T(8,128)(2,1)S(1)}, bf16[32,384]{1,0:T(8,128)(2,1)S(1)}, u32[]{:S(2)}, u32[]{:S(2)}) collective-permute-start(bf16[32,384]{1,0:T(8,128)(2,1)S(1)} %blend.1), channel_id=1, source_target_pairs={{0,1},{1,0},{2,3},{3,2},{4,5},{5,4},{6,7},{7,6},{8,9},{9,8},{10,11... | collective-permute-start | bytes 73736 | tf_op jit(solution)/shard_map/ppermute | solution.py:686
  20.2 2.8 %collective-permute-done.2.row_first_hbm = bf16[288,512]{1,0:T(8,128)(2,1)S(1)} collective-permute-done((bf16[288,512]{1,0:T(8,128)(2,1)}, bf16[288,512]{1,0:T(8,128)(2,1)S(1)}, u32[]{:S(2)}, u32[]{:S(2)}) %collective-permute-start.2) | collective-permute-done | bytes 294944 | tf_op jit(solution)/shard_map/ppermute | solution.py:655
  23.0 0.0 copy-start.6
  23.0 0.0 collective-permute-done.3.row_second_hbm
  23.0 0.0 copy-start.7
  23.0 0.0 collective-permute-done.1.side_second_ref
  23.0 0.0 copy-start.8
  23.0 0.0 collective-permute-done.side_first_ref
  23.0 0.0 copy-start.9
  23.1 0.0 copy-done
  23.1 0.6 copy-done.6
  23.7 0.1 copy-done.7
  23.8 0.0 copy-done.8
  23.8 0.0 copy-done.9
  23.8 21.8 %transfer.1 = (bf16[288,384]{1,0:T(8,128)(2,1)}, bf16[288,512]{1,0:T(8,128)(2,1)}, bf16[288,512]{1,0:T(8,128)(2,1)}, bf16[16,384]{1,0:T(8,128)(2,1)}, bf16[4,240,128]{2,1,0:T(8,128)(2,1)}) custom-call(s32[1,384]{1,0:T(1,128)} %cells_ref.5, f32[9,1,384]{2,1,0:T(1,128)} %weight_ref.5, s32[1,24]{1,0:T(1,128)} %instr_ref.1, s32[1,24]{1,0:T(1,128)} %dest_ref.1, ...), custom_call_target="tpu_custom_call" | custom-call | tf_op jit(solution)/shard_map/transfer/pallas_call | solution.py:689
  45.7 8.1 %all-to-all-start.1 = ((bf16[4,240,128]{2,1,0:T(8,128)(2,1)}), bf16[4,240,128]{2,1,0:T(8,128)(2,1)S(1)}, u32[]{:S(2)}, u32[]{:S(2)}) async-start(bf16[4,240,128]{2,1,0:T(8,128)(2,1)} %get-tuple-element.29), calls=%async_computation.1 | async-start | bytes 491520 | tf_op jit(solution)/shard_map/all_to_all | solution.py:731
  53.8 2.0 %collective-permute-start.4 = (bf16[288,512]{1,0:T(8,128)(2,1)}, bf16[288,512]{1,0:T(8,128)(2,1)S(1)}, u32[]{:S(2)}, u32[]{:S(2)}) collective-permute-start(bf16[288,512]{1,0:T(8,128)(2,1)} %get-tuple-element.26), channel_id=1, source_target_pairs={{0,4},{4,0},{8,12},{12,8},{1,5},{5,1},{9,13},{13,9},{2,6},{6,2},{1... | collective-permute-start | bytes 884744 | tf_op jit(solution)/shard_map/ppermute | solution.py:729
  55.8 0.7 collective-permute-start.5
  56.4 5.3 %all-to-all-done.1.lat_ref = bf16[4,240,128]{2,1,0:T(8,128)(2,1)S(1)} async-done(((bf16[4,240,128]{2,1,0:T(8,128)(2,1)}), bf16[4,240,128]{2,1,0:T(8,128)(2,1)S(1)}, u32[]{:S(2)}, u32[]{:S(2)}) %all-to-all-start.1) | async-done | bytes 245792 | tf_op jit(solution)/shard_map/all_to_all | solution.py:731
  61.7 0.0 copy-start.4
  61.7 0.7 copy-done.4
  62.4 0.1 collective-permute-start.7
  62.5 1.5 %collective-permute-start.6 = (bf16[16,384]{1,0:T(8,128)(2,1)S(1)}, bf16[16,384]{1,0:T(8,128)(2,1)S(1)}, u32[]{:S(2)}, u32[]{:S(2)}) collective-permute-start(bf16[16,384]{1,0:T(8,128)(2,1)S(1)} %corner.1), channel_id=1, source_target_pairs={{0,1},{1,0},{2,3},{3,2},{4,5},{5,4},{6,7},{7,6},{8,9},{9,8},{10,11... | collective-permute-start | bytes 36872 | tf_op jit(solution)/shard_map/ppermute | solution.py:741
  64.1 0.5 collective-permute-done.4.row_first_ref
  64.5 0.0 collective-permute-done.5.row_second_ref
  64.5 1.2 %collective-permute-done.7.side_second_ref = bf16[16,384]{1,0:T(8,128)(2,1)S(1)} collective-permute-done((bf16[16,384]{1,0:T(8,128)(2,1)S(1)}, bf16[16,384]{1,0:T(8,128)(2,1)S(1)}, u32[]{:S(2)}, u32[]{:S(2)}) %collective-permute-start.7) | collective-permute-done | bytes 12320 | tf_op jit(solution)/shard_map/ppermute | solution.py:742
  65.7 0.0 collective-permute-done.6.side_first_ref
  65.8 0.0 copy-done.2
  65.8 0.0 copy-done.3
  65.8 0.0 copy-start.1
  65.8 0.9 %copy-done.1 = bf16[288,384]{1,0:T(8,128)(2,1)S(1)} copy-done((bf16[288,384]{1,0:T(8,128)(2,1)S(1)}, bf16[288,384]{1,0:T(8,128)(2,1)}, u32[]{:S(2)}) %copy-start.1) | copy-done | bytes 221208
  66.7 5.1 %scatter.1 = (f32[2192,512]{1,0:T(8,128)}, f32[1,192,128]{2,1,0:T(8,128)}) custom-call(s32[1,384]{1,0:T(1,128)S(1)} %copy-done.3, f32[9,1,384]{2,1,0:T(1,128)S(1)} %copy-done.2, bf16[288,384]{1,0:T(8,128)(2,1)S(1)} %copy-done.1, bf16[288,512]{1,0:T(8,128)(2,1)S(1)} %collective-permute-done.4.row_first_ref, ...), custom_call_target="tpu_custom_call" | custom-call | tf_op jit(solution)/shard_map/scatter/pallas_call | solution.py:744
  (2 shorter events, 0.0 us)
Async XLA Ops:
  3.9 13.9 %copy-start.10 = (bf16[288,512]{1,0:T(8,128)(2,1)S(1)}, bf16[288,512]{1,0:T(8,128)(2,1)}, u32[]{:S(2)}) copy-start(bf16[288,512]{1,0:T(8,128)(2,1)} %get-tuple-element.24) | copy-start | bytes 884740
  3.9 14.6 %copy-start.5 = (bf16[16,384]{1,0:T(8,128)(2,1)S(1)}, bf16[16,384]{1,0:T(8,128)(2,1)}, u32[]{:S(2)}) copy-start(bf16[16,384]{1,0:T(8,128)(2,1)} %get-tuple-element.17.edge_ref) | copy-start | bytes 36868
  3.9 14.6 %all-to-all-start = ((bf16[4,240,128]{2,1,0:T(8,128)(2,1)}), bf16[4,240,128]{2,1,0:T(8,128)(2,1)S(1)}, u32[]{:S(2)}, u32[]{:S(2)}) async-start(bf16[4,240,128]{2,1,0:T(8,128)(2,1)} %get-tuple-element.18), calls=%async_computation | async-start | bytes 491520 | tf_op jit(solution)/shard_map/all_to_all | solution.py:654
  10.4 12.6 %collective-permute-start.2 = (bf16[288,512]{1,0:T(8,128)(2,1)}, bf16[288,512]{1,0:T(8,128)(2,1)S(1)}, u32[]{:S(2)}, u32[]{:S(2)}) collective-permute-start(bf16[288,512]{1,0:T(8,128)(2,1)} %get-tuple-element.23), channel_id=1, source_target_pairs={{0,4},{4,0},{8,12},{12,8},{1,5},{5,1},{9,13},{13,9},{2,6},{6,2},{1... | collective-permute-start | bytes 884744 | tf_op jit(solution)/shard_map/ppermute | solution.py:655
  17.8 48.0 %copy-start.2 = (f32[9,1,384]{2,1,0:T(1,128)S(1)}, f32[9,1,384]{2,1,0:T(1,128)}, u32[]{:S(2)}) copy-start(f32[9,1,384]{2,1,0:T(1,128)} %weight_ref.5) | copy-start | bytes 41476
  17.8 47.9 %copy-start.3 = (s32[1,384]{1,0:T(1,128)S(1)}, s32[1,384]{1,0:T(1,128)}, u32[]{:S(2)}) copy-start(s32[1,384]{1,0:T(1,128)} %cells_ref.5) | copy-start | bytes 4612
  17.8 5.2 %collective-permute-start.3 = (bf16[288,512]{1,0:T(8,128)(2,1)S(1)}, bf16[288,512]{1,0:T(8,128)(2,1)S(1)}, u32[]{:S(2)}, u32[]{:S(2)}) collective-permute-start(bf16[288,512]{1,0:T(8,128)(2,1)S(1)} %copy-done.10), channel_id=1, source_target_pairs={{4,8},{8,4},{5,9},{9,5},{6,10},{10,6},{7,11},{11,7},{20,24},{24,20... | collective-permute-start | bytes 884744 | tf_op jit(solution)/shard_map/ppermute | solution.py:675
  18.5 4.5 %copy-start = (bf16[4,240,128]{2,1,0:T(8,128)(2,1)}, bf16[4,240,128]{2,1,0:T(8,128)(2,1)S(1)}, u32[]{:S(2)}) copy-start(bf16[4,240,128]{2,1,0:T(8,128)(2,1)S(1)} %all-to-all-done.lat_ref.lat_hbm) | copy-start | bytes 737284
  18.6 4.4 %collective-permute-start.1 = (bf16[32,384]{1,0:T(8,128)(2,1)S(1)}, bf16[32,384]{1,0:T(8,128)(2,1)S(1)}, u32[]{:S(2)}, u32[]{:S(2)}) collective-permute-start(bf16[32,384]{1,0:T(8,128)(2,1)S(1)} %blend.1), channel_id=1, source_target_pairs={{0,3},{1,2},{2,1},{3,0},{4,7},{5,6},{6,5},{7,4},{8,11},{9,10},{10,... | collective-permute-start | bytes 73736 | tf_op jit(solution)/shard_map/ppermute | solution.py:687
  18.7 4.3 %collective-permute-start = (bf16[32,384]{1,0:T(8,128)(2,1)S(1)}, bf16[32,384]{1,0:T(8,128)(2,1)S(1)}, u32[]{:S(2)}, u32[]{:S(2)}) collective-permute-start(bf16[32,384]{1,0:T(8,128)(2,1)S(1)} %blend.1), channel_id=1, source_target_pairs={{0,1},{1,0},{2,3},{3,2},{4,5},{5,4},{6,7},{7,6},{8,9},{9,8},{10,11... | collective-permute-start | bytes 73736 | tf_op jit(solution)/shard_map/ppermute | solution.py:686
  23.0 0.7 copy-start.6
  23.0 0.8 %copy-start.7 = (bf16[288,512]{1,0:T(8,128)(2,1)}, bf16[288,512]{1,0:T(8,128)(2,1)S(1)}, u32[]{:S(2)}) copy-start(bf16[288,512]{1,0:T(8,128)(2,1)S(1)} %collective-permute-done.3.row_second_hbm) | copy-start | bytes 884740
  23.0 0.8 %copy-start.8 = (bf16[32,384]{1,0:T(8,128)(2,1)}, bf16[32,384]{1,0:T(8,128)(2,1)S(1)}, u32[]{:S(2)}) copy-start(bf16[32,384]{1,0:T(8,128)(2,1)S(1)} %collective-permute-done.1.side_second_ref) | copy-start | bytes 73732
  23.0 0.8 %copy-start.9 = (bf16[32,384]{1,0:T(8,128)(2,1)}, bf16[32,384]{1,0:T(8,128)(2,1)S(1)}, u32[]{:S(2)}) copy-start(bf16[32,384]{1,0:T(8,128)(2,1)S(1)} %collective-permute-done.side_first_ref) | copy-start | bytes 73732
  45.7 16.1 %all-to-all-start.1 = ((bf16[4,240,128]{2,1,0:T(8,128)(2,1)}), bf16[4,240,128]{2,1,0:T(8,128)(2,1)S(1)}, u32[]{:S(2)}, u32[]{:S(2)}) async-start(bf16[4,240,128]{2,1,0:T(8,128)(2,1)} %get-tuple-element.29), calls=%async_computation.1 | async-start | bytes 491520 | tf_op jit(solution)/shard_map/all_to_all | solution.py:731
  53.8 10.8 %collective-permute-start.4 = (bf16[288,512]{1,0:T(8,128)(2,1)}, bf16[288,512]{1,0:T(8,128)(2,1)S(1)}, u32[]{:S(2)}, u32[]{:S(2)}) collective-permute-start(bf16[288,512]{1,0:T(8,128)(2,1)} %get-tuple-element.26), channel_id=1, source_target_pairs={{0,4},{4,0},{8,12},{12,8},{1,5},{5,1},{9,13},{13,9},{2,6},{6,2},{1... | collective-permute-start | bytes 884744 | tf_op jit(solution)/shard_map/ppermute | solution.py:729
  55.8 8.8 %collective-permute-start.5 = (bf16[288,512]{1,0:T(8,128)(2,1)}, bf16[288,512]{1,0:T(8,128)(2,1)S(1)}, u32[]{:S(2)}, u32[]{:S(2)}) collective-permute-start(bf16[288,512]{1,0:T(8,128)(2,1)} %get-tuple-element.27), channel_id=1, source_target_pairs={{4,8},{8,4},{5,9},{9,5},{6,10},{10,6},{7,11},{11,7},{20,24},{24,20... | collective-permute-start | bytes 884744 | tf_op jit(solution)/shard_map/ppermute | solution.py:730
  61.7 0.7 copy-start.4
  62.4 3.3 %collective-permute-start.7 = (bf16[16,384]{1,0:T(8,128)(2,1)S(1)}, bf16[16,384]{1,0:T(8,128)(2,1)S(1)}, u32[]{:S(2)}, u32[]{:S(2)}) collective-permute-start(bf16[16,384]{1,0:T(8,128)(2,1)S(1)} %corner.1), channel_id=1, source_target_pairs={{0,3},{1,2},{2,1},{3,0},{4,7},{5,6},{6,5},{7,4},{8,11},{9,10},{10,... | collective-permute-start | bytes 36872 | tf_op jit(solution)/shard_map/ppermute | solution.py:742
  62.5 3.2 %collective-permute-start.6 = (bf16[16,384]{1,0:T(8,128)(2,1)S(1)}, bf16[16,384]{1,0:T(8,128)(2,1)S(1)}, u32[]{:S(2)}, u32[]{:S(2)}) collective-permute-start(bf16[16,384]{1,0:T(8,128)(2,1)S(1)} %corner.1), channel_id=1, source_target_pairs={{0,1},{1,0},{2,3},{3,2},{4,5},{5,4},{6,7},{7,6},{8,9},{9,8},{10,11... | collective-permute-start | bytes 36872 | tf_op jit(solution)/shard_map/ppermute | solution.py:741
  65.8 0.9 %copy-start.1 = (bf16[288,384]{1,0:T(8,128)(2,1)S(1)}, bf16[288,384]{1,0:T(8,128)(2,1)}, u32[]{:S(2)}) copy-start(bf16[288,384]{1,0:T(8,128)(2,1)} %get-tuple-element.25.grad_ref) | copy-start | bytes 663556

commit v4 on v3

--- a/solution.py
+++ b/solution.py
@@ -421,6 +421,10 @@
                 part = jnp.where(mine, part, 0.0).astype(BF16)
                 send_ref[at, proc + EDGE * t : proc + EDGE * (t + 1), :] = part
 
+    for t in range(edge_ref.shape[1] // LANES):
+        part = edge_ref[0:EDGE, t * LANES : (t + 1) * LANES].astype(BF16)
+        send_ref[lax.axis_index("lat"), proc + EDGE * t : proc + EDGE * (t + 1), :] = part
+
 
 def gather_kernel(
     dims,
@@ -473,7 +477,6 @@
     grad_ref,
     grad_first_ref,
     grad_second_ref,
-    grad_edge_ref,
     send_ref,
     columns_ref,
     turned_ref,
@@ -513,13 +516,15 @@
     row, _ = split_cells(cells_ref[...], width)
     halo_rows = pair_rows(rows, n_lat)
     edge_w = edge_weights(cells_ref, weight_ref, rows, width)
-    for move in moves:
-        move.wait()
+    moves[4].wait()
+    departures(batch, proc, dest_ref, lat_ref, cot_rows_ref, cot_t_ref)
+    for k in (0, 2, 3):
+        moves[k].wait()
     gather_halo(halo_rows, row, columns_ref, row_first_ref, row_second_ref, field_ref)
     gather_edges(rows, pad, n_lon, side_first_ref, side_second_ref, halo_ref, edge_w, field_ref)
-    departures(batch, proc, dest_ref, lat_ref, cot_rows_ref, cot_t_ref)
     chosen = chosen_instruments(batch, obs, instr_ref)
     prepare_levels(pad, field_ref, step_ref, rate_ref)
+    moves[1].wait()
     walk_levels(
         levels, instruments, chosen, turned_ref, cot_t_ref, rate_ref, step_ref, signal_ref, s_part_ref, r_part_ref
     )
@@ -541,14 +546,12 @@
         halo_ref,
         send_ref,
     )
-    grad_edge_ref[...] = halo_ref[0:EDGE, :].astype(BF16)
-
-
-def corner_kernel(proc, edge_ref, lat_ref, out_ref):
-    ups, downs = lat_block(lat_ref, proc, -1), lat_block(lat_ref, proc, 1)
-    for t in range(edge_ref.shape[1] // LANES):
-        lanes = slice(t * LANES, (t + 1) * LANES)
-        out_ref[:, lanes] = (edge_ref[:, lanes].astype(F32) + ups[t] + downs[t]).astype(BF16)
+
+
+def corner_kernel(proc, lat_ref, out_ref):
+    owns, ups, downs = [lat_block(lat_ref, proc, side) for side in (0, -1, 1)]
+    for t in range(out_ref.shape[1] // LANES):
+        out_ref[:, t * LANES : (t + 1) * LANES] = (owns[t] + ups[t] + downs[t]).astype(BF16)
 
 
 def scatter_kernel(
@@ -653,6 +656,7 @@
 
     lat_in = lax.all_to_all(lat_send, "lat", 0, 0, tiled=True)
     row_first = lax.ppermute(row_first, "lat", lat_pairs[0])
+    row_second = lax.ppermute(row_second, "lat", lat_pairs[1])
 
     field, turned = pl.pallas_call(
         functools.partial(gather_kernel, (levels, rows, width, pad)),
@@ -671,8 +675,7 @@
         compiler_params=params(56),
         name="gather",
     )(obs_cell, obs_weight, absorb, profiles)
-    row_second, field = lax.optimization_barrier((row_second, field))
-    row_second = lax.ppermute(row_second, "lat", lat_pairs[1])
+    edge, field = lax.optimization_barrier((edge, field))
 
     side = pl.pallas_call(
         functools.partial(blend_kernel, rows, proc),
@@ -686,11 +689,11 @@
     side_first = lax.ppermute(side, "lon", lon_pairs[0])
     side_second = lax.ppermute(side, "lon", lon_pairs[1])
 
-    grad, grad_first, grad_second, grad_edge, lat_back = pl.pallas_call(
+    grad, grad_first, grad_second, lat_back = pl.pallas_call(
         functools.partial(transfer_kernel, (levels, rows, width, pad, batch, proc, n_lat, n_lon)),
-        out_shape=(shape((2 * pad, obs), BF16), row_shape, row_shape, edge_shape, lat_shape),
+        out_shape=(shape((2 * pad, obs), BF16), row_shape, row_shape, lat_shape),
         in_specs=[VMEM, VMEM, SMEM, SMEM] + [VMEM] * 3 + [HBM] * 5,
-        out_specs=(VMEM,) * 5,
+        out_specs=(VMEM,) * 4,
         scratch_shapes=[
             pltpu.VMEM((3, width, obs), BF16),
             pltpu.VMEM((blocks, channels, LANES), F32),
@@ -732,12 +735,12 @@
     grad_side = pl.pallas_call(
         functools.partial(corner_kernel, proc),
         out_shape=edge_shape,
-        in_specs=[VMEM] * 2,
+        in_specs=[VMEM],
         out_specs=VMEM,
         compiler_params=params(4),
         cost_estimate=SMALL,
         name="corner",
-    )(grad_edge, lat_got)
+    )(lat_got)
     grad_side_first = lax.ppermute(grad_side, "lon", lon_pairs[0])
     grad_side_second = lax.ppermute(grad_side, "lon", lon_pairs[1])
 

time: 72.4 us -> 70 us (0.967)
  starting transfers between devices: 23.2 us -> 17.8 us
  waiting for transfers between devices: 9.72 us -> 13.9 us
  local copies, waits for them, and re-layouts: 2.46 us -> 1.56 us
    all_to_all x1, starting transfers between devices: 8.09 us -> 4.09 us  [per_device(): lat_got = lax.all_to_all(lat_back, 'lat', 0, 0, tiled=True)]
    ppermute x1, waiting for transfers between devices: 0.48 us -> 3.52 us  [per_device(): grad_first = lax.ppermute(grad_first, 'lat', lat_pairs[0])]
    all_to_all x1, waiting for transfers between devices: 5.26 us -> 7.03 us  [per_device(): lat_got = lax.all_to_all(lat_back, 'lat', 0, 0, tiled=True)]
    ppermute x1, starting transfers between devices: 1.54 us -> 0.07 us  [per_device(): grad_side_first = lax.ppermute(grad_side, 'lon', lon_pairs[0])]
    all_to_all x1, waiting for transfers between devices: 0.01 us -> 1.43 us  [per_device(): lat_in = lax.all_to_all(lat_send, 'lat', 0, 0, tiled=True)]
    ppermute x1, waiting for transfers between devices: 2.75 us -> 1.37 us  [per_device(): row_first = lax.ppermute(row_first, 'lat', lat_pairs[0])]
    ppermute x1, waiting for transfers between devices: 1.2 us -> 0.01 us  [per_device(): grad_side_second = lax.ppermute(grad_side, 'lon', lon_pairs[1])]
    unnamed x22 -> x18, local copies, waits for them, and re-layouts: 2.46 us -> 1.56 us
  transfers between devices with their start and end apart: 10 -> 10, of which waited for: 4 -> 5; matrix products, arithmetic and copies ran while one was open for 0% -> 0% of each run, Pallas kernels for 8% -> 8%
where the time goes in v4:
time: 70 us; the launch traced here: 69.5 us
  Pallas kernels  35.6 us (51%)
  starting transfers between devices  17.8 us (25%)
  waiting for transfers between devices  13.9 us (20%)
  local copies, waits for them, and re-layouts  1.56 us (2%)
  between operations  0.77 us (1%)
    pallas_call x1, Pallas kernels, per_device(): pl.pallas_call(functools.partial(transfer_kernel, (levels, rows, width, p...  21.8 us
    all_to_all x1, waiting for transfers between devices, per_device(): lat_got = lax.all_to_all(lat_back, 'lat', 0, 0, tiled=True)  7.03 us
    all_to_all x1, starting transfers between devices, per_device(): lat_in = lax.all_to_all(lat_send, 'lat', 0, 0, tiled=True)  6.33 us
    pallas_call x1, Pallas kernels, per_device(): pl.pallas_call(functools.partial(gather_kernel, (levels, rows, width, pad...  5.39 us
    pallas_call x1, Pallas kernels, per_device(): pl.pallas_call(functools.partial(scatter_kernel, (levels, rows, width, pa...  5.12 us
    all_to_all x1, starting transfers between devices, per_device(): lat_got = lax.all_to_all(lat_back, 'lat', 0, 0, tiled=True)  4.09 us
    ppermute x1, waiting for transfers between devices, per_device(): grad_first = lax.ppermute(grad_first, 'lat', lat_pairs[0])  3.52 us
    pallas_call x1, Pallas kernels, per_device(): pl.pallas_call(functools.partial(pack_kernel, (levels, rows, width, pad))...  3.26 us
  transfers between devices with their start and end apart: 10, of which 5 were waited for; matrix products, arithmetic and copies ran while one was open for 0% of the time, Pallas kernels for 8%

profile of v4, /device:TPU:0, one launch (start us, length us, event | category | flops | bytes accessed | tf_op | source)
XLA Modules:
  0.0 69.5 jit_solution(17575594047730569041)
XLA Ops:
  0.6 3.3 %pack.1 = (bf16[288,512]{1,0:T(8,128)(2,1)}, bf16[288,512]{1,0:T(8,128)(2,1)}, bf16[16,384]{1,0:T(8,128)(2,1)}, bf16[4,240,128]{2,1,0:T(8,128)(2,1)}) custom-call(bf16[274,8,512]{2,1,0:T(8,128)(2,1)} %bitcast.3, f32[1,192,128]{2,1,0:T(8,128)} %cot_hbm.1), custom_call_target="tpu_custom_call" | custom-call | tf_op jit(solution)/shard_map/pack/pallas_call | solution.py:641
  3.9 0.0 copy-start.4
  3.9 6.3 %all-to-all-start = ((bf16[4,240,128]{2,1,0:T(8,128)(2,1)}), bf16[4,240,128]{2,1,0:T(8,128)(2,1)S(1)}, u32[]{:S(2)}, u32[]{:S(2)}) async-start(bf16[4,240,128]{2,1,0:T(8,128)(2,1)} %get-tuple-element.19), calls=%async_computation | async-start | bytes 491520 | tf_op jit(solution)/shard_map/all_to_all | solution.py:657
  10.2 2.0 %collective-permute-start.2 = (bf16[288,512]{1,0:T(8,128)(2,1)}, bf16[288,512]{1,0:T(8,128)(2,1)S(1)}, u32[]{:S(2)}, u32[]{:S(2)}) collective-permute-start(bf16[288,512]{1,0:T(8,128)(2,1)} %get-tuple-element.22), channel_id=1, source_target_pairs={{0,4},{4,0},{8,12},{12,8},{1,5},{5,1},{9,13},{13,9},{2,6},{6,2},{1... | collective-permute-start | bytes 884744 | tf_op jit(solution)/shard_map/ppermute | solution.py:658
  12.3 0.7 collective-permute-start.3
  12.9 5.4 %gather.1 = (f32[288,384]{1,0:T(8,128)}, f32[18,128,128]{2,1,0:T(8,128)}) custom-call(s32[1,384]{1,0:T(1,128)} %cells_ref.5, f32[9,1,384]{2,1,0:T(1,128)} %weight_ref.5, bf16[137,16,128]{2,1,0:T(8,128)(2,1)} %bitcast.5, bf16[274,8,512]{2,1,0:T(8,128)(2,1)} %bitcast.4), custom_call_target="tpu_custom_call" | custom-call | tf_op jit(solution)/shard_map/gather/pallas_call | solution.py:661
  18.3 0.0 copy-start.2
  18.3 0.0 copy-start.3
  18.4 1.4 %all-to-all-done.lat_ref.lat_hbm = bf16[4,240,128]{2,1,0:T(8,128)(2,1)S(1)} async-done(((bf16[4,240,128]{2,1,0:T(8,128)(2,1)}), bf16[4,240,128]{2,1,0:T(8,128)(2,1)S(1)}, u32[]{:S(2)}, u32[]{:S(2)}) %all-to-all-start) | async-done | bytes 245792 | tf_op jit(solution)/shard_map/all_to_all | solution.py:657
  19.8 0.0 copy-done.4
  19.8 0.0 copy-start
  19.8 0.1 collective-permute-start.1
  19.9 1.6 %collective-permute-start = (bf16[32,384]{1,0:T(8,128)(2,1)S(1)}, bf16[32,384]{1,0:T(8,128)(2,1)S(1)}, u32[]{:S(2)}, u32[]{:S(2)}) collective-permute-start(bf16[32,384]{1,0:T(8,128)(2,1)S(1)} %blend.1), channel_id=1, source_target_pairs={{0,1},{1,0},{2,3},{3,2},{4,5},{5,4},{6,7},{7,6},{8,9},{9,8},{10,11... | collective-permute-start | bytes 73736 | tf_op jit(solution)/shard_map/ppermute | solution.py:689
  21.5 1.4 %collective-permute-done.2.row_first_hbm = bf16[288,512]{1,0:T(8,128)(2,1)S(1)} collective-permute-done((bf16[288,512]{1,0:T(8,128)(2,1)}, bf16[288,512]{1,0:T(8,128)(2,1)S(1)}, u32[]{:S(2)}, u32[]{:S(2)}) %collective-permute-start.2) | collective-permute-done | bytes 294944 | tf_op jit(solution)/shard_map/ppermute | solution.py:658
  22.9 0.0 copy-start.5
  22.9 0.0 collective-permute-done.3.row_second_hbm
  22.9 0.0 copy-start.6
  22.9 0.5 collective-permute-done.1.side_second_ref
  23.3 0.0 copy-start.7
  23.4 0.0 collective-permute-done.side_first_ref
  23.4 0.0 copy-start.8
  23.4 0.0 copy-done
  23.4 0.2 copy-done.5
  23.6 0.1 copy-done.6
  23.7 0.3 copy-done.7
  24.0 0.0 copy-done.8
  24.0 21.8 %transfer.1 = (bf16[288,384]{1,0:T(8,128)(2,1)}, bf16[288,512]{1,0:T(8,128)(2,1)}, bf16[288,512]{1,0:T(8,128)(2,1)}, bf16[4,240,128]{2,1,0:T(8,128)(2,1)}) custom-call(s32[1,384]{1,0:T(1,128)} %cells_ref.5, f32[9,1,384]{2,1,0:T(1,128)} %weight_ref.5, s32[1,24]{1,0:T(1,128)} %instr_ref.1, s32[1,24]{1,0:T(1,128)} %dest_ref.1, bf16[137,16,128]{2,1,0:T(8,128)(2,1)} %bitcast.6, ...), custom_call_target="tpu_custom_call" | custom-call | tf_op jit(solution)/shard_map/transfer/pallas_call | solution.py:692
  45.8 4.1 %all-to-all-start.1 = ((bf16[4,240,128]{2,1,0:T(8,128)(2,1)}), bf16[4,240,128]{2,1,0:T(8,128)(2,1)S(1)}, u32[]{:S(2)}, u32[]{:S(2)}) async-start(bf16[4,240,128]{2,1,0:T(8,128)(2,1)} %get-tuple-element.27), calls=%async_computation.1 | async-start | bytes 491520 | tf_op jit(solution)/shard_map/all_to_all | solution.py:734
  49.9 2.2 %collective-permute-start.4 = (bf16[288,512]{1,0:T(8,128)(2,1)}, bf16[288,512]{1,0:T(8,128)(2,1)S(1)}, u32[]{:S(2)}, u32[]{:S(2)}) collective-permute-start(bf16[288,512]{1,0:T(8,128)(2,1)} %get-tuple-element.25), channel_id=1, source_target_pairs={{0,4},{4,0},{8,12},{12,8},{1,5},{5,1},{9,13},{13,9},{2,6},{6,2},{1... | collective-permute-start | bytes 884744 | tf_op jit(solution)/shard_map/ppermute | solution.py:732
  52.0 0.7 collective-permute-start.5
  52.7 7.0 %all-to-all-done.1.lat_ref = bf16[4,240,128]{2,1,0:T(8,128)(2,1)S(1)} async-done(((bf16[4,240,128]{2,1,0:T(8,128)(2,1)}), bf16[4,240,128]{2,1,0:T(8,128)(2,1)S(1)}, u32[]{:S(2)}, u32[]{:S(2)}) %all-to-all-start.1) | async-done | bytes 245792 | tf_op jit(solution)/shard_map/all_to_all | solution.py:734
  59.8 0.1 collective-permute-start.7
  59.8 0.1 collective-permute-start.6
  59.9 3.5 %collective-permute-done.4.row_first_ref = bf16[288,512]{1,0:T(8,128)(2,1)S(1)} collective-permute-done((bf16[288,512]{1,0:T(8,128)(2,1)}, bf16[288,512]{1,0:T(8,128)(2,1)S(1)}, u32[]{:S(2)}, u32[]{:S(2)}) %collective-permute-start.4) | collective-permute-done | bytes 294944 | tf_op jit(solution)/shard_map/ppermute | solution.py:732
  63.4 0.0 collective-permute-done.5.row_second_ref
  63.4 0.0 collective-permute-done.7.side_second_ref
  63.5 0.0 collective-permute-done.6.side_first_ref
  63.5 0.0 copy-done.2
  63.5 0.0 copy-done.3
  63.5 0.0 copy-start.1
  63.5 0.9 %copy-done.1 = bf16[288,384]{1,0:T(8,128)(2,1)S(1)} copy-done((bf16[288,384]{1,0:T(8,128)(2,1)S(1)}, bf16[288,384]{1,0:T(8,128)(2,1)}, u32[]{:S(2)}) %copy-start.1) | copy-done | bytes 221208
  64.4 5.1 %scatter.1 = (f32[2192,512]{1,0:T(8,128)}, f32[1,192,128]{2,1,0:T(8,128)}) custom-call(s32[1,384]{1,0:T(1,128)S(1)} %copy-done.3, f32[9,1,384]{2,1,0:T(1,128)S(1)} %copy-done.2, bf16[288,384]{1,0:T(8,128)(2,1)S(1)} %copy-done.1, bf16[288,512]{1,0:T(8,128)(2,1)S(1)} %collective-permute-done.4.row_first_ref, ...), custom_call_target="tpu_custom_call" | custom-call | tf_op jit(solution)/shard_map/scatter/pallas_call | solution.py:747
  (2 shorter events, 0.0 us)
Async XLA Ops:
  3.9 15.9 %copy-start.4 = (bf16[16,384]{1,0:T(8,128)(2,1)S(1)}, bf16[16,384]{1,0:T(8,128)(2,1)}, u32[]{:S(2)}) copy-start(bf16[16,384]{1,0:T(8,128)(2,1)} %get-tuple-element.18.edge_ref) | copy-start | bytes 36868
  3.9 15.9 %all-to-all-start = ((bf16[4,240,128]{2,1,0:T(8,128)(2,1)}), bf16[4,240,128]{2,1,0:T(8,128)(2,1)S(1)}, u32[]{:S(2)}, u32[]{:S(2)}) async-start(bf16[4,240,128]{2,1,0:T(8,128)(2,1)} %get-tuple-element.19), calls=%async_computation | async-start | bytes 491520 | tf_op jit(solution)/shard_map/all_to_all | solution.py:657
  10.2 12.6 %collective-permute-start.2 = (bf16[288,512]{1,0:T(8,128)(2,1)}, bf16[288,512]{1,0:T(8,128)(2,1)S(1)}, u32[]{:S(2)}, u32[]{:S(2)}) collective-permute-start(bf16[288,512]{1,0:T(8,128)(2,1)} %get-tuple-element.22), channel_id=1, source_target_pairs={{0,4},{4,0},{8,12},{12,8},{1,5},{5,1},{9,13},{13,9},{2,6},{6,2},{1... | collective-permute-start | bytes 884744 | tf_op jit(solution)/shard_map/ppermute | solution.py:658
  12.3 10.6 %collective-permute-start.3 = (bf16[288,512]{1,0:T(8,128)(2,1)}, bf16[288,512]{1,0:T(8,128)(2,1)S(1)}, u32[]{:S(2)}, u32[]{:S(2)}) collective-permute-start(bf16[288,512]{1,0:T(8,128)(2,1)} %get-tuple-element.23), channel_id=1, source_target_pairs={{4,8},{8,4},{5,9},{9,5},{6,10},{10,6},{7,11},{11,7},{20,24},{24,20... | collective-permute-start | bytes 884744 | tf_op jit(solution)/shard_map/ppermute | solution.py:659
  18.3 45.1 %copy-start.2 = (f32[9,1,384]{2,1,0:T(1,128)S(1)}, f32[9,1,384]{2,1,0:T(1,128)}, u32[]{:S(2)}) copy-start(f32[9,1,384]{2,1,0:T(1,128)} %weight_ref.5) | copy-start | bytes 41476
  18.3 45.1 %copy-start.3 = (s32[1,384]{1,0:T(1,128)S(1)}, s32[1,384]{1,0:T(1,128)}, u32[]{:S(2)}) copy-start(s32[1,384]{1,0:T(1,128)} %cells_ref.5) | copy-start | bytes 4612
  19.8 3.6 %copy-start = (bf16[4,240,128]{2,1,0:T(8,128)(2,1)}, bf16[4,240,128]{2,1,0:T(8,128)(2,1)S(1)}, u32[]{:S(2)}) copy-start(bf16[4,240,128]{2,1,0:T(8,128)(2,1)S(1)} %all-to-all-done.lat_ref.lat_hbm) | copy-start | bytes 737284
  19.8 3.5 %collective-permute-start.1 = (bf16[32,384]{1,0:T(8,128)(2,1)S(1)}, bf16[32,384]{1,0:T(8,128)(2,1)S(1)}, u32[]{:S(2)}, u32[]{:S(2)}) collective-permute-start(bf16[32,384]{1,0:T(8,128)(2,1)S(1)} %blend.1), channel_id=1, source_target_pairs={{0,3},{1,2},{2,1},{3,0},{4,7},{5,6},{6,5},{7,4},{8,11},{9,10},{10,... | collective-permute-start | bytes 73736 | tf_op jit(solution)/shard_map/ppermute | solution.py:690
  19.9 3.5 %collective-permute-start = (bf16[32,384]{1,0:T(8,128)(2,1)S(1)}, bf16[32,384]{1,0:T(8,128)(2,1)S(1)}, u32[]{:S(2)}, u32[]{:S(2)}) collective-permute-start(bf16[32,384]{1,0:T(8,128)(2,1)S(1)} %blend.1), channel_id=1, source_target_pairs={{0,1},{1,0},{2,3},{3,2},{4,5},{5,4},{6,7},{7,6},{8,9},{9,8},{10,11... | collective-permute-start | bytes 73736 | tf_op jit(solution)/shard_map/ppermute | solution.py:689
  22.9 0.7 %copy-start.5 = (bf16[288,512]{1,0:T(8,128)(2,1)}, bf16[288,512]{1,0:T(8,128)(2,1)S(1)}, u32[]{:S(2)}) copy-start(bf16[288,512]{1,0:T(8,128)(2,1)S(1)} %collective-permute-done.2.row_first_hbm) | copy-start | bytes 884740
  22.9 0.8 %copy-start.6 = (bf16[288,512]{1,0:T(8,128)(2,1)}, bf16[288,512]{1,0:T(8,128)(2,1)S(1)}, u32[]{:S(2)}) copy-start(bf16[288,512]{1,0:T(8,128)(2,1)S(1)} %collective-permute-done.3.row_second_hbm) | copy-start | bytes 884740
  23.3 0.6 copy-start.7
  23.4 0.6 copy-start.8
  45.8 14.0 %all-to-all-start.1 = ((bf16[4,240,128]{2,1,0:T(8,128)(2,1)}), bf16[4,240,128]{2,1,0:T(8,128)(2,1)S(1)}, u32[]{:S(2)}, u32[]{:S(2)}) async-start(bf16[4,240,128]{2,1,0:T(8,128)(2,1)} %get-tuple-element.27), calls=%async_computation.1 | async-start | bytes 491520 | tf_op jit(solution)/shard_map/all_to_all | solution.py:734
  49.9 13.6 %collective-permute-start.4 = (bf16[288,512]{1,0:T(8,128)(2,1)}, bf16[288,512]{1,0:T(8,128)(2,1)S(1)}, u32[]{:S(2)}, u32[]{:S(2)}) collective-permute-start(bf16[288,512]{1,0:T(8,128)(2,1)} %get-tuple-element.25), channel_id=1, source_target_pairs={{0,4},{4,0},{8,12},{12,8},{1,5},{5,1},{9,13},{13,9},{2,6},{6,2},{1... | collective-permute-start | bytes 884744 | tf_op jit(solution)/shard_map/ppermute | solution.py:732
  52.0 11.4 %collective-permute-start.5 = (bf16[288,512]{1,0:T(8,128)(2,1)}, bf16[288,512]{1,0:T(8,128)(2,1)S(1)}, u32[]{:S(2)}, u32[]{:S(2)}) collective-permute-start(bf16[288,512]{1,0:T(8,128)(2,1)} %get-tuple-element.26), channel_id=1, source_target_pairs={{4,8},{8,4},{5,9},{9,5},{6,10},{10,6},{7,11},{11,7},{20,24},{24,20... | collective-permute-start | bytes 884744 | tf_op jit(solution)/shard_map/ppermute | solution.py:733
  59.8 3.7 %collective-permute-start.7 = (bf16[16,384]{1,0:T(8,128)(2,1)S(1)}, bf16[16,384]{1,0:T(8,128)(2,1)S(1)}, u32[]{:S(2)}, u32[]{:S(2)}) collective-permute-start(bf16[16,384]{1,0:T(8,128)(2,1)S(1)} %corner.1), channel_id=1, source_target_pairs={{0,3},{1,2},{2,1},{3,0},{4,7},{5,6},{6,5},{7,4},{8,11},{9,10},{10,... | collective-permute-start | bytes 36872 | tf_op jit(solution)/shard_map/ppermute | solution.py:745
  59.8 3.6 %collective-permute-start.6 = (bf16[16,384]{1,0:T(8,128)(2,1)S(1)}, bf16[16,384]{1,0:T(8,128)(2,1)S(1)}, u32[]{:S(2)}, u32[]{:S(2)}) collective-permute-start(bf16[16,384]{1,0:T(8,128)(2,1)S(1)} %corner.1), channel_id=1, source_target_pairs={{0,1},{1,0},{2,3},{3,2},{4,5},{5,4},{6,7},{7,6},{8,9},{9,8},{10,11... | collective-permute-start | bytes 36872 | tf_op jit(solution)/shard_map/ppermute | solution.py:744
  63.5 0.9 %copy-start.1 = (bf16[288,384]{1,0:T(8,128)(2,1)S(1)}, bf16[288,384]{1,0:T(8,128)(2,1)}, u32[]{:S(2)}) copy-start(bf16[288,384]{1,0:T(8,128)(2,1)} %get-tuple-element.24.grad_ref) | copy-start | bytes 663556

commit v5 on v4

--- a/solution.py
+++ b/solution.py
@@ -371,7 +371,7 @@
         for lane in range(0, obs, LANES):
             r_part_ref[lane // LANES, at, :] -= value[:, lane : lane + LANES]
 
-    step = 16
+    step = 32
 
     def contract_block(b, carry):
         contract(b * step, step)

time: 70 us -> 69.4 us (level)
  no operation moved by 1% of the time
where the time goes in v5:
time: 69.4 us; the launch traced here: 68.9 us
  Pallas kernels  35.1 us (51%)
  starting transfers between devices  17.6 us (25%)
  waiting for transfers between devices  13.8 us (20%)
  local copies, waits for them, and re-layouts  1.56 us (2%)
  between operations  0.77 us (1%)
    pallas_call x1, Pallas kernels, per_device(): pl.pallas_call(functools.partial(transfer_kernel, (levels, rows, width, p...  21.3 us
    all_to_all x1, waiting for transfers between devices, per_device(): lat_got = lax.all_to_all(lat_back, 'lat', 0, 0, tiled=True)  7.02 us
    all_to_all x1, starting transfers between devices, per_device(): lat_in = lax.all_to_all(lat_send, 'lat', 0, 0, tiled=True)  6.33 us
    pallas_call x1, Pallas kernels, per_device(): pl.pallas_call(functools.partial(gather_kernel, (levels, rows, width, pad...  5.39 us
    pallas_call x1, Pallas kernels, per_device(): pl.pallas_call(functools.partial(scatter_kernel, (levels, rows, width, pa...  5.12 us
    all_to_all x1, starting transfers between devices, per_device(): lat_got = lax.all_to_all(lat_back, 'lat', 0, 0, tiled=True)  3.96 us
    ppermute x1, waiting for transfers between devices, per_device(): grad_first = lax.ppermute(grad_first, 'lat', lat_pairs[0])  3.52 us
    pallas_call x1, Pallas kernels, per_device(): pl.pallas_call(functools.partial(pack_kernel, (levels, rows, width, pad))...  3.26 us
  transfers between devices with their start and end apart: 10, of which 5 were waited for; matrix products, arithmetic and copies ran while one was open for 0% of the time, Pallas kernels for 8%

profile of v5, /device:TPU:0, one launch (start us, length us, event | category | flops | bytes accessed | tf_op | source)
XLA Modules:
  0.0 68.9 jit_solution(174817500980463986)
XLA Ops:
  0.6 3.3 %pack.1 = (bf16[288,512]{1,0:T(8,128)(2,1)}, bf16[288,512]{1,0:T(8,128)(2,1)}, bf16[16,384]{1,0:T(8,128)(2,1)}, bf16[4,240,128]{2,1,0:T(8,128)(2,1)}) custom-call(bf16[274,8,512]{2,1,0:T(8,128)(2,1)} %bitcast.3, f32[1,192,128]{2,1,0:T(8,128)} %cot_hbm.1), custom_call_target="tpu_custom_call" | custom-call | tf_op jit(solution)/shard_map/pack/pallas_call | solution.py:641
  3.9 0.0 copy-start.4
  3.9 6.3 %all-to-all-start = ((bf16[4,240,128]{2,1,0:T(8,128)(2,1)}), bf16[4,240,128]{2,1,0:T(8,128)(2,1)S(1)}, u32[]{:S(2)}, u32[]{:S(2)}) async-start(bf16[4,240,128]{2,1,0:T(8,128)(2,1)} %get-tuple-element.19), calls=%async_computation | async-start | bytes 491520 | tf_op jit(solution)/shard_map/all_to_all | solution.py:657
  10.2 2.0 %collective-permute-start.2 = (bf16[288,512]{1,0:T(8,128)(2,1)}, bf16[288,512]{1,0:T(8,128)(2,1)S(1)}, u32[]{:S(2)}, u32[]{:S(2)}) collective-permute-start(bf16[288,512]{1,0:T(8,128)(2,1)} %get-tuple-element.22), channel_id=1, source_target_pairs={{0,4},{4,0},{8,12},{12,8},{1,5},{5,1},{9,13},{13,9},{2,6},{6,2},{1... | collective-permute-start | bytes 884744 | tf_op jit(solution)/shard_map/ppermute | solution.py:658
  12.3 0.7 collective-permute-start.3
  12.9 5.4 %gather.1 = (f32[288,384]{1,0:T(8,128)}, f32[18,128,128]{2,1,0:T(8,128)}) custom-call(s32[1,384]{1,0:T(1,128)} %cells_ref.5, f32[9,1,384]{2,1,0:T(1,128)} %weight_ref.5, bf16[137,16,128]{2,1,0:T(8,128)(2,1)} %bitcast.5, bf16[274,8,512]{2,1,0:T(8,128)(2,1)} %bitcast.4), custom_call_target="tpu_custom_call" | custom-call | tf_op jit(solution)/shard_map/gather/pallas_call | solution.py:661
  18.3 0.0 copy-start.2
  18.3 0.0 copy-start.3
  18.4 1.4 %all-to-all-done.lat_ref.lat_hbm = bf16[4,240,128]{2,1,0:T(8,128)(2,1)S(1)} async-done(((bf16[4,240,128]{2,1,0:T(8,128)(2,1)}), bf16[4,240,128]{2,1,0:T(8,128)(2,1)S(1)}, u32[]{:S(2)}, u32[]{:S(2)}) %all-to-all-start) | async-done | bytes 245792 | tf_op jit(solution)/shard_map/all_to_all | solution.py:657
  19.8 0.0 copy-done.4
  19.8 0.0 copy-start
  19.8 0.1 collective-permute-start.1
  19.9 1.6 %collective-permute-start = (bf16[32,384]{1,0:T(8,128)(2,1)S(1)}, bf16[32,384]{1,0:T(8,128)(2,1)S(1)}, u32[]{:S(2)}, u32[]{:S(2)}) collective-permute-start(bf16[32,384]{1,0:T(8,128)(2,1)S(1)} %blend.1), channel_id=1, source_target_pairs={{0,1},{1,0},{2,3},{3,2},{4,5},{5,4},{6,7},{7,6},{8,9},{9,8},{10,11... | collective-permute-start | bytes 73736 | tf_op jit(solution)/shard_map/ppermute | solution.py:689
  21.5 1.4 %collective-permute-done.2.row_first_hbm = bf16[288,512]{1,0:T(8,128)(2,1)S(1)} collective-permute-done((bf16[288,512]{1,0:T(8,128)(2,1)}, bf16[288,512]{1,0:T(8,128)(2,1)S(1)}, u32[]{:S(2)}, u32[]{:S(2)}) %collective-permute-start.2) | collective-permute-done | bytes 294944 | tf_op jit(solution)/shard_map/ppermute | solution.py:658
  22.9 0.0 copy-start.5
  22.9 0.0 collective-permute-done.3.row_second_hbm
  22.9 0.0 copy-start.6
  22.9 0.5 collective-permute-done.1.side_second_ref
  23.3 0.0 copy-start.7
  23.4 0.0 collective-permute-done.side_first_ref
  23.4 0.0 copy-start.8
  23.4 0.0 copy-done
  23.4 0.2 copy-done.5
  23.6 0.1 copy-done.6
  23.7 0.3 copy-done.7
  24.0 0.0 copy-done.8
  24.0 21.3 %transfer.1 = (bf16[288,384]{1,0:T(8,128)(2,1)}, bf16[288,512]{1,0:T(8,128)(2,1)}, bf16[288,512]{1,0:T(8,128)(2,1)}, bf16[4,240,128]{2,1,0:T(8,128)(2,1)}) custom-call(s32[1,384]{1,0:T(1,128)} %cells_ref.5, f32[9,1,384]{2,1,0:T(1,128)} %weight_ref.5, s32[1,24]{1,0:T(1,128)} %instr_ref.1, s32[1,24]{1,0:T(1,128)} %dest_ref.1, bf16[137,16,128]{2,1,0:T(8,128)(2,1)} %bitcast.6, ...), custom_call_target="tpu_custom_call" | custom-call | tf_op jit(solution)/shard_map/transfer/pallas_call | solution.py:692
  45.3 4.0 %all-to-all-start.1 = ((bf16[4,240,128]{2,1,0:T(8,128)(2,1)}), bf16[4,240,128]{2,1,0:T(8,128)(2,1)S(1)}, u32[]{:S(2)}, u32[]{:S(2)}) async-start(bf16[4,240,128]{2,1,0:T(8,128)(2,1)} %get-tuple-element.27), calls=%async_computation.1 | async-start | bytes 491520 | tf_op jit(solution)/shard_map/all_to_all | solution.py:734
  49.3 2.2 %collective-permute-start.4 = (bf16[288,512]{1,0:T(8,128)(2,1)}, bf16[288,512]{1,0:T(8,128)(2,1)S(1)}, u32[]{:S(2)}, u32[]{:S(2)}) collective-permute-start(bf16[288,512]{1,0:T(8,128)(2,1)} %get-tuple-element.25), channel_id=1, source_target_pairs={{0,4},{4,0},{8,12},{12,8},{1,5},{5,1},{9,13},{13,9},{2,6},{6,2},{1... | collective-permute-start | bytes 884744 | tf_op jit(solution)/shard_map/ppermute | solution.py:732
  51.4 0.7 collective-permute-start.5
  52.1 7.0 %all-to-all-done.1.lat_ref = bf16[4,240,128]{2,1,0:T(8,128)(2,1)S(1)} async-done(((bf16[4,240,128]{2,1,0:T(8,128)(2,1)}), bf16[4,240,128]{2,1,0:T(8,128)(2,1)S(1)}, u32[]{:S(2)}, u32[]{:S(2)}) %all-to-all-start.1) | async-done | bytes 245792 | tf_op jit(solution)/shard_map/all_to_all | solution.py:734
  59.1 0.1 collective-permute-start.7
  59.2 0.1 collective-permute-start.6
  59.3 3.5 %collective-permute-done.4.row_first_ref = bf16[288,512]{1,0:T(8,128)(2,1)S(1)} collective-permute-done((bf16[288,512]{1,0:T(8,128)(2,1)}, bf16[288,512]{1,0:T(8,128)(2,1)S(1)}, u32[]{:S(2)}, u32[]{:S(2)}) %collective-permute-start.4) | collective-permute-done | bytes 294944 | tf_op jit(solution)/shard_map/ppermute | solution.py:732
  62.8 0.0 collective-permute-done.5.row_second_ref
  62.8 0.0 collective-permute-done.7.side_second_ref
  62.8 0.0 collective-permute-done.6.side_first_ref
  62.8 0.0 copy-done.2
  62.9 0.0 copy-done.3
  62.9 0.0 copy-start.1
  62.9 0.9 %copy-done.1 = bf16[288,384]{1,0:T(8,128)(2,1)S(1)} copy-done((bf16[288,384]{1,0:T(8,128)(2,1)S(1)}, bf16[288,384]{1,0:T(8,128)(2,1)}, u32[]{:S(2)}) %copy-start.1) | copy-done | bytes 221208
  63.8 5.1 %scatter.1 = (f32[2192,512]{1,0:T(8,128)}, f32[1,192,128]{2,1,0:T(8,128)}) custom-call(s32[1,384]{1,0:T(1,128)S(1)} %copy-done.3, f32[9,1,384]{2,1,0:T(1,128)S(1)} %copy-done.2, bf16[288,384]{1,0:T(8,128)(2,1)S(1)} %copy-done.1, bf16[288,512]{1,0:T(8,128)(2,1)S(1)} %collective-permute-done.4.row_first_ref, ...), custom_call_target="tpu_custom_call" | custom-call | tf_op jit(solution)/shard_map/scatter/pallas_call | solution.py:747
  (2 shorter events, 0.0 us)
Async XLA Ops:
  3.9 15.9 %copy-start.4 = (bf16[16,384]{1,0:T(8,128)(2,1)S(1)}, bf16[16,384]{1,0:T(8,128)(2,1)}, u32[]{:S(2)}) copy-start(bf16[16,384]{1,0:T(8,128)(2,1)} %get-tuple-element.18.edge_ref) | copy-start | bytes 36868
  3.9 15.9 %all-to-all-start = ((bf16[4,240,128]{2,1,0:T(8,128)(2,1)}), bf16[4,240,128]{2,1,0:T(8,128)(2,1)S(1)}, u32[]{:S(2)}, u32[]{:S(2)}) async-start(bf16[4,240,128]{2,1,0:T(8,128)(2,1)} %get-tuple-element.19), calls=%async_computation | async-start | bytes 491520 | tf_op jit(solution)/shard_map/all_to_all | solution.py:657
  10.2 12.6 %collective-permute-start.2 = (bf16[288,512]{1,0:T(8,128)(2,1)}, bf16[288,512]{1,0:T(8,128)(2,1)S(1)}, u32[]{:S(2)}, u32[]{:S(2)}) collective-permute-start(bf16[288,512]{1,0:T(8,128)(2,1)} %get-tuple-element.22), channel_id=1, source_target_pairs={{0,4},{4,0},{8,12},{12,8},{1,5},{5,1},{9,13},{13,9},{2,6},{6,2},{1... | collective-permute-start | bytes 884744 | tf_op jit(solution)/shard_map/ppermute | solution.py:658
  12.3 10.6 %collective-permute-start.3 = (bf16[288,512]{1,0:T(8,128)(2,1)}, bf16[288,512]{1,0:T(8,128)(2,1)S(1)}, u32[]{:S(2)}, u32[]{:S(2)}) collective-permute-start(bf16[288,512]{1,0:T(8,128)(2,1)} %get-tuple-element.23), channel_id=1, source_target_pairs={{4,8},{8,4},{5,9},{9,5},{6,10},{10,6},{7,11},{11,7},{20,24},{24,20... | collective-permute-start | bytes 884744 | tf_op jit(solution)/shard_map/ppermute | solution.py:659
  18.3 44.5 %copy-start.2 = (f32[9,1,384]{2,1,0:T(1,128)S(1)}, f32[9,1,384]{2,1,0:T(1,128)}, u32[]{:S(2)}) copy-start(f32[9,1,384]{2,1,0:T(1,128)} %weight_ref.5) | copy-start | bytes 41476
  18.3 44.5 %copy-start.3 = (s32[1,384]{1,0:T(1,128)S(1)}, s32[1,384]{1,0:T(1,128)}, u32[]{:S(2)}) copy-start(s32[1,384]{1,0:T(1,128)} %cells_ref.5) | copy-start | bytes 4612
  19.8 3.6 %copy-start = (bf16[4,240,128]{2,1,0:T(8,128)(2,1)}, bf16[4,240,128]{2,1,0:T(8,128)(2,1)S(1)}, u32[]{:S(2)}) copy-start(bf16[4,240,128]{2,1,0:T(8,128)(2,1)S(1)} %all-to-all-done.lat_ref.lat_hbm) | copy-start | bytes 737284
  19.8 3.5 %collective-permute-start.1 = (bf16[32,384]{1,0:T(8,128)(2,1)S(1)}, bf16[32,384]{1,0:T(8,128)(2,1)S(1)}, u32[]{:S(2)}, u32[]{:S(2)}) collective-permute-start(bf16[32,384]{1,0:T(8,128)(2,1)S(1)} %blend.1), channel_id=1, source_target_pairs={{0,3},{1,2},{2,1},{3,0},{4,7},{5,6},{6,5},{7,4},{8,11},{9,10},{10,... | collective-permute-start | bytes 73736 | tf_op jit(solution)/shard_map/ppermute | solution.py:690
  19.9 3.5 %collective-permute-start = (bf16[32,384]{1,0:T(8,128)(2,1)S(1)}, bf16[32,384]{1,0:T(8,128)(2,1)S(1)}, u32[]{:S(2)}, u32[]{:S(2)}) collective-permute-start(bf16[32,384]{1,0:T(8,128)(2,1)S(1)} %blend.1), channel_id=1, source_target_pairs={{0,1},{1,0},{2,3},{3,2},{4,5},{5,4},{6,7},{7,6},{8,9},{9,8},{10,11... | collective-permute-start | bytes 73736 | tf_op jit(solution)/shard_map/ppermute | solution.py:689
  22.9 0.7 %copy-start.5 = (bf16[288,512]{1,0:T(8,128)(2,1)}, bf16[288,512]{1,0:T(8,128)(2,1)S(1)}, u32[]{:S(2)}) copy-start(bf16[288,512]{1,0:T(8,128)(2,1)S(1)} %collective-permute-done.2.row_first_hbm) | copy-start | bytes 884740
  22.9 0.8 %copy-start.6 = (bf16[288,512]{1,0:T(8,128)(2,1)}, bf16[288,512]{1,0:T(8,128)(2,1)S(1)}, u32[]{:S(2)}) copy-start(bf16[288,512]{1,0:T(8,128)(2,1)S(1)} %collective-permute-done.3.row_second_hbm) | copy-start | bytes 884740
  23.3 0.6 copy-start.7
  23.4 0.6 copy-start.8
  45.3 13.8 %all-to-all-start.1 = ((bf16[4,240,128]{2,1,0:T(8,128)(2,1)}), bf16[4,240,128]{2,1,0:T(8,128)(2,1)S(1)}, u32[]{:S(2)}, u32[]{:S(2)}) async-start(bf16[4,240,128]{2,1,0:T(8,128)(2,1)} %get-tuple-element.27), calls=%async_computation.1 | async-start | bytes 491520 | tf_op jit(solution)/shard_map/all_to_all | solution.py:734
  49.3 13.6 %collective-permute-start.4 = (bf16[288,512]{1,0:T(8,128)(2,1)}, bf16[288,512]{1,0:T(8,128)(2,1)S(1)}, u32[]{:S(2)}, u32[]{:S(2)}) collective-permute-start(bf16[288,512]{1,0:T(8,128)(2,1)} %get-tuple-element.25), channel_id=1, source_target_pairs={{0,4},{4,0},{8,12},{12,8},{1,5},{5,1},{9,13},{13,9},{2,6},{6,2},{1... | collective-permute-start | bytes 884744 | tf_op jit(solution)/shard_map/ppermute | solution.py:732
  51.4 11.4 %collective-permute-start.5 = (bf16[288,512]{1,0:T(8,128)(2,1)}, bf16[288,512]{1,0:T(8,128)(2,1)S(1)}, u32[]{:S(2)}, u32[]{:S(2)}) collective-permute-start(bf16[288,512]{1,0:T(8,128)(2,1)} %get-tuple-element.26), channel_id=1, source_target_pairs={{4,8},{8,4},{5,9},{9,5},{6,10},{10,6},{7,11},{11,7},{20,24},{24,20... | collective-permute-start | bytes 884744 | tf_op jit(solution)/shard_map/ppermute | solution.py:733
  59.1 3.7 %collective-permute-start.7 = (bf16[16,384]{1,0:T(8,128)(2,1)S(1)}, bf16[16,384]{1,0:T(8,128)(2,1)S(1)}, u32[]{:S(2)}, u32[]{:S(2)}) collective-permute-start(bf16[16,384]{1,0:T(8,128)(2,1)S(1)} %corner.1), channel_id=1, source_target_pairs={{0,3},{1,2},{2,1},{3,0},{4,7},{5,6},{6,5},{7,4},{8,11},{9,10},{10,... | collective-permute-start | bytes 36872 | tf_op jit(solution)/shard_map/ppermute | solution.py:745
  59.2 3.6 %collective-permute-start.6 = (bf16[16,384]{1,0:T(8,128)(2,1)S(1)}, bf16[16,384]{1,0:T(8,128)(2,1)S(1)}, u32[]{:S(2)}, u32[]{:S(2)}) collective-permute-start(bf16[16,384]{1,0:T(8,128)(2,1)S(1)} %corner.1), channel_id=1, source_target_pairs={{0,1},{1,0},{2,3},{3,2},{4,5},{5,4},{6,7},{7,6},{8,9},{9,8},{10,11... | collective-permute-start | bytes 36872 | tf_op jit(solution)/shard_map/ppermute | solution.py:744
  62.9 0.9 %copy-start.1 = (bf16[288,384]{1,0:T(8,128)(2,1)S(1)}, bf16[288,384]{1,0:T(8,128)(2,1)}, u32[]{:S(2)}) copy-start(bf16[288,384]{1,0:T(8,128)(2,1)} %get-tuple-element.24.grad_ref) | copy-start | bytes 663556

commit v6 on v5

--- a/solution.py
+++ b/solution.py
@@ -49,7 +49,7 @@
     width, obs = columns_ref.shape[1:]
     _, col = split_cells(cells_ref[...], width)
     weights = [weight_ref[k] for k in range(9)]
-    step = 32
+    step = 64
 
     def chunk(i, carry):
         base = pl.multiple_of(i * step, step)

time: 69.4 us -> 69.4 us (level)
  no operation moved by 1% of the time
where the time goes in v6:
time: 69.4 us; the launch traced here: 68.9 us
  Pallas kernels  35.1 us (51%)
  starting transfers between devices  17.6 us (25%)
  waiting for transfers between devices  13.8 us (20%)
  local copies, waits for them, and re-layouts  1.56 us (2%)
  between operations  0.77 us (1%)
    pallas_call x1, Pallas kernels, per_device(): pl.pallas_call(functools.partial(transfer_kernel, (levels, rows, width, p...  21.3 us
    all_to_all x1, waiting for transfers between devices, per_device(): lat_got = lax.all_to_all(lat_back, 'lat', 0, 0, tiled=True)  7.02 us
    all_to_all x1, starting transfers between devices, per_device(): lat_in = lax.all_to_all(lat_send, 'lat', 0, 0, tiled=True)  6.33 us
    pallas_call x1, Pallas kernels, per_device(): pl.pallas_call(functools.partial(gather_kernel, (levels, rows, width, pad...  5.39 us
    pallas_call x1, Pallas kernels, per_device(): pl.pallas_call(functools.partial(scatter_kernel, (levels, rows, width, pa...  5.12 us
    all_to_all x1, starting transfers between devices, per_device(): lat_got = lax.all_to_all(lat_back, 'lat', 0, 0, tiled=True)  3.91 us
    ppermute x1, waiting for transfers between devices, per_device(): grad_first = lax.ppermute(grad_first, 'lat', lat_pairs[0])  3.52 us
    pallas_call x1, Pallas kernels, per_device(): pl.pallas_call(functools.partial(pack_kernel, (levels, rows, width, pad))...  3.26 us
  transfers between devices with their start and end apart: 10, of which 5 were waited for; matrix products, arithmetic and copies ran while one was open for 0% of the time, Pallas kernels for 8%

profile of v6, /device:TPU:0, one launch (start us, length us, event | category | flops | bytes accessed | tf_op | source)
XLA Modules:
  0.0 68.9 jit_solution(4729368310432757002)
XLA Ops:
  0.6 3.3 %pack.1 = (bf16[288,512]{1,0:T(8,128)(2,1)}, bf16[288,512]{1,0:T(8,128)(2,1)}, bf16[16,384]{1,0:T(8,128)(2,1)}, bf16[4,240,128]{2,1,0:T(8,128)(2,1)}) custom-call(bf16[274,8,512]{2,1,0:T(8,128)(2,1)} %bitcast.3, f32[1,192,128]{2,1,0:T(8,128)} %cot_hbm.1), custom_call_target="tpu_custom_call" | custom-call | tf_op jit(solution)/shard_map/pack/pallas_call | solution.py:641
  3.9 0.0 copy-start.4
  3.9 6.3 %all-to-all-start = ((bf16[4,240,128]{2,1,0:T(8,128)(2,1)}), bf16[4,240,128]{2,1,0:T(8,128)(2,1)S(1)}, u32[]{:S(2)}, u32[]{:S(2)}) async-start(bf16[4,240,128]{2,1,0:T(8,128)(2,1)} %get-tuple-element.19), calls=%async_computation | async-start | bytes 491520 | tf_op jit(solution)/shard_map/all_to_all | solution.py:657
  10.2 2.0 %collective-permute-start.2 = (bf16[288,512]{1,0:T(8,128)(2,1)}, bf16[288,512]{1,0:T(8,128)(2,1)S(1)}, u32[]{:S(2)}, u32[]{:S(2)}) collective-permute-start(bf16[288,512]{1,0:T(8,128)(2,1)} %get-tuple-element.22), channel_id=1, source_target_pairs={{0,4},{4,0},{8,12},{12,8},{1,5},{5,1},{9,13},{13,9},{2,6},{6,2},{1... | collective-permute-start | bytes 884744 | tf_op jit(solution)/shard_map/ppermute | solution.py:658
  12.3 0.7 collective-permute-start.3
  12.9 5.4 %gather.1 = (f32[288,384]{1,0:T(8,128)}, f32[18,128,128]{2,1,0:T(8,128)}) custom-call(s32[1,384]{1,0:T(1,128)} %cells_ref.5, f32[9,1,384]{2,1,0:T(1,128)} %weight_ref.5, bf16[137,16,128]{2,1,0:T(8,128)(2,1)} %bitcast.5, bf16[274,8,512]{2,1,0:T(8,128)(2,1)} %bitcast.4), custom_call_target="tpu_custom_call" | custom-call | tf_op jit(solution)/shard_map/gather/pallas_call | solution.py:661
  18.3 0.0 copy-start.2
  18.3 0.0 copy-start.3
  18.4 1.4 %all-to-all-done.lat_ref.lat_hbm = bf16[4,240,128]{2,1,0:T(8,128)(2,1)S(1)} async-done(((bf16[4,240,128]{2,1,0:T(8,128)(2,1)}), bf16[4,240,128]{2,1,0:T(8,128)(2,1)S(1)}, u32[]{:S(2)}, u32[]{:S(2)}) %all-to-all-start) | async-done | bytes 245792 | tf_op jit(solution)/shard_map/all_to_all | solution.py:657
  19.8 0.0 copy-done.4
  19.8 0.0 copy-start
  19.8 0.1 collective-permute-start.1
  19.9 1.6 %collective-permute-start = (bf16[32,384]{1,0:T(8,128)(2,1)S(1)}, bf16[32,384]{1,0:T(8,128)(2,1)S(1)}, u32[]{:S(2)}, u32[]{:S(2)}) collective-permute-start(bf16[32,384]{1,0:T(8,128)(2,1)S(1)} %blend.1), channel_id=1, source_target_pairs={{0,1},{1,0},{2,3},{3,2},{4,5},{5,4},{6,7},{7,6},{8,9},{9,8},{10,11... | collective-permute-start | bytes 73736 | tf_op jit(solution)/shard_map/ppermute | solution.py:689
  21.5 1.4 %collective-permute-done.2.row_first_hbm = bf16[288,512]{1,0:T(8,128)(2,1)S(1)} collective-permute-done((bf16[288,512]{1,0:T(8,128)(2,1)}, bf16[288,512]{1,0:T(8,128)(2,1)S(1)}, u32[]{:S(2)}, u32[]{:S(2)}) %collective-permute-start.2) | collective-permute-done | bytes 294944 | tf_op jit(solution)/shard_map/ppermute | solution.py:658
  22.9 0.0 copy-start.5
  22.9 0.0 collective-permute-done.3.row_second_hbm
  22.9 0.0 copy-start.6
  22.9 0.5 collective-permute-done.1.side_second_ref
  23.3 0.0 copy-start.7
  23.4 0.0 collective-permute-done.side_first_ref
  23.4 0.0 copy-start.8
  23.4 0.0 copy-done
  23.4 0.2 copy-done.5
  23.6 0.1 copy-done.6
  23.7 0.3 copy-done.7
  24.0 0.0 copy-done.8
  24.0 21.3 %transfer.1 = (bf16[288,384]{1,0:T(8,128)(2,1)}, bf16[288,512]{1,0:T(8,128)(2,1)}, bf16[288,512]{1,0:T(8,128)(2,1)}, bf16[4,240,128]{2,1,0:T(8,128)(2,1)}) custom-call(s32[1,384]{1,0:T(1,128)} %cells_ref.5, f32[9,1,384]{2,1,0:T(1,128)} %weight_ref.5, s32[1,24]{1,0:T(1,128)} %instr_ref.1, s32[1,24]{1,0:T(1,128)} %dest_ref.1, bf16[137,16,128]{2,1,0:T(8,128)(2,1)} %bitcast.6, ...), custom_call_target="tpu_custom_call" | custom-call | tf_op jit(solution)/shard_map/transfer/pallas_call | solution.py:692
  45.3 3.9 %all-to-all-start.1 = ((bf16[4,240,128]{2,1,0:T(8,128)(2,1)}), bf16[4,240,128]{2,1,0:T(8,128)(2,1)S(1)}, u32[]{:S(2)}, u32[]{:S(2)}) async-start(bf16[4,240,128]{2,1,0:T(8,128)(2,1)} %get-tuple-element.27), calls=%async_computation.1 | async-start | bytes 491520 | tf_op jit(solution)/shard_map/all_to_all | solution.py:734
  49.2 2.2 %collective-permute-start.4 = (bf16[288,512]{1,0:T(8,128)(2,1)}, bf16[288,512]{1,0:T(8,128)(2,1)S(1)}, u32[]{:S(2)}, u32[]{:S(2)}) collective-permute-start(bf16[288,512]{1,0:T(8,128)(2,1)} %get-tuple-element.25), channel_id=1, source_target_pairs={{0,4},{4,0},{8,12},{12,8},{1,5},{5,1},{9,13},{13,9},{2,6},{6,2},{1... | collective-permute-start | bytes 884744 | tf_op jit(solution)/shard_map/ppermute | solution.py:732
  51.4 0.7 collective-permute-start.5
  52.1 7.0 %all-to-all-done.1.lat_ref = bf16[4,240,128]{2,1,0:T(8,128)(2,1)S(1)} async-done(((bf16[4,240,128]{2,1,0:T(8,128)(2,1)}), bf16[4,240,128]{2,1,0:T(8,128)(2,1)S(1)}, u32[]{:S(2)}, u32[]{:S(2)}) %all-to-all-start.1) | async-done | bytes 245792 | tf_op jit(solution)/shard_map/all_to_all | solution.py:734
  59.1 0.1 collective-permute-start.7
  59.2 0.1 collective-permute-start.6
  59.3 3.5 %collective-permute-done.4.row_first_ref = bf16[288,512]{1,0:T(8,128)(2,1)S(1)} collective-permute-done((bf16[288,512]{1,0:T(8,128)(2,1)}, bf16[288,512]{1,0:T(8,128)(2,1)S(1)}, u32[]{:S(2)}, u32[]{:S(2)}) %collective-permute-start.4) | collective-permute-done | bytes 294944 | tf_op jit(solution)/shard_map/ppermute | solution.py:732
  62.8 0.0 collective-permute-done.5.row_second_ref
  62.8 0.0 collective-permute-done.7.side_second_ref
  62.8 0.0 collective-permute-done.6.side_first_ref
  62.8 0.0 copy-done.2
  62.8 0.0 copy-done.3
  62.8 0.0 copy-start.1
  62.8 0.9 %copy-done.1 = bf16[288,384]{1,0:T(8,128)(2,1)S(1)} copy-done((bf16[288,384]{1,0:T(8,128)(2,1)S(1)}, bf16[288,384]{1,0:T(8,128)(2,1)}, u32[]{:S(2)}) %copy-start.1) | copy-done | bytes 221208
  63.8 5.1 %scatter.1 = (f32[2192,512]{1,0:T(8,128)}, f32[1,192,128]{2,1,0:T(8,128)}) custom-call(s32[1,384]{1,0:T(1,128)S(1)} %copy-done.3, f32[9,1,384]{2,1,0:T(1,128)S(1)} %copy-done.2, bf16[288,384]{1,0:T(8,128)(2,1)S(1)} %copy-done.1, bf16[288,512]{1,0:T(8,128)(2,1)S(1)} %collective-permute-done.4.row_first_ref, ...), custom_call_target="tpu_custom_call" | custom-call | tf_op jit(solution)/shard_map/scatter/pallas_call | solution.py:747
  (2 shorter events, 0.0 us)
Async XLA Ops:
  3.9 15.9 %copy-start.4 = (bf16[16,384]{1,0:T(8,128)(2,1)S(1)}, bf16[16,384]{1,0:T(8,128)(2,1)}, u32[]{:S(2)}) copy-start(bf16[16,384]{1,0:T(8,128)(2,1)} %get-tuple-element.18.edge_ref) | copy-start | bytes 36868
  3.9 15.9 %all-to-all-start = ((bf16[4,240,128]{2,1,0:T(8,128)(2,1)}), bf16[4,240,128]{2,1,0:T(8,128)(2,1)S(1)}, u32[]{:S(2)}, u32[]{:S(2)}) async-start(bf16[4,240,128]{2,1,0:T(8,128)(2,1)} %get-tuple-element.19), calls=%async_computation | async-start | bytes 491520 | tf_op jit(solution)/shard_map/all_to_all | solution.py:657
  10.2 12.6 %collective-permute-start.2 = (bf16[288,512]{1,0:T(8,128)(2,1)}, bf16[288,512]{1,0:T(8,128)(2,1)S(1)}, u32[]{:S(2)}, u32[]{:S(2)}) collective-permute-start(bf16[288,512]{1,0:T(8,128)(2,1)} %get-tuple-element.22), channel_id=1, source_target_pairs={{0,4},{4,0},{8,12},{12,8},{1,5},{5,1},{9,13},{13,9},{2,6},{6,2},{1... | collective-permute-start | bytes 884744 | tf_op jit(solution)/shard_map/ppermute | solution.py:658
  12.3 10.6 %collective-permute-start.3 = (bf16[288,512]{1,0:T(8,128)(2,1)}, bf16[288,512]{1,0:T(8,128)(2,1)S(1)}, u32[]{:S(2)}, u32[]{:S(2)}) collective-permute-start(bf16[288,512]{1,0:T(8,128)(2,1)} %get-tuple-element.23), channel_id=1, source_target_pairs={{4,8},{8,4},{5,9},{9,5},{6,10},{10,6},{7,11},{11,7},{20,24},{24,20... | collective-permute-start | bytes 884744 | tf_op jit(solution)/shard_map/ppermute | solution.py:659
  18.3 44.5 %copy-start.2 = (f32[9,1,384]{2,1,0:T(1,128)S(1)}, f32[9,1,384]{2,1,0:T(1,128)}, u32[]{:S(2)}) copy-start(f32[9,1,384]{2,1,0:T(1,128)} %weight_ref.5) | copy-start | bytes 41476
  18.3 44.5 %copy-start.3 = (s32[1,384]{1,0:T(1,128)S(1)}, s32[1,384]{1,0:T(1,128)}, u32[]{:S(2)}) copy-start(s32[1,384]{1,0:T(1,128)} %cells_ref.5) | copy-start | bytes 4612
  19.8 3.6 %copy-start = (bf16[4,240,128]{2,1,0:T(8,128)(2,1)}, bf16[4,240,128]{2,1,0:T(8,128)(2,1)S(1)}, u32[]{:S(2)}) copy-start(bf16[4,240,128]{2,1,0:T(8,128)(2,1)S(1)} %all-to-all-done.lat_ref.lat_hbm) | copy-start | bytes 737284
  19.8 3.5 %collective-permute-start.1 = (bf16[32,384]{1,0:T(8,128)(2,1)S(1)}, bf16[32,384]{1,0:T(8,128)(2,1)S(1)}, u32[]{:S(2)}, u32[]{:S(2)}) collective-permute-start(bf16[32,384]{1,0:T(8,128)(2,1)S(1)} %blend.1), channel_id=1, source_target_pairs={{0,3},{1,2},{2,1},{3,0},{4,7},{5,6},{6,5},{7,4},{8,11},{9,10},{10,... | collective-permute-start | bytes 73736 | tf_op jit(solution)/shard_map/ppermute | solution.py:690
  19.9 3.5 %collective-permute-start = (bf16[32,384]{1,0:T(8,128)(2,1)S(1)}, bf16[32,384]{1,0:T(8,128)(2,1)S(1)}, u32[]{:S(2)}, u32[]{:S(2)}) collective-permute-start(bf16[32,384]{1,0:T(8,128)(2,1)S(1)} %blend.1), channel_id=1, source_target_pairs={{0,1},{1,0},{2,3},{3,2},{4,5},{5,4},{6,7},{7,6},{8,9},{9,8},{10,11... | collective-permute-start | bytes 73736 | tf_op jit(solution)/shard_map/ppermute | solution.py:689
  22.9 0.7 %copy-start.5 = (bf16[288,512]{1,0:T(8,128)(2,1)}, bf16[288,512]{1,0:T(8,128)(2,1)S(1)}, u32[]{:S(2)}) copy-start(bf16[288,512]{1,0:T(8,128)(2,1)S(1)} %collective-permute-done.2.row_first_hbm) | copy-start | bytes 884740
  22.9 0.8 %copy-start.6 = (bf16[288,512]{1,0:T(8,128)(2,1)}, bf16[288,512]{1,0:T(8,128)(2,1)S(1)}, u32[]{:S(2)}) copy-start(bf16[288,512]{1,0:T(8,128)(2,1)S(1)} %collective-permute-done.3.row_second_hbm) | copy-start | bytes 884740
  23.3 0.6 copy-start.7
  23.4 0.6 copy-start.8
  45.3 13.8 %all-to-all-start.1 = ((bf16[4,240,128]{2,1,0:T(8,128)(2,1)}), bf16[4,240,128]{2,1,0:T(8,128)(2,1)S(1)}, u32[]{:S(2)}, u32[]{:S(2)}) async-start(bf16[4,240,128]{2,1,0:T(8,128)(2,1)} %get-tuple-element.27), calls=%async_computation.1 | async-start | bytes 491520 | tf_op jit(solution)/shard_map/all_to_all | solution.py:734
  49.2 13.6 %collective-permute-start.4 = (bf16[288,512]{1,0:T(8,128)(2,1)}, bf16[288,512]{1,0:T(8,128)(2,1)S(1)}, u32[]{:S(2)}, u32[]{:S(2)}) collective-permute-start(bf16[288,512]{1,0:T(8,128)(2,1)} %get-tuple-element.25), channel_id=1, source_target_pairs={{0,4},{4,0},{8,12},{12,8},{1,5},{5,1},{9,13},{13,9},{2,6},{6,2},{1... | collective-permute-start | bytes 884744 | tf_op jit(solution)/shard_map/ppermute | solution.py:732
  51.4 11.4 %collective-permute-start.5 = (bf16[288,512]{1,0:T(8,128)(2,1)}, bf16[288,512]{1,0:T(8,128)(2,1)S(1)}, u32[]{:S(2)}, u32[]{:S(2)}) collective-permute-start(bf16[288,512]{1,0:T(8,128)(2,1)} %get-tuple-element.26), channel_id=1, source_target_pairs={{4,8},{8,4},{5,9},{9,5},{6,10},{10,6},{7,11},{11,7},{20,24},{24,20... | collective-permute-start | bytes 884744 | tf_op jit(solution)/shard_map/ppermute | solution.py:733
  59.1 3.7 %collective-permute-start.7 = (bf16[16,384]{1,0:T(8,128)(2,1)S(1)}, bf16[16,384]{1,0:T(8,128)(2,1)S(1)}, u32[]{:S(2)}, u32[]{:S(2)}) collective-permute-start(bf16[16,384]{1,0:T(8,128)(2,1)S(1)} %corner.1), channel_id=1, source_target_pairs={{0,3},{1,2},{2,1},{3,0},{4,7},{5,6},{6,5},{7,4},{8,11},{9,10},{10,... | collective-permute-start | bytes 36872 | tf_op jit(solution)/shard_map/ppermute | solution.py:745
  59.2 3.6 %collective-permute-start.6 = (bf16[16,384]{1,0:T(8,128)(2,1)S(1)}, bf16[16,384]{1,0:T(8,128)(2,1)S(1)}, u32[]{:S(2)}, u32[]{:S(2)}) collective-permute-start(bf16[16,384]{1,0:T(8,128)(2,1)S(1)} %corner.1), channel_id=1, source_target_pairs={{0,1},{1,0},{2,3},{3,2},{4,5},{5,4},{6,7},{7,6},{8,9},{9,8},{10,11... | collective-permute-start | bytes 36872 | tf_op jit(solution)/shard_map/ppermute | solution.py:744
  62.8 0.9 %copy-start.1 = (bf16[288,384]{1,0:T(8,128)(2,1)S(1)}, bf16[288,384]{1,0:T(8,128)(2,1)}, u32[]{:S(2)}) copy-start(bf16[288,384]{1,0:T(8,128)(2,1)} %get-tuple-element.24.grad_ref) | copy-start | bytes 663556
